TPU v7x, 256 devices: a whole 4x4x8 slice. The times are simulated.
256 devices in a mesh: step: 8 (over z), seq: 32 (over y, x, core).
Axes of the slice: x: 4, y: 4, z: 8, core: 2. Of those that a mesh axis runs over, the one named last changes fastest.
Arguments:
- trajectory: float32 [8, 2, 1024, 64], P('step', None, 'seq'), may hold values from -3 to 3
- noise: float32 [8, 2, 1024, 64], P('step', None, 'seq'), may hold values from -1.5 to 1.5
- step_sizes: float32 [8], P('step'), may hold values from 0.1 to 0.3
- modulation: float32 [8, 7, 3072], P('step'), may hold values from -3 to 3
- text_states: bfloat16 [2, 512, 3072], P(None, 'seq'), may hold values from -3.5 to 3.5
- w_latent: bfloat16 [64, 3072], replicated, may hold values from -0.75 to 0.75
- w_image_qkv: bfloat16 [3072, 3, 16, 128], P('seq'), may hold values from -0.054487432 to 0.054487432
- w_text_kv: bfloat16 [3072, 2, 16, 128], P('seq'), may hold values from -0.109375 to 0.109375
- w_out_t: bfloat16 [3072, 16, 128], P('seq'), may hold values from -0.125 to 0.125
- qk_gains: float32 [3, 128], replicated, may hold values from 0.5 to 1.5
- w_final: bfloat16 [3072, 64], replicated, may hold values from -0.109375 to 0.109375
Outputs:
- trajectory_out: float32 [8, 2, 1024, 64], P('step', None, 'seq')
All inputs are finite; a program needn't handle non-finite values.
Results may differ from a plain program's by a relative error of at most 0.0025.
Values may be sent and summed in bfloat16 or wider, within the bound.
No kernel may reach another device: no remote copies, remote signals or barrier semaphores. Data moves between devices by JAX's collectives and lax.ppermute only.
A program may use at most 128 MiB of HBM per device.

v0:
```python
import math

import jax
import jax.numpy as jnp
from jax import lax
from jax.sharding import PartitionSpec as P

ITERS = 2


def prefix_2(array, axis, combine, identity):
    devices, place = (lax.axis_size(axis), lax.axis_index(axis))
    everything = lax.all_gather(array, axis)
    start = jnp.broadcast_to(jnp.asarray(identity, array.dtype), array.shape)

    def step(k, before):
        reached = k < place
        new = combine(before, everything[k])
        return jnp.where(reached, new, before)

    return lax.fori_loop(0, devices, step, start)


def layer_norm(values):
    centre = values - jnp.mean(values, axis=-1, keepdims=True)
    spread = jnp.mean(centre * centre, axis=-1, keepdims=True)
    return centre * lax.rsqrt(spread + 1e-06)


def rms_scale(values, gains):
    return values * lax.rsqrt(jnp.mean(values * values, axis=-1, keepdims=True) + 1e-06) * gains


def add_terms(earlier, later):
    return earlier + later


def local(
    trajectory,
    noise,
    step_sizes,
    modulation,
    text_states,
    w_latent,
    w_image_qkv,
    w_text_kv,
    w_out_t,
    qk_gains,
    w_final,
):
    seq_count = lax.axis_size("seq")
    images, rows, chans = (trajectory.shape[1], trajectory.shape[2], trajectory.shape[3])
    width = w_latent.shape[1]
    heads, head_dim = (w_out_t.shape[1], w_out_t.shape[2])
    local_width = w_out_t.shape[0]
    group = seq_count // images
    shifts = modulation[0]
    step_size = step_sizes[0]
    factor = 1.0 / math.sqrt(head_dim)
    text_norm = layer_norm(text_states.astype(jnp.float32)).astype(jnp.bfloat16)
    text_send = jnp.repeat(text_norm, group, axis=0)
    stacked = jnp.concatenate([w_image_qkv, w_text_kv], axis=1)
    stacked = jnp.transpose(stacked, (2, 0, 1, 3)).reshape(heads, local_width, 5 * head_dim)
    weight_send = jnp.tile(stacked, (images, 1, 1))
    columns, text_rows = (
        lax.all_to_all(weight_send, "seq", split_axis=0, concat_axis=1, tiled=True),
        lax.all_to_all(text_send, "seq", split_axis=0, concat_axis=1, tiled=True),
    )
    columns = columns.reshape(columns.shape[0], columns.shape[1], 5, head_dim)
    text_in = (text_rows[0].astype(jnp.float32) * (1.0 + shifts[4]) + shifts[3]).astype(
        jnp.bfloat16
    )
    text_pairs = jnp.einsum(
        "td,idce->icte", text_in, columns[:, :, 3:5], preferred_element_type=jnp.float32
    )
    text_keys = rms_scale(text_pairs[:, 0], qk_gains[2]).astype(jnp.bfloat16)
    text_values = text_pairs[:, 1].astype(jnp.bfloat16)
    start = trajectory[0]
    is_first = lax.axis_index("step") == 0
    current = start
    result = start
    for iteration in range(ITERS):
        latent = current.astype(jnp.bfloat16)
        paired = latent.reshape(images, rows // 2, 2 * chans)
        sent = jnp.repeat(paired, group, axis=0)
        whole_latent = lax.all_to_all(sent, "seq", split_axis=0, concat_axis=1, tiled=True)
        image_latent = whole_latent.reshape(whole_latent.shape[1] * 2, chans)
        hidden = jnp.dot(image_latent, w_latent, preferred_element_type=jnp.float32)
        image_in = (layer_norm(hidden) * (1.0 + shifts[1]) + shifts[0]).astype(jnp.bfloat16)
        projected = jnp.einsum(
            "td,idce->icte", image_in, columns[:, :, 0:3], preferred_element_type=jnp.float32
        )
        queries = rms_scale(projected[:, 0], qk_gains[0]).astype(jnp.bfloat16)
        image_keys = rms_scale(projected[:, 1], qk_gains[1]).astype(jnp.bfloat16)
        image_values = projected[:, 2].astype(jnp.bfloat16)
        keys = jnp.concatenate([text_keys, image_keys], axis=1)
        values = jnp.concatenate([text_values, image_values], axis=1)
        scores = (
            jnp.einsum("iqe,ike->iqk", queries, keys, preferred_element_type=jnp.float32) * factor
        )
        powers = jnp.exp(scores)
        probs = (powers / jnp.sum(powers, axis=-1, keepdims=True)).astype(jnp.bfloat16)
        attended = jnp.einsum(
            "iqk,ike->iqe", probs, values, preferred_element_type=jnp.float32
        ).astype(jnp.bfloat16)
        every = lax.all_gather(attended, "seq", axis=0, tiled=True)
        every = every.reshape(images, heads, every.shape[1], head_dim)
        block = jnp.einsum("bhte,dhe->btd", every, w_out_t, preferred_element_type=jnp.float32)
        mixed = lax.all_to_all(block, "seq", split_axis=1, concat_axis=2, tiled=True)
        local_hidden = jnp.dot(
            latent.reshape(images * rows, chans), w_latent, preferred_element_type=jnp.float32
        )
        combined = local_hidden.reshape(images, rows, width) + shifts[2] * mixed
        final_in = (layer_norm(combined) * (1.0 + shifts[6]) + shifts[5]).astype(jnp.bfloat16)
        drift = jnp.dot(
            final_in.reshape(images * rows, width), w_final, preferred_element_type=jnp.float32
        )
        increment = step_size * drift.reshape(images, rows, chans) + noise[0]
        contrib = increment + jnp.where(is_first, start, jnp.zeros_like(start))
        prefix = prefix_2(contrib, "step", add_terms, jnp.zeros_like(contrib))
        result = prefix + contrib
        current = jnp.where(is_first, start, prefix)
    return result[None]


def solution(mesh):
    placed = (
        P("step", None, "seq", None),
        P("step", None, "seq", None),
        P("step"),
        P("step", None, None),
        P(None, "seq", None),
        P(),
        P("seq", None, None, None),
        P("seq", None, None, None),
        P("seq", None, None),
        P(),
        P(),
    )
    return jax.shard_map(
        local, mesh=mesh, in_specs=placed, out_specs=P("step", None, "seq", None), check_vma=False
    )
```

profile of v0, /device:TPU:1, one launch (start us, length us, event | category | flops | bytes accessed | tf_op | source)
XLA Modules:
  0.0 418.0 jit_solution(5876242648786972277)
XLA Ops:
  6.5 0.8 convert_element_type.154
  7.4 0.7 broadcast_in_dim.8
  8.1 8.6 %all-to-all-start.1 = ((bf16[32,16,128]{2,1,0:T(8,128)(2,1)}), bf16[32,16,128]{2,1,0:T(8,128)(2,1)S(1)}, u32[]{:S(2)}, u32[]{:S(2)}) async-start(bf16[32,16,128]{2,1,0:T(8,128)(2,1)} %bitcast.8), calls=%async_computation.1 | async-start | bytes 262144 | tf_op jit(solution)/shard_map/all_to_all | solution.py:86
  16.7 1.0 convert_reduce_fusion
  17.8 1.1 fusion.26
  18.9 1.1 fusion.27
  19.9 4.4 %all-to-all-done.1 = bf16[32,16,128]{2,1,0:T(8,128)(2,1)S(1)} async-done(((bf16[32,16,128]{2,1,0:T(8,128)(2,1)}), bf16[32,16,128]{2,1,0:T(8,128)(2,1)S(1)}, u32[]{:S(2)}, u32[]{:S(2)}) %all-to-all-start.1) | async-done | bytes 131104 | tf_op jit(solution)/shard_map/all_to_all | solution.py:86
  24.3 2.0 broadcast_in_dim.9
  26.4 4.1 all-to-all-start.2
  30.5 3.0 maximum_bitcast_fusion
  33.5 4.5 %copy.24 = bf16[16,96,5,128]{1,3,2,0:T(8,128)(2,1)} copy(bf16[16,96,5,128]{3,0,2,1:T(8,128)(2,1)} %maximum_bitcast_fusion) | data formatting | bytes 3932160 | tf_op jit(solution)/shard_map/transpose | solution.py:63
  38.0 4.2 %copy.25 = bf16[16,96,640]{2,1,0:T(8,128)(2,1)} copy(bf16[16,96,640]{1,2,0:T(8,128)(2,1)} %bitcast.200) | data formatting | bytes 3932160 | tf_op jit(solution)/shard_map/tile | solution.py:64
  42.3 27.5 %all-to-all-done.2 = bf16[32,16,3072]{2,1,0:T(8,128)(2,1)S(1)} async-done(((bf16[32,16,3072]{2,1,0:T(8,128)(2,1)}), bf16[32,16,3072]{2,1,0:T(8,128)(2,1)S(1)}, u32[]{:S(2)}, u32[]{:S(2)}) %all-to-all-start.2) | async-done | bytes 3145760 | tf_op jit(solution)/shard_map/all_to_all | solution.py:67
  69.8 3.7 tile.11
  73.5 7.3 %all-to-all-start = ((bf16[32,96,640]{2,1,0:T(8,128)(2,1)}), bf16[32,96,640]{2,1,0:T(8,128)(2,1)}, u32[]{:S(2)}, u32[]{:S(2)}) async-start(bf16[32,96,640]{2,1,0:T(8,128)(2,1)} %bitcast.198), calls=%async_computation | async-start | bytes 7864320 | tf_op jit(solution)/shard_map/all_to_all | solution.py:66
  81.4 1.5 slice_add_fusion
  82.9 1.8 reshape.659
  84.6 2.8 fusion.77
  87.5 1.4 multiply_reduce_fusion.1
  88.9 3.1 copy-done.1
  92.6 2.5 add_convert_fusion.2
  95.1 33.3 %all-to-all-done = bf16[32,96,640]{2,1,0:T(8,128)(2,1)} async-done(((bf16[32,96,640]{2,1,0:T(8,128)(2,1)}), bf16[32,96,640]{2,1,0:T(8,128)(2,1)}, u32[]{:S(2)}, u32[]{:S(2)}) %all-to-all-start) | async-done | bytes 3932192 | tf_op jit(solution)/shard_map/all_to_all | solution.py:66
  128.5 8.3 %copy.26 = bf16[32,96,640]{1,0,2:T(8,128)(2,1)} copy(bf16[32,96,640]{2,1,0:T(8,128)(2,1)} %all-to-all-done) | data formatting | bytes 7864320 | tf_op jit(solution)/shard_map/all_to_all | solution.py:66
  136.7 10.6 %reshape.656 = bf16[1,3072,5,128]{1,3,2,0:T(8,128)(2,1)} reshape(bf16[32,96,640]{1,0,2:T(8,128)(2,1)} %copy.26) | data formatting | bytes 7864320 | tf_op jit(solution)/shard_map/reshape | solution.py:69
  147.4 2.6 fusion.17
  150.1 6.4 %fusion.11 = f32[1,3,1024,128]{2,3,1,0:T(8,128)S(1)} fusion(f32[1024,3072]{1,0:T(8,128)} %copy-done.1, f32[3072]{0:T(1024)S(1)} %bitcast.216, f32[3072]{0:T(1024)S(1)} %bitcast.218, f32[1024]{0:T(1024)S(1)} %copy-done.28, f32[1024]{0:T(1024)S(1)} %broadcast_multiply_fusion.1, bf16[1,3072,5,128]{1,3,2,0:T(8,128)(2,1)S(1)} %copy-done.2), kind=kOutput, calls=%fused_computation.25 | convolution fusion | flops 2431647744 | bytes 16547840 | tf_op jit(solution)/shard_map/td,idce->icte/dot_general | solution.py:90
  157.0 1.3 fusion.6
  158.3 1.9 fusion.19
  160.3 59.6 %all-gather.7.cloned.1.call-done = bf16[32768,128]{1,0:T(8,128)(2,1)} async-done(((bf16[1024,128]{1,0:T(8,128)(2,1)}), bf16[32768,128]{1,0:T(8,128)(2,1)}) %all-gather.7.cloned.1.call-update) | async-done | bytes 8388624 | tf_op jit(solution)/shard_map/all_gather | solution.py:106
  219.8 6.0 %convolution_bitcast_fusion.1 = f32[2,1024,96]{1,2,0:T(8,128)S(1)} fusion(bf16[2,16,1024,128]{3,2,1,0:T(8,128)(2,1)} %bitcast.196, bf16[96,16,128]{2,1,0:T(8,128)(2,1)S(1)} %copy-done.6), kind=kOutput, calls=%fused_computation.28 | convolution fusion | flops 805306368 | bytes 9568256 | tf_op jit(solution)/shard_map/bhte,dhe->btd/dot_general | solution.py:108
  225.9 1.3 copy.28
  227.2 5.5 %all-to-all-start.3 = ((f32[2,1024,96]{2,0,1:T(2,128)}), f32[2,1024,96]{2,0,1:T(2,128)S(1)}, u32[]{:S(2)}, u32[]{:S(2)}) async-start(f32[2,1024,96]{2,0,1:T(2,128)} %copy.28), calls=%async_computation.3 | async-start | bytes 2097152 | tf_op jit(solution)/shard_map/all_to_all | solution.py:109
  233.4 16.5 %all-to-all-done.3 = f32[2,1024,96]{2,0,1:T(2,128)S(1)} async-done(((f32[2,1024,96]{2,0,1:T(2,128)}), f32[2,1024,96]{2,0,1:T(2,128)S(1)}, u32[]{:S(2)}, u32[]{:S(2)}) %all-to-all-start.3) | async-done | bytes 786464 | tf_op jit(solution)/shard_map/all_to_all | solution.py:109
  252.1 20.0 %all-gather.1 = f32[16,32,64]{2,1,0:T(8,128)S(1)} all-gather(f32[2,32,64]{2,1,0:T(8,128)S(1)} %fusion.23), channel_id=3, replica_groups=mesh['step'=8,'seq'=32] {'step'}, dimensions={0}, use_global_device_ids=true | all-gather | bytes 147456 | tf_op jit(solution)/shard_map/all_gather | solution.py:13
  272.6 17.2 %all_to_all.72 = bf16[32,16,128]{2,1,0:T(8,128)(2,1)S(1)} all-to-all(bf16[32,16,128]{2,1,0:T(8,128)(2,1)S(1)} %bitcast.206), channel_id=1, replica_groups=mesh['step'=8,'seq'=32] {'seq'}, dimensions={0} | all-to-all | bytes 262144 | tf_op jit(solution)/shard_map/all_to_all | solution.py:86
  290.0 1.9 fusion.79
  292.5 2.8 multiply_reduce_fusion
  295.3 0.7 add_rsqrt_fusion.2
  295.9 3.9 fusion.14
  300.1 1.3 fusion.7
  301.5 1.9 fusion.18
  303.4 54.5 %all-gather.9.cloned.1.call-done = bf16[32768,128]{1,0:T(8,128)(2,1)} async-done(((bf16[1024,128]{1,0:T(8,128)(2,1)}), bf16[32768,128]{1,0:T(8,128)(2,1)}) %all-gather.9.cloned.1.call-update) | async-done | bytes 8388624 | tf_op jit(solution)/shard_map/all_gather | solution.py:106
  357.9 6.0 %convolution_bitcast_fusion = f32[2,1024,96]{1,2,0:T(8,128)S(1)} fusion(bf16[2,16,1024,128]{3,2,1,0:T(8,128)(2,1)} %bitcast.197, bf16[96,16,128]{2,1,0:T(8,128)(2,1)S(1)} %copy-done.6), kind=kOutput, calls=%fused_computation.27 | convolution fusion | flops 805306368 | bytes 9568256 | tf_op jit(solution)/shard_map/bhte,dhe->btd/dot_general | solution.py:108
  364.0 1.3 copy.32
  365.3 5.5 %all-to-all-start.5 = ((f32[2,1024,96]{2,0,1:T(2,128)}), f32[2,1024,96]{2,0,1:T(2,128)S(1)}, u32[]{:S(2)}, u32[]{:S(2)}) async-start(f32[2,1024,96]{2,0,1:T(2,128)} %copy.32), calls=%async_computation.5 | async-start | bytes 2097152 | tf_op jit(solution)/shard_map/all_to_all | solution.py:109
  370.8 17.2 %all-to-all-done.5 = f32[2,1024,96]{2,0,1:T(2,128)S(1)} async-done(((f32[2,1024,96]{2,0,1:T(2,128)}), f32[2,1024,96]{2,0,1:T(2,128)S(1)}, u32[]{:S(2)}, u32[]{:S(2)}) %all-to-all-start.5) | async-done | bytes 786464 | tf_op jit(solution)/shard_map/all_to_all | solution.py:109
  390.2 20.0 %all-gather.3 = f32[16,32,64]{2,1,0:T(8,128)S(1)} all-gather(f32[2,32,64]{2,1,0:T(8,128)S(1)} %fusion.21), channel_id=5, replica_groups=mesh['step'=8,'seq'=32] {'step'}, dimensions={0}, use_global_device_ids=true | all-gather | bytes 147456 | tf_op jit(solution)/shard_map/all_gather | solution.py:13
  410.6 0.6 add_bitcast_fusion
  (128 shorter events, 8.3 us)
Async XLA Ops:
  6.5 78.1 %copy-start = (bf16[64,3072]{1,0:T(8,128)(2,1)S(1)}, bf16[64,3072]{1,0:T(8,128)(2,1)}, u32[]{:S(2)}) copy-start(bf16[64,3072]{1,0:T(8,128)(2,1)} %param.20) | copy-start | bytes 1179652
  8.1 16.2 %all-to-all-start.1 = ((bf16[32,16,128]{2,1,0:T(8,128)(2,1)}), bf16[32,16,128]{2,1,0:T(8,128)(2,1)S(1)}, u32[]{:S(2)}, u32[]{:S(2)}) async-start(bf16[32,16,128]{2,1,0:T(8,128)(2,1)} %bitcast.8), calls=%async_computation.1 | async-start | bytes 262144 | tf_op jit(solution)/shard_map/all_to_all | solution.py:86
  24.3 2.0 copy-start.9
  26.4 43.4 %all-to-all-start.2 = ((bf16[32,16,3072]{2,1,0:T(8,128)(2,1)}), bf16[32,16,3072]{2,1,0:T(8,128)(2,1)S(1)}, u32[]{:S(2)}, u32[]{:S(2)}) async-start(bf16[32,16,3072]{2,1,0:T(8,128)(2,1)} %bitcast.199), calls=%async_computation.2 | async-start | bytes 6291456 | tf_op jit(solution)/shard_map/all_to_all | solution.py:67
  42.3 38.6 %copy-start.30 = (f32[3,128]{1,0:T(4,128)S(1)}, f32[3,128]{1,0:T(4,128)}, u32[]{:S(2)}) copy-start(f32[3,128]{1,0:T(4,128)} %param.24) | copy-start | bytes 4612
  73.5 55.0 %all-to-all-start = ((bf16[32,96,640]{2,1,0:T(8,128)(2,1)}), bf16[32,96,640]{2,1,0:T(8,128)(2,1)}, u32[]{:S(2)}, u32[]{:S(2)}) async-start(bf16[32,96,640]{2,1,0:T(8,128)(2,1)} %bitcast.198), calls=%async_computation | async-start | bytes 7864320 | tf_op jit(solution)/shard_map/all_to_all | solution.py:66
  80.8 139.0 %all-gather.7.cloned.1.call-start = ((), (), s32[]{:S(2)}) async-start(), calls=%async_computation.6 | async-start | bytes 8650752 | tf_op jit(solution)/shard_map/all_gather | solution.py:106
  87.4 4.5 %copy-start.1 = (f32[1024,3072]{1,0:T(8,128)}, f32[1024,3072]{1,0:T(8,128)S(1)}, u32[]{:S(2)}) copy-start(f32[1024,3072]{1,0:T(8,128)S(1)} %get-tuple-element.222) | copy-start | bytes 37748740
  87.5 5.1 %copy-start.20 = (f32[1,1,3072]{2,0,1:T(1,128)S(1)}, f32[1,1,3072]{2,0,1:T(1,128)}, u32[]{:S(2)}) copy-start(f32[1,1,3072]{2,0,1:T(1,128)} %get-tuple-element.212) | copy-start | bytes 36868
  87.5 5.1 %copy-start.21 = (f32[1,1,3072]{2,0,1:T(1,128)S(1)}, f32[1,1,3072]{2,0,1:T(1,128)}, u32[]{:S(2)}) copy-start(f32[1,1,3072]{2,0,1:T(1,128)} %get-tuple-element.213) | copy-start | bytes 36868
  136.7 10.6 %copy-start.4 = (bf16[32,16,3072]{2,1,0:T(8,128)(2,1)S(1)}, bf16[32,16,3072]{2,1,0:T(8,128)(2,1)}, u32[]{:S(2)}) copy-start(bf16[32,16,3072]{2,1,0:T(8,128)(2,1)} %add_convert_fusion.2) | copy-start | bytes 9437188
  147.3 2.7 copy-start.2
  147.3 2.7 copy-start.22
  147.3 2.7 copy-start.23
  147.3 2.7 copy-start.28
  150.0 8.3 %copy-start.14 = (bf16[1,512,128]{1,2,0:T(8,128)(2,1)}, bf16[1,512,128]{1,2,0:T(8,128)(2,1)S(1)}, u32[]{:S(2)}) copy-start(bf16[1,512,128]{1,2,0:T(8,128)(2,1)S(1)} %fusion.68) | copy-start | bytes 393220
  150.1 6.7 %copy-start.29 = (f32[128]{0:T(128)S(1)}, f32[128]{0:T(128)}, u32[]{:S(2)}) copy-start(f32[128]{0:T(128)} %get-tuple-element.220) | copy-start | bytes 1540
  150.1 6.8 %copy-start.26 = (f32[128]{0:T(128)S(1)}, f32[128]{0:T(128)}, u32[]{:S(2)}) copy-start(f32[128]{0:T(128)} %get-tuple-element.219) | copy-start | bytes 1540
  150.1 6.9 %copy-start.24 = (f32[128]{0:T(128)S(1)}, f32[128]{0:T(128)}, u32[]{:S(2)}) copy-start(f32[128]{0:T(128)} %get-tuple-element.218) | copy-start | bytes 1540
  158.3 61.5 %copy-start.6 = (bf16[96,16,128]{2,1,0:T(8,128)(2,1)S(1)}, bf16[96,16,128]{2,1,0:T(8,128)(2,1)}, u32[]{:S(2)}) copy-start(bf16[96,16,128]{2,1,0:T(8,128)(2,1)} %param.23) | copy-start | bytes 1179652
  225.9 25.3 %copy-start.7 = (f32[1,2,32,64]{3,2,1,0:T(8,128)S(1)}, f32[1,2,32,64]{3,2,1,0:T(8,128)}, u32[]{:S(2)}) copy-start(f32[1,2,32,64]{3,2,1,0:T(8,128)} %param.15) | copy-start | bytes 49156
  225.9 25.3 %copy-start.18 = (f32[1,1,3072]{2,0,1:T(1,128)S(1)}, f32[1,1,3072]{2,0,1:T(1,128)}, u32[]{:S(2)}) copy-start(f32[1,1,3072]{2,0,1:T(1,128)} %get-tuple-element.216) | copy-start | bytes 36868
  225.9 25.9 %copy-start.5 = (bf16[3072,64]{0,1:T(8,128)(2,1)S(1)}, bf16[3072,64]{0,1:T(8,128)(2,1)}, u32[]{:S(2)}) copy-start(bf16[3072,64]{0,1:T(8,128)(2,1)} %param.25) | copy-start | bytes 1179652
  225.9 25.9 %copy-start.12 = (f32[1,2,32,64]{3,2,1,0:T(8,128)S(1)}, f32[1,2,32,64]{3,2,1,0:T(8,128)}, u32[]{:S(2)}) copy-start(f32[1,2,32,64]{3,2,1,0:T(8,128)} %param.16) | copy-start | bytes 49156
  225.9 25.9 %copy-start.16 = (f32[1,1,3072]{2,0,1:T(1,128)S(1)}, f32[1,1,3072]{2,0,1:T(1,128)}, u32[]{:S(2)}) copy-start(f32[1,1,3072]{2,0,1:T(1,128)} %get-tuple-element.217) | copy-start | bytes 36868
  227.2 22.6 %all-to-all-start.3 = ((f32[2,1024,96]{2,0,1:T(2,128)}), f32[2,1024,96]{2,0,1:T(2,128)S(1)}, u32[]{:S(2)}, u32[]{:S(2)}) async-start(f32[2,1024,96]{2,0,1:T(2,128)} %copy.28), calls=%async_computation.3 | async-start | bytes 2097152 | tf_op jit(solution)/shard_map/all_to_all | solution.py:109
  232.7 125.3 %all-gather.9.cloned.1.call-start = ((), (), s32[]{:S(2)}) async-start(), calls=%async_computation.7 | async-start | bytes 8650752 | tf_op jit(solution)/shard_map/all_gather | solution.py:106
  272.5 19.4 %copy-start.10 = (bf16[2,32,64]{2,1,0:T(8,128)(2,1)}, bf16[2,32,64]{2,1,0:T(8,128)(2,1)S(1)}, u32[]{:S(2)}) copy-start(bf16[2,32,64]{2,1,0:T(8,128)(2,1)S(1)} %fusion.69) | copy-start | bytes 24580
  292.5 3.5 copy-start.3
  295.9 4.1 copy-start.27
  295.9 4.2 %copy-start.25 = (f32[128]{0:T(128)S(1)}, f32[128]{0:T(128)}, u32[]{:S(2)}) copy-start(f32[128]{0:T(128)} %get-tuple-element.218) | copy-start | bytes 1540
  299.8 1.6 copy-start.15
  364.0 25.3 %copy-start.11 = (bf16[2,32,64]{2,1,0:T(8,128)(2,1)S(1)}, bf16[2,32,64]{2,1,0:T(8,128)(2,1)}, u32[]{:S(2)}) copy-start(bf16[2,32,64]{2,1,0:T(8,128)(2,1)} %copy-done.10) | copy-start | bytes 24580
  364.0 25.3 %copy-start.19 = (f32[1,1,3072]{2,0,1:T(1,128)S(1)}, f32[1,1,3072]{2,0,1:T(1,128)}, u32[]{:S(2)}) copy-start(f32[1,1,3072]{2,0,1:T(1,128)} %get-tuple-element.216) | copy-start | bytes 36868
  364.0 25.9 %copy-start.8 = (f32[1,2,32,64]{3,2,1,0:T(8,128)S(1)}, f32[1,2,32,64]{3,2,1,0:T(8,128)}, u32[]{:S(2)}) copy-start(f32[1,2,32,64]{3,2,1,0:T(8,128)} %param.15) | copy-start | bytes 49156
  364.0 25.9 %copy-start.13 = (f32[1,2,32,64]{3,2,1,0:T(8,128)S(1)}, f32[1,2,32,64]{3,2,1,0:T(8,128)}, u32[]{:S(2)}) copy-start(f32[1,2,32,64]{3,2,1,0:T(8,128)} %param.16) | copy-start | bytes 49156
  364.0 25.9 %copy-start.17 = (f32[1,1,3072]{2,0,1:T(1,128)S(1)}, f32[1,1,3072]{2,0,1:T(1,128)}, u32[]{:S(2)}) copy-start(f32[1,1,3072]{2,0,1:T(1,128)} %get-tuple-element.217) | copy-start | bytes 36868
  365.3 22.7 %all-to-all-start.5 = ((f32[2,1024,96]{2,0,1:T(2,128)}), f32[2,1024,96]{2,0,1:T(2,128)S(1)}, u32[]{:S(2)}, u32[]{:S(2)}) async-start(f32[2,1024,96]{2,0,1:T(2,128)} %copy.32), calls=%async_computation.5 | async-start | bytes 2097152 | tf_op jit(solution)/shard_map/all_to_all | solution.py:109
Sparse Core Ops, SparseCore 0:
  160.4 59.3 all-gather.6
  303.6 54.3 all-gather.8
where the time goes:
time: 424 us; the launch traced here: 418 us
  waiting for transfers between devices  213 us (50%)
  blocking collectives  57.3 us (14%)
  local copies, waits for them, and re-layouts  45.3 us (11%)
  matrix products  37.5 us (9%)
  starting transfers between devices  31 us (7%)
  other arithmetic  18.9 us (4%)
  between operations  14.7 us (3%)
    all_gather x2, waiting for transfers between devices, local(): every = lax.all_gather(attended, 'seq', axis=0, tiled=True)  114 us
    all_gather x2, blocking collectives, prefix_2(): everything = lax.all_gather(array, axis)  40 us
    all_to_all x2, waiting for transfers between devices, local(): lax.all_to_all(block, 'seq', split_axis=1, concat_axis=2, tiled=True)  33.6 us
    all_to_all x1, waiting for transfers between devices, local(): lax.all_to_all(weight_send, 'seq', split_axis=0, concat_axis=1, tiled=True)  33.3 us
    all_to_all x1, waiting for transfers between devices, local(): lax.all_to_all(text_send, 'seq', split_axis=0, concat_axis=1, tiled=True)  27.5 us
    all_to_all x1, blocking collectives, local(): lax.all_to_all(sent, 'seq', split_axis=0, concat_axis=1, tiled=True)  17.2 us
    dot_general x2, matrix products, local(): jnp.einsum('bhte,dhe->btd', every, w_out_t, preferred_element_type=jnp.fl...  12 us
    all_to_all x2, starting transfers between devices, local(): lax.all_to_all(block, 'seq', split_axis=1, concat_axis=2, tiled=True)  10.9 us
  transfers between devices with their start and end apart: 7, of which 7 were waited for; matrix products, arithmetic and copies ran while one was open for 6% of the time, Pallas kernels for 0%

commit v1 on v0

v1 whole, which is shorter than its diff:
```python
import math

import jax
import jax.numpy as jnp
from jax import lax
from jax.sharding import Mesh
from jax.sharding import PartitionSpec as P

ITERS = 2
CHIPS = ("y", "x")
SEQ = ("y", "x", "core")
F32, BF16 = jnp.float32, jnp.bfloat16


def layer_norm(values):
    centre = values - jnp.mean(values, axis=-1, keepdims=True)
    spread = jnp.mean(centre * centre, axis=-1, keepdims=True)
    return centre * lax.rsqrt(spread + 1e-06)


def rms_scale(values, gains):
    return values * lax.rsqrt(jnp.mean(values * values, axis=-1, keepdims=True) + 1e-06) * gains


def split_high(values):
    high = lax.reduce_precision(values, 8, 7)
    return high.astype(BF16), (values - high).astype(BF16)


def swap_cores(values):
    return lax.ppermute(values, "core", [(0, 1), (1, 0)])


def local(
    trajectory,
    noise,
    step_sizes,
    modulation,
    text_states,
    w_latent,
    w_image_qkv,
    w_text_kv,
    w_out_t,
    qk_gains,
    w_final,
):
    steps = lax.axis_size("step")
    chips = lax.axis_size(CHIPS)
    place, core, chip = lax.axis_index("step"), lax.axis_index("core"), lax.axis_index(CHIPS)
    seq = lax.axis_index(SEQ)
    images, rows, chans = trajectory.shape[1:]
    width = w_latent.shape[1]
    part, heads, hd = w_out_t.shape
    text_rows = text_states.shape[1] // steps
    shifts = modulation[0]
    factor = 1.0 / math.sqrt(hd)

    w_out = lax.all_gather(w_out_t.reshape(part, heads * hd), SEQ, tiled=True)

    mods = lax.all_to_all(
        jnp.broadcast_to(shifts[None, 3:5], (steps, 2, width)), "step", 0, 0, tiled=True
    )

    text_mine = lax.dynamic_slice_in_dim(text_states, place * text_rows, text_rows, 1)
    text_norm = layer_norm(text_mine.astype(F32)).astype(BF16)
    text_block = jnp.broadcast_to(
        text_norm.reshape(1, images, text_rows * width // hd, hd),
        (chips, images, text_rows * width // hd, hd),
    ).reshape(chips * images, -1, hd)
    weight_block = jnp.transpose(w_text_kv, (2, 1, 0, 3)).reshape(2 * heads, part, hd)
    latent = trajectory[0].astype(BF16)
    latent = jnp.concatenate([latent, latent], axis=-1)
    latent_block = jnp.broadcast_to(latent[None], (chips, images, rows, 2 * chans)).reshape(
        chips * images, rows, 2 * chans
    )
    packed = jnp.concatenate([weight_block, text_block, latent_block], axis=1)
    packed = lax.all_to_all(packed, SEQ, 0, 0, tiled=True)
    cut = packed.shape[1] - rows
    w_text_mine = packed[:, :part].reshape(width, hd)
    text_here = packed[:, part:cut].reshape(-1, width)
    latents = packed[:, cut:].reshape(-1, 2 * chans)

    w_lat = w_latent.astype(F32)
    centred = w_lat - jnp.mean(w_lat, axis=1, keepdims=True)
    gram = (
        lax.dot_general(
            centred, centred, (((1,), (1,)), ((), ())), precision=lax.Precision.HIGHEST
        )
        / width
    )
    half = chans // 2
    scaled = centred * (1.0 + shifts[1])
    pad = jnp.zeros((7, width), F32)
    left = jnp.concatenate(
        [scaled[:half], shifts[0:1], pad, scaled[half:], jnp.zeros((8, width), F32)], axis=0
    )
    left = lax.dynamic_slice_in_dim(left, seq * part, part, 1)
    stacked = jnp.concatenate(split_high(left), axis=0)
    columns = jnp.transpose(w_image_qkv, (0, 2, 1, 3)).reshape(part, heads * 3 * hd)
    partial = jnp.dot(stacked, columns, preferred_element_type=F32)
    count = left.shape[0]
    partial = partial[:count] + partial[count:]
    mine = lax.dynamic_slice_in_dim(partial, core * (count // 2), count // 2, 0)
    other = lax.dynamic_slice_in_dim(partial, (1 - core) * (count // 2), count // 2, 0)
    mine = mine + swap_cores(other)
    mine = jnp.transpose(mine.reshape(count // 2, heads, 3 * hd), (1, 0, 2))
    mine = jnp.sum(lax.all_to_all(mine, CHIPS, 0, 0, tiled=True), axis=0)
    theirs = swap_cores(mine)
    first = jnp.where(core == 0, mine, theirs)
    second = jnp.where(core == 0, theirs, mine)
    folded = jnp.concatenate([first[:half], second[:half]], axis=0)
    bias = first[half : half + 1]
    folded = jnp.concatenate([folded, gram], axis=1)
    folded = jnp.concatenate(split_high(folded), axis=0)

    w_text_other = swap_cores(w_text_mine)
    w_keys = jnp.where(core == 0, w_text_mine, w_text_other)
    w_values = jnp.where(core == 0, w_text_other, w_text_mine)
    text_in = (
        text_here.astype(F32)[None] * (1.0 + mods[:, 1][:, None]) + mods[:, 0][:, None]
    ).astype(BF16)
    text_in = text_in.reshape(-1, width)
    text_keys = rms_scale(jnp.dot(text_in, w_keys, preferred_element_type=F32), qk_gains[2])
    text_values = jnp.dot(text_in, w_values, preferred_element_type=F32)
    text_pairs = jnp.concatenate([text_keys.astype(BF16), text_values.astype(BF16)], axis=1)
    text_pairs = lax.all_to_all(
        text_pairs.reshape(steps, -1, 2 * hd), "step", 0, 0, tiled=True
    ).reshape(-1, 2 * hd)

    pair = jnp.stack([noise[0], trajectory[0]], axis=1)
    kept = lax.dynamic_index_in_dim(pair, core, 0, keepdims=False)
    came = swap_cores(lax.dynamic_index_in_dim(pair, 1 - core, 0, keepdims=False))
    own = jnp.concatenate(
        [jnp.where(core == 0, kept, came), jnp.where(core == 0, came, kept)], axis=1
    )
    own_noise, own_start = own[0], own[1]
    tokens = images * rows

    result = own_start
    for iteration in range(ITERS):
        projected = jnp.dot(latents, folded, preferred_element_type=F32)
        spread = jnp.sum(
            projected[:, 3 * hd :] * latents[:, :chans].astype(F32), axis=1, keepdims=True
        )
        projected = projected[:, : 3 * hd] * lax.rsqrt(spread + 1e-06) + bias
        queries = rms_scale(projected[:, :hd], qk_gains[0]).astype(BF16)
        image_keys = rms_scale(projected[:, hd : 2 * hd], qk_gains[1]).astype(BF16)
        image_values = projected[:, 2 * hd :].astype(BF16)
        keys = jnp.concatenate([text_pairs[:, :hd], image_keys], axis=0)
        values = jnp.concatenate([text_pairs[:, hd:], image_values], axis=0)
        scores = (
            lax.dot_general(
                queries, keys, (((1,), (1,)), ((), ())), preferred_element_type=F32
            )
            * factor
        )
        powers = jnp.exp(scores)
        probs = (powers / jnp.sum(powers, axis=-1, keepdims=True)).astype(BF16)
        attended = jnp.dot(probs, values, preferred_element_type=F32).astype(BF16)
        attended = lax.all_to_all(
            attended.reshape(chips, tokens, hd), CHIPS, 0, 0, tiled=True
        )
        attended = jnp.transpose(attended, (1, 0, 2)).reshape(tokens, heads * hd)
        mixed = lax.dot_general(
            attended, w_out, (((1,), (1,)), ((), ())), preferred_element_type=F32
        )
        mine_x = lax.dynamic_slice_in_dim(latents, chip * tokens, tokens, 0)[:, :chans]
        hidden = jnp.dot(mine_x, w_latent, preferred_element_type=F32)
        combined = hidden + shifts[2] * mixed
        final_in = (layer_norm(combined) * (1.0 + shifts[6]) + shifts[5]).astype(BF16)
        drift = jnp.dot(final_in, w_final, preferred_element_type=F32)
        increment = step_sizes[0] * drift + own_noise
        contrib = increment + jnp.where(place == 0, own_start, jnp.zeros_like(own_start))
        everyone = lax.all_to_all(
            jnp.broadcast_to(contrib[None], (steps, tokens, chans)), "step", 0, 0, tiled=True
        )
        earlier = jnp.arange(steps)[:, None, None] < place
        prefix = jnp.sum(jnp.where(earlier, everyone, 0.0), axis=0)
        result = prefix + contrib
        if iteration + 1 < ITERS:
            current = jnp.where(place == 0, own_start, prefix).astype(BF16)
            current = jnp.concatenate([current, current], axis=-1)
            latents = lax.all_to_all(
                jnp.broadcast_to(current[None], (chips, tokens, 2 * chans)),
                CHIPS,
                0,
                0,
                tiled=True,
            ).reshape(-1, 2 * chans)
    halves = result.reshape(2, rows, chans)
    kept = lax.dynamic_index_in_dim(halves, core, 0, keepdims=False)
    came = swap_cores(lax.dynamic_index_in_dim(halves, 1 - core, 0, keepdims=False))
    return jnp.stack(
        [jnp.where(core == 0, kept, came), jnp.where(core == 0, came, kept)], axis=0
    )[None]


def solution(mesh):
    steps, seq = mesh.devices.shape
    fine = Mesh(mesh.devices.reshape(steps, 4, 4, 2), ("step", "y", "x", "core"))
    placed = (
        P("step", None, SEQ, None),
        P("step", None, SEQ, None),
        P("step"),
        P("step", None, None),
        P(None, SEQ, None),
        P(),
        P(SEQ, None, None, None),
        P(SEQ, None, None, None),
        P(SEQ, None, None),
        P(),
        P(),
    )
    return jax.shard_map(
        local,
        mesh=fine,
        in_specs=placed,
        out_specs=P("step", None, SEQ, None),
        check_vma=False,
    )
```

time: 424 us -> 249 us (0.59); the launches traced: 418 us -> 247 us
  waiting for transfers between devices: 213 us -> 74.5 us
  blocking collectives: 57.3 us -> 20.6 us
  local copies, waits for them, and re-layouts: 45.3 us -> 25.8 us
  starting transfers between devices: 31 us -> 49.7 us
  other arithmetic: 18.9 us -> 26.8 us
    all_gather x2 -> x1, waiting for transfers between devices: 114 us -> 0.01 us  [local(): w_out = lax.all_gather(w_out_t.reshape(part, heads * hd), SEQ, tiled=True)]
    all_gather x2 -> x0, blocking collectives: 40 us -> none  [prefix_2(): everything = lax.all_gather(array, axis)]
    all_to_all x5 -> x7, waiting for transfers between devices: 98.8 us -> 73.6 us  [the longest x1 30.8 us: local(): packed = lax.all_to_all(packed, SEQ, 0, 0, tiled=True)]
    ppermute x0 -> x5, starting transfers between devices: none -> 12.3 us  [swap_cores(): return lax.ppermute(values, 'core', [(0, 1), (1, 0)])]
    reshape x4 -> x2, local copies, waits for them, and re-layouts: 12.6 us -> 2.14 us  [the longest x1 1.09 us: local(): jnp.transpose(w_image_qkv, (0, 2, 1, 3)).reshape(part, heads * 3 * hd)]
    all_to_all x7 -> x1, local copies, waits for them, and re-layouts: 10.9 us -> 0.51 us  [local(): lax.all_to_all(jnp.broadcast_to(contrib[None], (steps, tokens, chans)), '...]
    another operation x2 -> x0, local copies, waits for them, and re-layouts: 7.96 us -> none  [local(): weight_send = jnp.tile(stacked, (images, 1, 1))]
    all_to_all x5 -> x7, starting transfers between devices: 30.9 us -> 37.4 us  [the longest x1 7.37 us: local(): packed = lax.all_to_all(packed, SEQ, 0, 0, tiled=True)]
  transfers between devices with their start and end apart: 7 -> 13, of which waited for: 7 -> 7; matrix products, arithmetic and copies ran while one was open for 6% -> 23% of each run, Pallas kernels for 0% -> 0%
where the time goes in v1:
time: 249 us; the launch traced here: 247 us
  waiting for transfers between devices  74.5 us (30%)
  starting transfers between devices  49.7 us (20%)
  matrix products  35.1 us (14%)
  other arithmetic  26.8 us (11%)
  local copies, waits for them, and re-layouts  25.8 us (10%)
  blocking collectives  20.6 us (8%)
  between operations  14.8 us (6%)
    all_to_all x1, waiting for transfers between devices, local(): packed = lax.all_to_all(packed, SEQ, 0, 0, tiled=True)  30.8 us
    dot_general x2, matrix products, local(): lax.dot_general(attended, w_out, (((1,), (1,)), ((), ())), preferred_elem...  17.3 us
    all_to_all x2, waiting for transfers between devices, local(): lax.all_to_all(attended.reshape(chips, tokens, hd), CHIPS, 0, 0, tiled=True)  14.3 us
    ppermute x5, starting transfers between devices, swap_cores(): return lax.ppermute(values, 'core', [(0, 1), (1, 0)])  12.3 us
    all_to_all x1, waiting for transfers between devices, local(): lax.all_to_all(text_pairs.reshape(steps, -1, 2 * hd), 'step', 0, 0, tiled...  10.5 us
    all_to_all x1, blocking collectives, local(): lax.all_to_all(jnp.broadcast_to(current[None], (chips, tokens, 2 * chans)...  10.3 us
    all_to_all x1, blocking collectives, local(): lax.all_to_all(jnp.broadcast_to(contrib[None], (steps, tokens, chans)), '...  10.3 us
    all_to_all x1, waiting for transfers between devices, local(): mine = jnp.sum(lax.all_to_all(mine, CHIPS, 0, 0, tiled=True), axis=0)  10.1 us
  transfers between devices with their start and end apart: 13, of which 7 were waited for; matrix products, arithmetic and copies ran while one was open for 23% of the time, Pallas kernels for 0%

profile of v1, /device:TPU:1, one launch (start us, length us, event | category | flops | bytes accessed | tf_op | source)
XLA Modules:
  0.0 247.4 jit_solution(14756543751847404850)
XLA Ops:
  6.5 1.9 copy.73
  8.5 2.2 copy.35
  10.7 1.1 reshape.198
  12.0 1.4 slice_add_fusion.2
  13.6 3.0 %concatenate.45 = f32[80,3072]{1,0:T(8,128)} concatenate(f32[32,3072]{1,0:T(8,128)S(1)} %get-tuple-element.12, f32[1,3072]{1,0:T(1,128)S(1)} %get-tuple-element.22, f32[7,3072]{1,0:T(8,128)S(1)} %broadcast_in_dim.42, f32[32,3072]{1,0:T(8,128)S(1)} %get-tuple-element.11, f32[8,3072]{1,0:T(8,128)S(1)} %broadcast_in_dim.43), dimensions={0} | concatenate | bytes 1966080 | tf_op jit(solution)/shard_map/concatenate | solution.py:94
  18.5 1.1 constant_dynamic-slice_fusion
  19.6 3.2 %collective-permute-start.1 = (f32[40,6144]{1,0:T(8,128)}, f32[40,6144]{1,0:T(8,128)}, u32[]{:S(2)}, u32[]{:S(2)}) collective-permute-start(f32[40,6144]{1,0:T(8,128)} %constant_dynamic-slice_fusion), channel_id=1, source_target_pairs={{0,1},{1,0},{2,3},{3,2},{4,5},{5,4},{6,7},{7,6},{8,9},{9,8},{10,11... | collective-permute-start | bytes 2949128 | tf_op jit(solution)/shard_map/ppermute | solution.py:31
  23.6 6.4 %all-to-all-start.2 = ((f32[8,2,3072]{2,1,0:T(2,128)}), f32[8,2,3072]{2,1,0:T(2,128)}, u32[]{:S(2)}, u32[]{:S(2)}) async-start(f32[8,2,3072]{2,1,0:T(2,128)} %broadcast_in_dim.45), calls=%async_computation.2 | async-start | bytes 393216 | tf_op jit(solution)/shard_map/all_to_all | solution.py:60
  30.0 1.3 fusion.60
  32.7 1.1 fusion.50
  33.8 1.6 fusion.51
  35.4 1.4 broadcast_in_dim.39
  38.5 2.3 convolution_multiply_fusion.2
  41.6 1.2 pad_maximum_fusion
  43.5 1.4 broadcast_select_fusion.2
  44.9 7.4 %all-to-all-start = ((bf16[32,176,128]{2,1,0:T(8,128)(2,1)}), bf16[32,176,128]{2,1,0:T(8,128)(2,1)}, u32[]{:S(2)}, u32[]{:S(2)}) async-start(bf16[32,176,128]{2,1,0:T(8,128)(2,1)} %pad_maximum_fusion), calls=%async_computation | async-start | bytes 2883584 | tf_op jit(solution)/shard_map/all_to_all | solution.py:77
  52.3 1.2 slice_add_fusion.1
  53.5 1.3 dynamic-slice_add_fusion
  54.8 1.1 copy.72
  55.9 30.8 %all-to-all-done = bf16[32,176,128]{2,1,0:T(8,128)(2,1)} async-done(((bf16[32,176,128]{2,1,0:T(8,128)(2,1)}), bf16[32,176,128]{2,1,0:T(8,128)(2,1)}, u32[]{:S(2)}, u32[]{:S(2)}) %all-to-all-start) | async-done | bytes 1441824 | tf_op jit(solution)/shard_map/all_to_all | solution.py:77
  86.7 6.1 %all-to-all-start.1 = ((f32[16,40,384]{2,1,0:T(8,128)}), f32[16,40,384]{2,1,0:T(8,128)S(1)}, u32[]{:S(2)}, u32[]{:S(2)}) async-start(f32[16,40,384]{2,1,0:T(8,128)} %bitcast.115), calls=%async_computation.1 | async-start | bytes 1966080 | tf_op jit(solution)/shard_map/all_to_all | solution.py:107
  95.6 2.1 slice.192
  98.3 10.1 %all-to-all-done.1 = f32[16,40,384]{2,1,0:T(8,128)S(1)} async-done(((f32[16,40,384]{2,1,0:T(8,128)}), f32[16,40,384]{2,1,0:T(8,128)S(1)}, u32[]{:S(2)}, u32[]{:S(2)}) %all-to-all-start.1) | async-done | bytes 983072 | tf_op jit(solution)/shard_map/all_to_all | solution.py:107
  109.1 1.9 collective-permute-start.2
  111.1 1.9 add_convert_fusion
  113.0 1.7 slice.176
  114.7 1.7 copy.47
  118.9 1.4 fusion.47
  122.7 2.3 multiply_reduce_fusion.6
  125.1 2.3 convolution_convert_fusion
  128.4 6.8 %all-to-all-start.3 = ((bf16[8,64,256]{2,1,0:T(8,128)(2,1)}), bf16[8,64,256]{2,1,0:T(8,128)(2,1)S(1)}, u32[]{:S(2)}, u32[]{:S(2)}) async-start(bf16[8,64,256]{2,1,0:T(8,128)(2,1)} %bitcast.21), calls=%async_computation.3 | async-start | bytes 524288 | tf_op jit(solution)/shard_map/all_to_all | solution.py:126
  135.9 1.1 multiply_convert_fusion.2
  137.1 10.5 %all-to-all-done.3 = bf16[8,64,256]{2,1,0:T(8,128)(2,1)S(1)} async-done(((bf16[8,64,256]{2,1,0:T(8,128)(2,1)}), bf16[8,64,256]{2,1,0:T(8,128)(2,1)S(1)}, u32[]{:S(2)}, u32[]{:S(2)}) %all-to-all-start.3) | async-done | bytes 262176 | tf_op jit(solution)/shard_map/all_to_all | solution.py:126
  147.9 1.3 fusion
  149.2 1.9 fusion.9
  151.1 3.5 %all-to-all-start.4 = ((bf16[16,64,128]{2,1,0:T(8,128)(2,1)}), bf16[16,64,128]{2,1,0:T(8,128)(2,1)S(1)}, u32[]{:S(2)}, u32[]{:S(2)}) async-start(bf16[16,64,128]{2,1,0:T(8,128)(2,1)} %bitcast.24), calls=%async_computation.4 | async-start | bytes 524288 | tf_op jit(solution)/shard_map/all_to_all | solution.py:160
  155.6 7.3 %all-to-all-done.4 = bf16[16,64,128]{2,1,0:T(8,128)(2,1)S(1)} async-done(((bf16[16,64,128]{2,1,0:T(8,128)(2,1)}), bf16[16,64,128]{2,1,0:T(8,128)(2,1)S(1)}, u32[]{:S(2)}, u32[]{:S(2)}) %all-to-all-start.4) | async-done | bytes 262176 | tf_op jit(solution)/shard_map/all_to_all | solution.py:160
  162.9 8.6 %fusion.83 = (f32[64]{0:T(128)S(1)}, f32[64,3072]{1,0:T(8,128)S(1)}) fusion(f32[64,3072]{1,0:T(8,128)S(1)} %fusion.66, bf16[3072,2048]{1,0:T(8,128)(2,1)} %all-gather.2.cloned.1.call-done, f32[3072]{0:T(1024)S(1)} %bitcast.144, bf16[16,64,128]{2,1,0:T(8,128)(2,1)S(1)} %all-to-all-done.4), kind=kOutput, calls=%fused_computation.184 | convolution fusion | flops 805896128 | bytes 14430464 | tf_op jit(solution)/shard_map/dot_general | solution.py:164
  173.1 3.4 %all-to-all-start.5 = ((f32[8,1,4096]{2,1,0:T(1,128)}), f32[8,1,4096]{2,1,0:T(1,128)S(1)}, u32[]{:S(2)}, u32[]{:S(2)}) async-start(f32[8,1,4096]{2,1,0:T(1,128)} %reshape.212), calls=%async_computation.5 | async-start | bytes 262144 | tf_op jit(solution)/shard_map/all_to_all | solution.py:174
  176.5 7.9 %all-to-all-done.5 = f32[8,1,4096]{2,1,0:T(1,128)S(1)} async-done(((f32[8,1,4096]{2,1,0:T(1,128)}), f32[8,1,4096]{2,1,0:T(1,128)S(1)}, u32[]{:S(2)}, u32[]{:S(2)}) %all-to-all-start.5) | async-done | bytes 131104 | tf_op jit(solution)/shard_map/all_to_all | solution.py:174
  186.3 10.3 %all_to_all.45 = bf16[16,64,128]{2,1,0:T(8,128)(2,1)S(1)} all-to-all(bf16[16,64,128]{2,1,0:T(8,128)(2,1)S(1)} %broadcast_in_dim.48), channel_id=1, replica_groups=mesh['step'=8,'y'=4,'x'=4,'core'=2] {'y','x'}, dimensions={0} | all-to-all | bytes 524288 | tf_op jit(solution)/shard_map/all_to_all | solution.py:183
  197.8 1.3 fusion.1
  199.1 1.9 fusion.8
  201.0 3.8 %all-to-all-start.7 = ((bf16[16,64,128]{2,1,0:T(8,128)(2,1)}), bf16[16,64,128]{2,1,0:T(8,128)(2,1)S(1)}, u32[]{:S(2)}, u32[]{:S(2)}) async-start(bf16[16,64,128]{2,1,0:T(8,128)(2,1)} %bitcast.30), calls=%async_computation.7 | async-start | bytes 524288 | tf_op jit(solution)/shard_map/all_to_all | solution.py:160
  205.0 7.0 %all-to-all-done.7 = bf16[16,64,128]{2,1,0:T(8,128)(2,1)S(1)} async-done(((bf16[16,64,128]{2,1,0:T(8,128)(2,1)}), bf16[16,64,128]{2,1,0:T(8,128)(2,1)S(1)}, u32[]{:S(2)}, u32[]{:S(2)}) %all-to-all-start.7) | async-done | bytes 262176 | tf_op jit(solution)/shard_map/all_to_all | solution.py:160
  212.0 8.6 %fusion.84 = (f32[64]{0:T(128)S(1)}, f32[64,3072]{1,0:T(8,128)S(1)}) fusion(f32[64,3072]{1,0:T(8,128)S(1)} %fusion.64, bf16[3072,2048]{1,0:T(8,128)(2,1)} %all-gather.2.cloned.1.call-done, f32[3072]{0:T(1024)S(1)} %bitcast.145, bf16[16,64,128]{2,1,0:T(8,128)(2,1)S(1)} %all-to-all-done.7), kind=kOutput, calls=%fused_computation.185 | convolution fusion | flops 805896128 | bytes 14430464 | tf_op jit(solution)/shard_map/dot_general | solution.py:164
  221.5 10.3 %all_to_all.46 = f32[8,1,4096]{2,1,0:T(1,128)S(1)} all-to-all(f32[8,1,4096]{2,1,0:T(1,128)S(1)} %reshape.214), channel_id=1, replica_groups=mesh['step'=8,'y'=4,'x'=4,'core'=2] {'step'}, dimensions={0} | all-to-all | bytes 262144 | tf_op jit(solution)/shard_map/all_to_all | solution.py:174
  233.0 6.1 %collective-permute-start.4 = (f32[32,64]{1,0:T(8,128)S(1)}, f32[32,64]{1,0:T(8,128)S(1)}, u32[]{:S(2)}, u32[]{:S(2)}) collective-permute-start(f32[32,64]{1,0:T(8,128)S(1)} %dynamic-slice_bitcast_fusion), channel_id=1, source_target_pairs={{0,1},{1,0},{2,3},{3,2},{4,5},{5,4},{6,7},{7,6},{8,9},{9,8},{10,11... | collective-permute-start | bytes 24584 | tf_op jit(solution)/shard_map/ppermute | solution.py:31
  (140 shorter events, 26.8 us)
Async XLA Ops:
  6.5 165.3 %copy-start = (bf16[3072,64]{0,1:T(8,128)(2,1)S(1)}, bf16[3072,64]{0,1:T(8,128)(2,1)}, u32[]{:S(2)}) copy-start(bf16[3072,64]{0,1:T(8,128)(2,1)} %param.21) | copy-start | bytes 1179652
  6.5 156.4 %all-gather.2.cloned.1.call-start = ((), (), s32[]{:S(2)}) async-start(), calls=%async_computation.9 | async-start | bytes 12976128 | tf_op jit(solution)/shard_map/all_gather | solution.py:58
  8.5 3.3 %copy-start.3 = (bf16[64,3072]{1,0:T(8,128)(2,1)S(1)}, bf16[64,3072]{1,0:T(8,128)(2,1)}, u32[]{:S(2)}) copy-start(bf16[64,3072]{1,0:T(8,128)(2,1)} %param.16) | copy-start | bytes 1179652
  12.0 6.3 %copy-start.22 = (f32[64]{0:T(128)}, f32[64]{0:T(128)S(1)}, u32[]{:S(2)}) copy-start(f32[64]{0:T(128)S(1)} %broadcast_multiply_fusion.3) | copy-start | bytes 772
  18.2 4.6 %slice-start = ((f32[1,7,3072]{2,0,1:T(1,128)}), f32[1,2,3072]{2,0,1:T(1,128)S(1)}, s32[]{:S(2)}) async-start(f32[1,7,3072]{2,0,1:T(1,128)} %param.14), calls=%async_computation.10 | async-start | bytes 49152 | tf_op jit(solution)/shard_map/slice | solution.py:61
  18.5 18.2 %copy-start.5 = (bf16[96,2,16,128]{3,2,1,0:T(8,128)(2,1)S(1)}, bf16[96,2,16,128]{3,2,1,0:T(8,128)(2,1)}, u32[]{:S(2)}) copy-start(bf16[96,2,16,128]{3,2,1,0:T(8,128)(2,1)} %param.18) | copy-start | bytes 2359300
  18.5 19.5 %copy-start.21 = (f32[3,128]{1,0:T(4,128)S(1)}, f32[3,128]{1,0:T(4,128)}, u32[]{:S(2)}) copy-start(f32[3,128]{1,0:T(4,128)} %param.20) | copy-start | bytes 4612
  19.6 33.9 %collective-permute-start.1 = (f32[40,6144]{1,0:T(8,128)}, f32[40,6144]{1,0:T(8,128)}, u32[]{:S(2)}, u32[]{:S(2)}) collective-permute-start(f32[40,6144]{1,0:T(8,128)} %constant_dynamic-slice_fusion), channel_id=1, source_target_pairs={{0,1},{1,0},{2,3},{3,2},{4,5},{5,4},{6,7},{7,6},{8,9},{9,8},{10,11... | collective-permute-start | bytes 2949128 | tf_op jit(solution)/shard_map/ppermute | solution.py:31
  23.6 21.4 %all-to-all-start.2 = ((f32[8,2,3072]{2,1,0:T(2,128)}), f32[8,2,3072]{2,1,0:T(2,128)}, u32[]{:S(2)}, u32[]{:S(2)}) async-start(f32[8,2,3072]{2,1,0:T(2,128)} %broadcast_in_dim.45), calls=%async_computation.2 | async-start | bytes 393216 | tf_op jit(solution)/shard_map/all_to_all | solution.py:60
  31.4 12.1 %collective-permute-start = (f32[2,32,64]{2,1,0:T(8,128)}, f32[2,32,64]{2,1,0:T(8,128)}, u32[]{:S(2)}, u32[]{:S(2)}) collective-permute-start(f32[2,32,64]{2,1,0:T(8,128)} %fusion.60), channel_id=1, source_target_pairs={{0,1},{1,0},{2,3},{3,2},{4,5},{5,4},{6,7},{7,6},{8,9},{9,8},{10,11... | collective-permute-start | bytes 49160 | tf_op jit(solution)/shard_map/ppermute | solution.py:31
  37.0 6.5 %copy-start.11 = (f32[1,2,32,64]{3,2,1,0:T(8,128)S(1)}, f32[1,2,32,64]{3,2,1,0:T(8,128)}, u32[]{:S(2)}) copy-start(f32[1,2,32,64]{3,2,1,0:T(8,128)} %param.11) | copy-start | bytes 49156
  37.0 6.5 %copy-start.13 = (f32[1,2,32,64]{3,2,1,0:T(8,128)S(1)}, f32[1,2,32,64]{3,2,1,0:T(8,128)}, u32[]{:S(2)}) copy-start(f32[1,2,32,64]{3,2,1,0:T(8,128)} %param.12) | copy-start | bytes 49156
  44.9 41.7 %all-to-all-start = ((bf16[32,176,128]{2,1,0:T(8,128)(2,1)}), bf16[32,176,128]{2,1,0:T(8,128)(2,1)}, u32[]{:S(2)}, u32[]{:S(2)}) async-start(bf16[32,176,128]{2,1,0:T(8,128)(2,1)} %pad_maximum_fusion), calls=%async_computation | async-start | bytes 2883584 | tf_op jit(solution)/shard_map/all_to_all | solution.py:77
  86.7 21.8 %all-to-all-start.1 = ((f32[16,40,384]{2,1,0:T(8,128)}), f32[16,40,384]{2,1,0:T(8,128)S(1)}, u32[]{:S(2)}, u32[]{:S(2)}) async-start(f32[16,40,384]{2,1,0:T(8,128)} %bitcast.115), calls=%async_computation.1 | async-start | bytes 1966080 | tf_op jit(solution)/shard_map/all_to_all | solution.py:107
  97.6 25.1 %collective-permute-start.3 = (bf16[3072,128]{1,0:T(8,128)(2,1)}, bf16[3072,128]{1,0:T(8,128)(2,1)}, u32[]{:S(2)}, u32[]{:S(2)}) collective-permute-start(bf16[3072,128]{1,0:T(8,128)(2,1)} %bitcast.19), channel_id=1, source_target_pairs={{0,1},{1,0},{2,3},{3,2},{4,5},{5,4},{6,7},{7,6},{8,9},{9,8},{10,11... | collective-permute-start | bytes 2359304 | tf_op jit(solution)/shard_map/ppermute | solution.py:31
  109.1 7.3 %collective-permute-start.2 = (f32[40,384]{1,0:T(8,128)}, f32[40,384]{1,0:T(8,128)}, u32[]{:S(2)}, u32[]{:S(2)}) collective-permute-start(f32[40,384]{1,0:T(8,128)} %reduce_sum.174), channel_id=1, source_target_pairs={{0,1},{1,0},{2,3},{3,2},{4,5},{5,4},{6,7},{7,6},{8,9},{9,8},{10,11... | collective-permute-start | bytes 184328 | tf_op jit(solution)/shard_map/ppermute | solution.py:31
  116.4 4.0 %copy-start.10 = (bf16[1024,64]{0,1:T(8,128)(2,1)S(1)}, bf16[1024,64]{0,1:T(8,128)(2,1)}, u32[]{:S(2)}) copy-start(bf16[1024,64]{0,1:T(8,128)(2,1)} %copy.47) | copy-start | bytes 393220
  118.9 1.6 copy-start.6
  118.9 1.6 copy-start.8
  120.7 1.3 copy-start.1
  122.0 3.0 %copy-start.20 = (f32[128]{0:T(128)S(1)}, f32[128]{0:T(128)}, u32[]{:S(2)}) copy-start(f32[128]{0:T(128)} %get-tuple-element.30) | copy-start | bytes 1540
  127.5 20.4 %copy-start.2 = (f32[1024,384]{0,1:T(8,128)S(1)}, f32[1024,384]{0,1:T(8,128)}, u32[]{:S(2)}) copy-start(f32[1024,384]{0,1:T(8,128)} %copy-done.1) | copy-start | bytes 4718596
  127.5 20.4 %copy-start.16 = (f32[128]{0:T(128)S(1)}, f32[128]{0:T(128)}, u32[]{:S(2)}) copy-start(f32[128]{0:T(128)} %get-tuple-element.28) | copy-start | bytes 1540
  128.4 19.2 %all-to-all-start.3 = ((bf16[8,64,256]{2,1,0:T(8,128)(2,1)}), bf16[8,64,256]{2,1,0:T(8,128)(2,1)S(1)}, u32[]{:S(2)}, u32[]{:S(2)}) async-start(bf16[8,64,256]{2,1,0:T(8,128)(2,1)} %bitcast.21), calls=%async_computation.3 | async-start | bytes 524288 | tf_op jit(solution)/shard_map/all_to_all | solution.py:126
  147.9 1.3 copy-start.12
  149.2 5.5 %copy-start.4 = (bf16[64,3072]{1,0:T(8,128)(2,1)S(1)}, bf16[64,3072]{1,0:T(8,128)(2,1)}, u32[]{:S(2)}) copy-start(bf16[64,3072]{1,0:T(8,128)(2,1)} %param.16) | copy-start | bytes 1179652
  151.1 11.8 %all-to-all-start.4 = ((bf16[16,64,128]{2,1,0:T(8,128)(2,1)}), bf16[16,64,128]{2,1,0:T(8,128)(2,1)S(1)}, u32[]{:S(2)}, u32[]{:S(2)}) async-start(bf16[16,64,128]{2,1,0:T(8,128)(2,1)} %bitcast.24), calls=%async_computation.4 | async-start | bytes 524288 | tf_op jit(solution)/shard_map/all_to_all | solution.py:160
  162.9 9.0 %copy-start.14 = (f32[2,32,64]{2,1,0:T(8,128)S(1)}, f32[2,32,64]{2,1,0:T(8,128)}, u32[]{:S(2)}) copy-start(f32[2,32,64]{2,1,0:T(8,128)} %get-tuple-element.19) | copy-start | bytes 49156
  162.9 9.0 %copy-start.15 = (f32[2,32,64]{2,1,0:T(8,128)S(1)}, f32[2,32,64]{2,1,0:T(8,128)}, u32[]{:S(2)}) copy-start(f32[2,32,64]{2,1,0:T(8,128)} %get-tuple-element.20) | copy-start | bytes 49156
  162.9 9.0 %copy-start.17 = (f32[1,1,3072]{2,0,1:T(1,128)S(1)}, f32[1,1,3072]{2,0,1:T(1,128)}, u32[]{:S(2)}) copy-start(f32[1,1,3072]{2,0,1:T(1,128)} %get-tuple-element.21) | copy-start | bytes 36868
  162.9 9.0 %copy-start.18 = (f32[1,1,3072]{2,0,1:T(1,128)S(1)}, f32[1,1,3072]{2,0,1:T(1,128)}, u32[]{:S(2)}) copy-start(f32[1,1,3072]{2,0,1:T(1,128)} %get-tuple-element.25) | copy-start | bytes 36868
  171.6 25.0 %copy-start.7 = (bf16[64,448]{1,0:T(8,128)(2,1)S(1)}, bf16[64,448]{1,0:T(8,128)(2,1)}, u32[]{:S(2)}) copy-start(bf16[64,448]{1,0:T(8,128)(2,1)} %copy-done.6) | copy-start | bytes 172036
  171.6 25.0 %copy-start.9 = (bf16[64,448]{1,0:T(8,128)(2,1)S(1)}, bf16[64,448]{1,0:T(8,128)(2,1)}, u32[]{:S(2)}) copy-start(bf16[64,448]{1,0:T(8,128)(2,1)} %copy-done.8) | copy-start | bytes 172036
  173.1 11.3 %all-to-all-start.5 = ((f32[8,1,4096]{2,1,0:T(1,128)}), f32[8,1,4096]{2,1,0:T(1,128)S(1)}, u32[]{:S(2)}, u32[]{:S(2)}) async-start(f32[8,1,4096]{2,1,0:T(1,128)} %reshape.212), calls=%async_computation.5 | async-start | bytes 262144 | tf_op jit(solution)/shard_map/all_to_all | solution.py:174
  197.1 0.6 copy-start.19
  201.0 11.0 %all-to-all-start.7 = ((bf16[16,64,128]{2,1,0:T(8,128)(2,1)}), bf16[16,64,128]{2,1,0:T(8,128)(2,1)S(1)}, u32[]{:S(2)}, u32[]{:S(2)}) async-start(bf16[16,64,128]{2,1,0:T(8,128)(2,1)} %bitcast.30), calls=%async_computation.7 | async-start | bytes 524288 | tf_op jit(solution)/shard_map/all_to_all | solution.py:160
  233.0 6.9 %collective-permute-start.4 = (f32[32,64]{1,0:T(8,128)S(1)}, f32[32,64]{1,0:T(8,128)S(1)}, u32[]{:S(2)}, u32[]{:S(2)}) collective-permute-start(f32[32,64]{1,0:T(8,128)S(1)} %dynamic-slice_bitcast_fusion), channel_id=1, source_target_pairs={{0,1},{1,0},{2,3},{3,2},{4,5},{5,4},{6,7},{7,6},{8,9},{9,8},{10,11... | collective-permute-start | bytes 24584 | tf_op jit(solution)/shard_map/ppermute | solution.py:31
Sparse Core Ops, SparseCore 0:
  9.9 87.3 all-gather.1

commit v2 on v1

v2 whole, which is shorter than its diff:
```python
import math

import jax
import jax.numpy as jnp
from jax import lax
from jax.experimental import pallas as pl
from jax.experimental.pallas import tpu as pltpu
from jax.sharding import Mesh
from jax.sharding import PartitionSpec as P

ITERS = 2
CHIPS = ("y", "x")
SEQ = ("y", "x", "core")
F32, BF16 = jnp.float32, jnp.bfloat16
NT = (((1,), (1,)), ((), ()))
MIB = 1 << 20


def layer_norm(values):
    centre = values - jnp.mean(values, axis=-1, keepdims=True)
    spread = jnp.mean(centre * centre, axis=-1, keepdims=True)
    return centre * lax.rsqrt(spread + 1e-06)


def rms_scale(values, gains):
    return values * lax.rsqrt(jnp.mean(values * values, axis=-1, keepdims=True) + 1e-06) * gains


def split_high(values):
    high = lax.reduce_precision(values, 8, 7)
    return high.astype(BF16), (values - high).astype(BF16)


def swap_cores(values):
    return lax.ppermute(values, "core", [(0, 1), (1, 0)])


def own_half(values, core):
    kept = lax.dynamic_index_in_dim(values, core, 0, keepdims=False)
    came = swap_cores(lax.dynamic_index_in_dim(values, 1 - core, 0, keepdims=False))
    return jnp.where(core == 0, kept, came), jnp.where(core == 0, came, kept)


def attention_kernel(
    x_ref, folded_ref, gram_ref, bias_ref, gains_ref, text_ref, out_ref, q_ref, k_ref, v_ref
):
    hd = gains_ref.shape[1]
    chans = folded_ref.shape[0]
    pairs = x_ref.shape[0]
    text = text_ref.shape[0]
    chips, block, _ = out_ref.shape
    factor = math.log2(math.e) / math.sqrt(hd)
    x = x_ref[...]
    doubled = jnp.concatenate([x, x], axis=1)
    blank = jnp.zeros((chans, 4 * hd), BF16)
    k_ref[:text] = text_ref[:, :hd]
    v_ref[:text, :hd] = text_ref[:, hd:]
    v_ref[:, hd:] = jnp.ones((v_ref.shape[0], hd), BF16)
    for parity in range(2):
        weights = jnp.concatenate(
            [folded_ref[...], gram_ref[:, parity * hd : (parity + 1) * hd]], axis=1
        )
        high = weights.astype(BF16)
        low = (weights - high.astype(F32)).astype(BF16)
        rows = [high, blank, low, blank] if parity == 0 else [blank, high, blank, low]
        projected = jnp.dot(
            doubled, jnp.concatenate(rows, axis=0), preferred_element_type=F32
        )
        spread = jnp.sum(projected[:, 3 * hd :] * x.astype(F32), axis=1, keepdims=True)
        projected = projected[:, : 3 * hd] * lax.rsqrt(spread + 1e-06) + bias_ref[...]
        mine = pl.ds(parity * pairs, pairs)
        image = pl.ds(text + parity * pairs, pairs)
        q_ref[mine] = rms_scale(projected[:, :hd], gains_ref[0:1]).astype(BF16)
        k_ref[image] = rms_scale(projected[:, hd : 2 * hd], gains_ref[1:2]).astype(BF16)
        v_ref[image, :hd] = projected[:, 2 * hd :].astype(BF16)
    half = block // 2
    size = 256
    for start in range(0, 2 * pairs, size):
        scores = lax.dot_general(
            q_ref[start : start + size], k_ref[...], NT, preferred_element_type=F32
        )
        powers = jnp.exp2(scores * factor).astype(BF16)
        both = jnp.dot(powers, v_ref[...], preferred_element_type=F32)
        attended = (both[:, :hd] / both[:, hd:]).astype(BF16)
        parity, first = divmod(start, pairs)
        out_ref[first // half : (first + size) // half, parity * half : (parity + 1) * half] = (
            attended.reshape(size // half, half, hd)
        )


def attention(latents, folded, gram, bias, gains, text_pairs, chips):
    pairs = latents.shape[0]
    text, hd = text_pairs.shape[0], gains.shape[1]
    keys = text + 2 * pairs
    return pl.pallas_call(
        attention_kernel,
        out_shape=jax.ShapeDtypeStruct((chips, 2 * pairs // chips, hd), BF16),
        scratch_shapes=[
            pltpu.VMEM((2 * pairs, hd), BF16),
            pltpu.VMEM((keys, hd), BF16),
            pltpu.VMEM((keys, 2 * hd), BF16),
        ],
        compiler_params=pltpu.CompilerParams(vmem_limit_bytes=24 * MIB),
        cost_estimate=pl.CostEstimate(
            flops=8 * pairs * keys * hd, bytes_accessed=2 * MIB, transcendentals=2 * pairs * keys
        ),
        name="attention",
    )(latents, folded, gram, bias, gains, text_pairs)


def output_kernel(
    attended_ref, w_out_ref, x_ref, w_lat_ref, gate_ref, shift_ref, scale_ref, w_fin_ref,
    step_ref, added_ref, out_ref, rows_ref, mixed_ref
):
    at = pl.program_id(0)
    heads, tokens, hd = attended_ref.shape
    size = w_out_ref.shape[0]
    chans = w_lat_ref.shape[0] // 4

    @pl.when(at == 0)
    def _():
        for head in range(heads):
            rows_ref[:, head * hd : (head + 1) * hd] = attended_ref[head]

    mixed = lax.dot_general(rows_ref[...], w_out_ref[...], NT, preferred_element_type=F32)
    hidden = jnp.dot(x_ref[...], w_lat_ref[...], preferred_element_type=F32)
    mixed_ref[at] = hidden + gate_ref[...] * mixed

    @pl.when(at == pl.num_programs(0) - 1)
    def _():
        blocks = mixed_ref.shape[0]
        width = blocks * size
        total = jnp.zeros((tokens, 1), F32)
        for b in range(blocks):
            total += jnp.sum(mixed_ref[b], axis=1, keepdims=True)
        mean = total / width
        total = jnp.zeros((tokens, 1), F32)
        for b in range(blocks):
            centre = mixed_ref[b] - mean
            total += jnp.sum(centre * centre, axis=1, keepdims=True)
        scale = lax.rsqrt(total / width + 1e-06)
        half = tokens // 2
        drift = jnp.zeros((half, 2 * chans), F32)
        for b in range(blocks):
            cut = slice(b * size, (b + 1) * size)
            normal = (mixed_ref[b] - mean) * scale
            final_in = (normal * (1.0 + scale_ref[:, cut]) + shift_ref[:, cut]).astype(BF16)
            for parity in range(2):
                drift += lax.dot_general(
                    final_in[parity * half : (parity + 1) * half],
                    w_fin_ref[parity, :, cut],
                    NT,
                    preferred_element_type=F32,
                )
        contrib = step_ref[0] * drift + added_ref[...]
        out_ref[...] = jnp.broadcast_to(contrib[None], out_ref.shape)


def output_stage(attended, w_out, x, w_lat, gate, shift, scale, w_fin, step_size, added, steps):
    heads, tokens, hd = attended.shape
    width = w_out.shape[0]
    size = 512
    whole = lambda *shape: pl.BlockSpec(shape, lambda i: (0,) * len(shape))
    return pl.pallas_call(
        output_kernel,
        grid=(width // size,),
        in_specs=[
            whole(*attended.shape),
            pl.BlockSpec((size, heads * hd), lambda i: (i, 0)),
            whole(*x.shape),
            pl.BlockSpec((w_lat.shape[0], size), lambda i: (0, i)),
            pl.BlockSpec((1, size), lambda i: (0, i)),
            whole(1, width),
            whole(1, width),
            whole(*w_fin.shape),
            pl.BlockSpec(memory_space=pltpu.SMEM),
            whole(*added.shape),
        ],
        out_specs=whole(steps, *added.shape),
        out_shape=jax.ShapeDtypeStruct((steps,) + added.shape, F32),
        scratch_shapes=[
            pltpu.VMEM((tokens, heads * hd), BF16),
            pltpu.VMEM((width // size, tokens, size), F32),
        ],
        compiler_params=pltpu.CompilerParams(vmem_limit_bytes=32 * MIB),
        cost_estimate=pl.CostEstimate(
            flops=2 * tokens * width * heads * hd,
            bytes_accessed=2 * width * heads * hd,
            transcendentals=tokens,
        ),
        name="output_stage",
    )(attended, w_out, x, w_lat, gate, shift, scale, w_fin, step_size, added)


def scan_kernel(place_ref, everyone_ref, mine_ref, start_ref, out_ref, x_ref):
    place = place_ref[0]
    prefix = jnp.zeros(start_ref.shape, F32)
    for step in range(everyone_ref.shape[0]):
        prefix += jnp.where(step < place, everyone_ref[step], 0.0)
    out_ref[...] = prefix + mine_ref[0]
    current = jnp.where(place == 0, start_ref[...], prefix).astype(BF16)
    x_ref[...] = jnp.broadcast_to(current[None], x_ref.shape)


def scan(place, everyone, mine, start, chips):
    return pl.pallas_call(
        scan_kernel,
        in_specs=[pl.BlockSpec(memory_space=pltpu.SMEM)]
        + [pl.BlockSpec(memory_space=pltpu.VMEM)] * 3,
        out_shape=(
            jax.ShapeDtypeStruct(start.shape, F32),
            jax.ShapeDtypeStruct((chips,) + start.shape, BF16),
        ),
        name="scan",
    )(place, everyone, mine, start)


def local(
    trajectory,
    noise,
    step_sizes,
    modulation,
    text_states,
    w_latent,
    w_image_qkv,
    w_text_kv,
    w_out_t,
    qk_gains,
    w_final,
):
    steps = lax.axis_size("step")
    chips = lax.axis_size(CHIPS)
    place, core = lax.axis_index("step"), lax.axis_index("core")
    seq = lax.axis_index(SEQ)
    images, rows, chans = trajectory.shape[1:]
    width = w_latent.shape[1]
    part, heads, hd = w_out_t.shape
    text_rows = text_states.shape[1] // steps
    shifts = modulation[0]

    w_out_mine = w_out_t.reshape(part, heads * hd)
    mods_mine = jnp.broadcast_to(shifts[None, 3:5], (steps, 2, width))
    w_out_mine, mods_mine, text_states, w_text_kv, trajectory = lax.optimization_barrier(
        (w_out_mine, mods_mine, text_states, w_text_kv, trajectory)
    )
    w_out = lax.all_gather(w_out_mine, SEQ, tiled=True)

    mods = lax.all_to_all(mods_mine, "step", 0, 0, tiled=True)

    text_mine = lax.dynamic_slice_in_dim(text_states, place * text_rows, text_rows, 1)
    text_norm = layer_norm(text_mine.astype(F32)).astype(BF16)
    text_block = jnp.broadcast_to(
        text_norm.reshape(1, images, text_rows * width // hd, hd),
        (chips, images, text_rows * width // hd, hd),
    ).reshape(chips * images, -1, hd)
    weight_block = jnp.transpose(w_text_kv, (2, 1, 0, 3)).reshape(2 * heads, part, hd)
    start_pairs = trajectory[0].reshape(images, rows // 2, 2 * chans)
    latent_block = jnp.broadcast_to(
        start_pairs.astype(BF16)[None], (chips, images, rows // 2, 2 * chans)
    ).reshape(chips * images, rows // 2, 2 * chans)
    packed = jnp.concatenate([weight_block, text_block, latent_block], axis=1)
    (
        packed, mods, w_latent, w_image_qkv, shifts, noise, start_pairs, w_final
    ) = lax.optimization_barrier(
        (packed, mods, w_latent, w_image_qkv, shifts, noise, start_pairs, w_final)
    )
    packed = lax.all_to_all(packed, SEQ, 0, 0, tiled=True)

    w_lat = w_latent.astype(F32)
    centred = w_lat - jnp.mean(w_lat, axis=1, keepdims=True)
    gram = (
        lax.dot_general(centred, centred, NT, precision=lax.Precision.HIGHEST) / width
    )
    half = chans // 2
    scaled = centred * (1.0 + shifts[1])
    pad = jnp.zeros((7, width), F32)
    left = jnp.concatenate(
        [scaled[:half], shifts[0:1], pad, scaled[half:], jnp.zeros((8, width), F32)], axis=0
    )
    left = lax.dynamic_slice_in_dim(left, seq * part, part, 1)
    stacked = jnp.concatenate(split_high(left), axis=0)
    columns = jnp.transpose(w_image_qkv, (0, 2, 1, 3)).reshape(part, heads * 3 * hd)
    partial = jnp.dot(stacked, columns, preferred_element_type=F32)
    count = left.shape[0]
    partial = partial[:count] + partial[count:]
    mine = lax.dynamic_slice_in_dim(partial, core * (count // 2), count // 2, 0)
    other = lax.dynamic_slice_in_dim(partial, (1 - core) * (count // 2), count // 2, 0)
    mine = mine + swap_cores(other)
    mine = jnp.transpose(mine.reshape(count // 2, heads, 3 * hd), (1, 0, 2))

    noise_pairs = noise[0].reshape(images, rows // 2, 2 * chans)
    own = jnp.concatenate(
        own_half(jnp.stack([noise_pairs, start_pairs], axis=1), core), axis=1
    )
    own_noise, own_start = own[0], own[1]
    added = own_noise + jnp.where(place == 0, own_start, jnp.zeros_like(own_start))
    zeros = jnp.zeros_like(w_latent)
    w_lat_pairs = jnp.concatenate([w_latent, zeros, zeros, w_latent], axis=0)
    w_fin = jnp.swapaxes(w_final, 0, 1)
    w_fin_pairs = jnp.stack(
        [
            jnp.concatenate([w_fin, jnp.zeros_like(w_fin)], axis=0),
            jnp.concatenate([jnp.zeros_like(w_fin), w_fin], axis=0),
        ]
    )
    gram_blank = jnp.zeros((chans, 2 * chans), F32)
    gram_pairs = jnp.concatenate([gram, gram_blank, gram], axis=1)

    mine, packed = lax.optimization_barrier((mine, packed))
    mine = lax.all_to_all(mine, CHIPS, 0, 0, tiled=True)

    cut = packed.shape[1] - rows // 2
    w_text_mine = packed[:, :part].reshape(width, hd)
    text_here = packed[:, part:cut].reshape(-1, width)
    latents = packed[:, cut:].reshape(-1, 2 * chans)
    w_text_other = swap_cores(w_text_mine)
    w_keys = jnp.where(core == 0, w_text_mine, w_text_other)
    w_values = jnp.where(core == 0, w_text_other, w_text_mine)
    text_in = (
        text_here.astype(F32)[None] * (1.0 + mods[:, 1][:, None]) + mods[:, 0][:, None]
    ).astype(BF16)
    text_in = text_in.reshape(-1, width)
    text_keys = rms_scale(jnp.dot(text_in, w_keys, preferred_element_type=F32), qk_gains[2])
    text_values = jnp.dot(text_in, w_values, preferred_element_type=F32)
    text_pairs = jnp.concatenate([text_keys.astype(BF16), text_values.astype(BF16)], axis=1)
    text_pairs = text_pairs.reshape(steps, -1, 2 * hd)

    text_pairs, mine = lax.optimization_barrier((text_pairs, mine))
    text_pairs = lax.all_to_all(text_pairs, "step", 0, 0, tiled=True).reshape(-1, 2 * hd)
    mine = jnp.sum(mine, axis=0)
    theirs = swap_cores(mine)
    first = jnp.where(core == 0, mine, theirs)
    second = jnp.where(core == 0, theirs, mine)
    folded = jnp.concatenate([first[:half], second[:half]], axis=0)
    bias = first[half : half + 1]

    place_ref = place.reshape(1).astype(jnp.int32)
    x_own = own_start.astype(BF16)
    result = own_start
    for iteration in range(ITERS):
        attended = attention(latents, folded, gram_pairs, bias, qk_gains, text_pairs, chips)
        attended = lax.all_to_all(attended, CHIPS, 0, 0, tiled=True)
        blank = jnp.zeros_like(x_own)
        x_rows = jnp.concatenate(
            [
                jnp.concatenate([x_own, blank], axis=1),
                jnp.concatenate([blank, x_own], axis=1),
            ],
            axis=0,
        )
        contrib = output_stage(
            attended,
            w_out,
            x_rows,
            w_lat_pairs,
            shifts[2:3],
            shifts[5:6],
            shifts[6:7],
            w_fin_pairs,
            step_sizes,
            added,
            steps,
        )
        everyone = lax.all_to_all(contrib, "step", 0, 0, tiled=True)
        result, latents = scan(place_ref, everyone, contrib, own_start, chips)
        if iteration + 1 < ITERS:
            x_own = latents[0]
            latents = lax.all_to_all(latents, CHIPS, 0, 0, tiled=True).reshape(-1, 2 * chans)
    first, second = own_half(
        jnp.swapaxes(result.reshape(1, 2, rows // 2, 2 * chans), 0, 1), core
    )
    return jnp.concatenate([first, second], axis=0).reshape(1, images, rows, chans)


def solution(mesh):
    steps = mesh.devices.shape[0]
    fine = Mesh(mesh.devices.reshape(steps, 4, 4, 2), ("step", "y", "x", "core"))
    placed = (
        P("step", None, SEQ, None),
        P("step", None, SEQ, None),
        P("step"),
        P("step", None, None),
        P(None, SEQ, None),
        P(),
        P(SEQ, None, None, None),
        P(SEQ, None, None, None),
        P(SEQ, None, None),
        P(),
        P(),
    )
    return jax.shard_map(
        local,
        mesh=fine,
        in_specs=placed,
        out_specs=P("step", None, SEQ, None),
        check_vma=False,
    )
```

time: 249 us -> 241 us (0.968)
  matrix products: 35.1 us -> 6.86 us
  Pallas kernels: 0 us -> 20.5 us
  waiting for transfers between devices: 74.5 us -> 56.7 us
  local copies, waits for them, and re-layouts: 25.8 us -> 42.6 us
  blocking collectives: 20.6 us -> 32.4 us
  other arithmetic: 26.8 us -> 20.5 us
  starting transfers between devices: 49.7 us -> 44.3 us
    dot_general x13 -> x1, matrix products: 29.8 us -> 1.55 us  [local(): lax.dot_general(centred, centred, NT, precision=lax.Precision.HIGHEST)]
    pallas_call x0 -> x6, Pallas kernels: none -> 20.5 us  [the longest x2 11.8 us: output_stage(): pl.pallas_call(output_kernel, grid=(width // size,), in_specs=[whole(*att...]
    unnamed x58 -> x86, local copies, waits for them, and re-layouts: 6.84 us -> 27.1 us
    all_to_all x2 -> x3, blocking collectives: 20.6 us -> 32.4 us  [the longest x2 22.1 us: local(): everyone = lax.all_to_all(contrib, 'step', 0, 0, tiled=True)]
    all_to_all x6 -> x5, waiting for transfers between devices: 42.9 us -> 33.7 us  [the longest x2 13 us: local(): attended = lax.all_to_all(attended, CHIPS, 0, 0, tiled=True)]
    all_to_all x1, waiting for transfers between devices: 30.8 us -> 22.2 us  [local(): packed = lax.all_to_all(packed, SEQ, 0, 0, tiled=True)]
    all_to_all x6 -> x5, starting transfers between devices: 30.1 us -> 24.7 us  [the longest x1 9.03 us: local(): mods = lax.all_to_all(mods_mine, 'step', 0, 0, tiled=True)]
    concatenate x2 -> x6, other arithmetic: 0.16 us -> 3.68 us  [the longest x1 1.54 us: local(): gram_pairs = jnp.concatenate([gram, gram_blank, gram], axis=1)]
  transfers between devices with their start and end apart: 13 -> 12, of which waited for: 7 -> 7; matrix products, arithmetic and copies ran while one was open for 23% -> 17% of each run, Pallas kernels for 0% -> 1%
where the time goes in v2:
time: 241 us; the launch traced here: 238 us
  waiting for transfers between devices  56.7 us (24%)
  starting transfers between devices  44.3 us (18%)
  local copies, waits for them, and re-layouts  42.6 us (18%)
  blocking collectives  32.4 us (13%)
  other arithmetic  20.5 us (9%)
  Pallas kernels  20.5 us (9%)
  between operations  14.7 us (6%)
  matrix products  6.86 us (3%)
    unnamed x86, local copies, waits for them, and re-layouts  27.1 us
    all_to_all x1, waiting for transfers between devices, local(): packed = lax.all_to_all(packed, SEQ, 0, 0, tiled=True)  22.2 us
    all_to_all x2, blocking collectives, local(): everyone = lax.all_to_all(contrib, 'step', 0, 0, tiled=True)  22.1 us
    all_to_all x2, waiting for transfers between devices, local(): attended = lax.all_to_all(attended, CHIPS, 0, 0, tiled=True)  13 us
    ppermute x5, starting transfers between devices, swap_cores(): return lax.ppermute(values, 'core', [(0, 1), (1, 0)])  11.9 us
    pallas_call x2, Pallas kernels, output_stage(): pl.pallas_call(output_kernel, grid=(width // size,), in_specs=[whole(*att...  11.8 us
    all_to_all x1, blocking collectives, local(): lax.all_to_all(latents, CHIPS, 0, 0, tiled=True).reshape(-1, 2 * chans)  10.3 us
    all_to_all x1, waiting for transfers between devices, local(): lax.all_to_all(text_pairs, 'step', 0, 0, tiled=True).reshape(-1, 2 * hd)  9.99 us
  transfers between devices with their start and end apart: 12, of which 7 were waited for; matrix products, arithmetic and copies ran while one was open for 17% of the time, Pallas kernels for 1%

profile of v2, /device:TPU:1, one launch (start us, length us, event | category | flops | bytes accessed | tf_op | source)
XLA Modules:
  0.0 238.5 jit_solution(4933634664920716913)
XLA Ops:
  6.5 1.9 copy.36
  10.0 9.0 %all-to-all-start = ((f32[8,2,3072]{2,1,0:T(2,128)}), f32[8,2,3072]{2,1,0:T(2,128)S(1)}, u32[]{:S(2)}, u32[]{:S(2)}) async-start(f32[8,2,3072]{2,1,0:T(2,128)} %broadcast_in_dim.19), calls=%async_computation | async-start | bytes 393216 | tf_op jit(solution)/shard_map/all_to_all | solution.py:248
  19.9 1.0 convert_reduce_fusion.1
  21.0 1.1 fusion.13
  22.1 1.0 fusion.14
  24.5 1.2 pad_maximum_fusion.2
  25.7 2.1 all-to-all-done
  28.5 2.6 %collective-permute-start.3 = (f32[2,16,128]{2,1,0:T(8,128)}, f32[2,16,128]{2,1,0:T(8,128)}, u32[]{:S(2)}, u32[]{:S(2)}) collective-permute-start(f32[2,16,128]{2,1,0:T(8,128)} %fusion.25), channel_id=1, source_target_pairs={{0,1},{1,0},{2,3},{3,2},{4,5},{5,4},{6,7},{7,6},{8,9},{9,8},{10,11... | collective-permute-start | bytes 49160 | tf_op jit(solution)/shard_map/ppermute | solution.py:35
  32.0 1.1 reshape.92
  34.2 1.0 concatenate.55
  36.2 1.3 copy-done.24
  37.4 1.0 constant_dynamic-slice_fusion
  38.5 7.6 %all-to-all-start.1 = ((bf16[32,160,128]{2,1,0:T(8,128)(2,1)}), bf16[32,160,128]{2,1,0:T(8,128)(2,1)}, u32[]{:S(2)}, u32[]{:S(2)}) async-start(bf16[32,160,128]{2,1,0:T(8,128)(2,1)} %pad_maximum_fusion.2), calls=%async_computation.1 | async-start | bytes 2621440 | tf_op jit(solution)/shard_map/all_to_all | solution.py:267
  47.4 1.5 convolution_multiply_fusion
  49.2 1.3 dynamic-slice_add_fusion
  50.5 1.0 copy.35
  51.5 22.2 %all-to-all-done.1 = bf16[32,160,128]{2,1,0:T(8,128)(2,1)} async-done(((bf16[32,160,128]{2,1,0:T(8,128)(2,1)}), bf16[32,160,128]{2,1,0:T(8,128)(2,1)}, u32[]{:S(2)}, u32[]{:S(2)}) %all-to-all-start.1) | async-done | bytes 1310752 | tf_op jit(solution)/shard_map/all_to_all | solution.py:267
  73.7 2.1 slice.81
  75.8 1.8 collective-permute-start.1
  77.6 2.0 slice_convert_fusion
  79.6 2.2 reshape.100
  81.8 4.3 %all-to-all-start.2 = ((f32[16,40,384]{2,1,0:T(8,128)}), f32[16,40,384]{2,1,0:T(8,128)}, u32[]{:S(2)}, u32[]{:S(2)}) async-start(f32[16,40,384]{2,1,0:T(8,128)} %bitcast.80), calls=%async_computation.2 | async-start | bytes 1966080 | tf_op jit(solution)/shard_map/all_to_all | solution.py:310
  86.2 1.8 add_convert_fusion
  88.0 2.3 multiply_reduce_fusion
  90.5 2.3 convolution_convert_fusion
  93.6 8.6 %all-to-all-done.2 = f32[16,40,384]{2,1,0:T(8,128)} async-done(((f32[16,40,384]{2,1,0:T(8,128)}), f32[16,40,384]{2,1,0:T(8,128)}, u32[]{:S(2)}, u32[]{:S(2)}) %all-to-all-start.2) | async-done | bytes 983072 | tf_op jit(solution)/shard_map/all_to_all | solution.py:310
  102.2 1.9 reduce_sum.49
  104.1 1.6 collective-permute-start.2
  105.8 1.5 pad_maximum_fusion.5.gram_ref
  108.2 4.3 %all-to-all-start.3 = ((bf16[8,64,256]{2,1,0:T(8,128)(2,1)}), bf16[8,64,256]{2,1,0:T(8,128)(2,1)S(1)}, u32[]{:S(2)}, u32[]{:S(2)}) async-start(bf16[8,64,256]{2,1,0:T(8,128)(2,1)} %bitcast.86), calls=%async_computation.3 | async-start | bytes 524288 | tf_op jit(solution)/shard_map/all_to_all | solution.py:329
  114.9 10.0 %all-to-all-done.3 = bf16[8,64,256]{2,1,0:T(8,128)(2,1)S(1)} async-done(((bf16[8,64,256]{2,1,0:T(8,128)(2,1)}), bf16[8,64,256]{2,1,0:T(8,128)(2,1)S(1)}, u32[]{:S(2)}, u32[]{:S(2)}) %all-to-all-start.3) | async-done | bytes 262176 | tf_op jit(solution)/shard_map/all_to_all | solution.py:329
  124.9 1.0 copy-done.16
  126.7 2.7 %attention.2 = bf16[16,64,128]{2,1,0:T(8,128)(2,1)S(1)} custom-call(bf16[512,128]{1,0:T(8,128)(2,1)S(1)} %bitcast.76, f32[64,384]{1,0:T(8,128)S(1)} %copy-done.16, f32[64,256]{1,0:T(8,128)S(1)} %copy-done.18, f32[1,384]{1,0:T(1,128)S(1)} %slice.99.bias_ref, f32[3,128]{1,0:T(4,128)S(1)} %copy-done.22, bf16[512,256]{1,0:T(8,128)(2,1)S(1)} %bitcast.74), custom_call_target="tpu_custom_call" | custom-call | flops 805306368 | bytes 2097152 | tf_op jit(solution)/shard_map/attention/pallas_call | solution.py:95
  130.1 3.5 %all-to-all-start.4 = ((bf16[16,64,128]{2,1,0:T(8,128)(2,1)}), bf16[16,64,128]{2,1,0:T(8,128)(2,1)S(1)}, u32[]{:S(2)}, u32[]{:S(2)}) async-start(bf16[16,64,128]{2,1,0:T(8,128)(2,1)} %copy-done.6), calls=%async_computation.4 | async-start | bytes 524288 | tf_op jit(solution)/shard_map/all_to_all | solution.py:342
  135.2 6.8 %all-to-all-done.4.attended_ref = bf16[16,64,128]{2,1,0:T(8,128)(2,1)S(1)} async-done(((bf16[16,64,128]{2,1,0:T(8,128)(2,1)}), bf16[16,64,128]{2,1,0:T(8,128)(2,1)S(1)}, u32[]{:S(2)}, u32[]{:S(2)}) %all-to-all-start.4) | async-done | bytes 262176 | tf_op jit(solution)/shard_map/all_to_all | solution.py:342
  142.0 4.6 %copy-done = bf16[3072,2048]{1,0:T(8,128)(2,1)S(1)} copy-done((bf16[3072,2048]{1,0:T(8,128)(2,1)S(1)}, bf16[3072,2048]{1,0:T(8,128)(2,1)}, u32[]{:S(2)}) %copy-start) | copy-done | bytes 12582936
  149.4 5.9 %output_stage.2.mine_ref = f32[8,32,128]{2,1,0:T(8,128)S(1)} custom-call(bf16[16,64,128]{2,1,0:T(8,128)(2,1)S(1)} %all-to-all-done.4.attended_ref, bf16[3072,2048]{1,0:T(8,128)(2,1)S(1)} %copy-done, bf16[64,256]{1,0:T(8,128)(2,1)S(1)} %copy-done.9, bf16[256,3072]{1,0:T(8,128)(2,1)S(1)} %pad_maximum_fusion.w_lat_ref, f32[1,3072]{1,0:T(1,128)S(1)} %copy-done.14, ...), custom_call_target="tpu_custom_call" | custom-call | flops 805306368 | bytes 12582912 | tf_op jit(solution)/shard_map/output_stage/pallas_call | solution.py:164
  155.3 11.1 %all_to_all.45.everyone_ref = f32[8,32,128]{2,1,0:T(8,128)} all-to-all(f32[8,32,128]{2,1,0:T(8,128)S(1)} %output_stage.2.mine_ref), channel_id=1, replica_groups=mesh['step'=8,'y'=4,'x'=4,'core'=2] {'step'}, dimensions={0} | all-to-all | bytes 262144 | tf_op jit(solution)/shard_map/all_to_all | solution.py:364
  166.4 1.7 scan.2
  168.1 10.3 %all_to_all.46 = bf16[16,32,128]{2,1,0:T(8,128)(2,1)S(1)} all-to-all(bf16[16,32,128]{2,1,0:T(8,128)(2,1)} %get-tuple-element.41), channel_id=1, replica_groups=mesh['step'=8,'y'=4,'x'=4,'core'=2] {'y','x'}, dimensions={0} | all-to-all | bytes 262144 | tf_op jit(solution)/shard_map/all_to_all | solution.py:368
  182.4 2.7 %attention.3 = bf16[16,64,128]{2,1,0:T(8,128)(2,1)S(1)} custom-call(bf16[512,128]{1,0:T(8,128)(2,1)S(1)} %bitcast.77, f32[64,384]{1,0:T(8,128)S(1)} %copy-done.17, f32[64,256]{1,0:T(8,128)S(1)} %copy-done.19, f32[1,384]{1,0:T(1,128)S(1)} %copy-done.21, f32[3,128]{1,0:T(4,128)S(1)} %copy-done.23, bf16[512,256]{1,0:T(8,128)(2,1)S(1)} %bitcast.75), custom_call_target="tpu_custom_call" | custom-call | flops 805306368 | bytes 2097152 | tf_op jit(solution)/shard_map/attention/pallas_call | solution.py:95
  185.9 3.5 %all-to-all-start.7 = ((bf16[16,64,128]{2,1,0:T(8,128)(2,1)}), bf16[16,64,128]{2,1,0:T(8,128)(2,1)S(1)}, u32[]{:S(2)}, u32[]{:S(2)}) async-start(bf16[16,64,128]{2,1,0:T(8,128)(2,1)} %copy-done.7), calls=%async_computation.7 | async-start | bytes 524288 | tf_op jit(solution)/shard_map/all_to_all | solution.py:342
  190.7 6.2 %all-to-all-done.7.attended_ref = bf16[16,64,128]{2,1,0:T(8,128)(2,1)S(1)} async-done(((bf16[16,64,128]{2,1,0:T(8,128)(2,1)}), bf16[16,64,128]{2,1,0:T(8,128)(2,1)S(1)}, u32[]{:S(2)}, u32[]{:S(2)}) %all-to-all-start.7) | async-done | bytes 262176 | tf_op jit(solution)/shard_map/all_to_all | solution.py:342
  196.9 4.6 %copy-done.1 = bf16[3072,2048]{1,0:T(8,128)(2,1)S(1)} copy-done((bf16[3072,2048]{1,0:T(8,128)(2,1)S(1)}, bf16[3072,2048]{1,0:T(8,128)(2,1)}, u32[]{:S(2)}) %copy-start.1) | copy-done | bytes 12582936
  204.4 5.9 %output_stage.3.mine_ref = f32[8,32,128]{2,1,0:T(8,128)S(1)} custom-call(bf16[16,64,128]{2,1,0:T(8,128)(2,1)S(1)} %all-to-all-done.7.attended_ref, bf16[3072,2048]{1,0:T(8,128)(2,1)S(1)} %copy-done.1, bf16[64,256]{1,0:T(8,128)(2,1)S(1)} %copy-done.8, bf16[256,3072]{1,0:T(8,128)(2,1)S(1)} %pad_maximum_fusion.w_lat_ref, f32[1,3072]{1,0:T(1,128)S(1)} %copy-done.15, ...), custom_call_target="tpu_custom_call" | custom-call | flops 805306368 | bytes 12582912 | tf_op jit(solution)/shard_map/output_stage/pallas_call | solution.py:164
  210.3 11.0 %all_to_all.47.everyone_ref = f32[8,32,128]{2,1,0:T(8,128)} all-to-all(f32[8,32,128]{2,1,0:T(8,128)S(1)} %output_stage.3.mine_ref), channel_id=1, replica_groups=mesh['step'=8,'y'=4,'x'=4,'core'=2] {'step'}, dimensions={0} | all-to-all | bytes 262144 | tf_op jit(solution)/shard_map/all_to_all | solution.py:364
  221.3 1.6 scan.3
  223.6 5.8 %collective-permute-start.4 = (f32[1,16,128]{2,1,0:T(8,128)S(1)}, f32[1,16,128]{2,1,0:T(8,128)S(1)}, u32[]{:S(2)}, u32[]{:S(2)}) collective-permute-start(f32[1,16,128]{2,1,0:T(8,128)S(1)} %dynamic-slice_bitcast_fusion), channel_id=1, source_target_pairs={{0,1},{1,0},{2,3},{3,2},{4,5},{5,4},{6,7},{7,6},{8,9},{9,8},{10,11... | collective-permute-start | bytes 24584 | tf_op jit(solution)/shard_map/ppermute | solution.py:35
  (142 shorter events, 30.0 us)
Async XLA Ops:
  6.5 16.5 %copy-start.37 = (f32[1,2,32,64]{3,2,1,0:T(8,128)S(1)}, f32[1,2,32,64]{3,2,1,0:T(8,128)}, u32[]{:S(2)}) copy-start(f32[1,2,32,64]{3,2,1,0:T(8,128)} %param.11) | copy-start | bytes 49156
  6.5 16.6 %copy-start.28 = (bf16[96,2,16,128]{3,2,1,0:T(8,128)(2,1)S(1)}, bf16[96,2,16,128]{3,2,1,0:T(8,128)(2,1)}, u32[]{:S(2)}) copy-start(bf16[96,2,16,128]{3,2,1,0:T(8,128)(2,1)} %param.18) | copy-start | bytes 2359300
  6.5 135.4 %all-gather.2.cloned.1.call-start = ((), (), s32[]{:S(2)}) async-start(), calls=%async_computation.9 | async-start | bytes 12976128 | tf_op jit(solution)/shard_map/all_gather | solution.py:246
  10.0 17.8 %all-to-all-start = ((f32[8,2,3072]{2,1,0:T(2,128)}), f32[8,2,3072]{2,1,0:T(2,128)S(1)}, u32[]{:S(2)}, u32[]{:S(2)}) async-start(f32[8,2,3072]{2,1,0:T(2,128)} %broadcast_in_dim.19), calls=%async_computation | async-start | bytes 393216 | tf_op jit(solution)/shard_map/all_to_all | solution.py:248
  23.2 4.7 %copy-start.34 = (f32[2,16,128]{2,1,0:T(8,128)}, f32[2,16,128]{2,1,0:T(8,128)S(1)}, u32[]{:S(2)}) copy-start(f32[2,16,128]{2,1,0:T(8,128)S(1)} %reshape_squeeze.3) | copy-start | bytes 49156
  23.5 2.2 copy-start.22
  23.5 4.3 %copy-start.38 = (f32[1,2,32,64]{3,2,1,0:T(8,128)S(1)}, f32[1,2,32,64]{3,2,1,0:T(8,128)}, u32[]{:S(2)}) copy-start(f32[1,2,32,64]{3,2,1,0:T(8,128)} %param.12) | copy-start | bytes 49156
  23.5 7.6 %copy-start.27 = (bf16[96,3,16,128]{3,2,1,0:T(8,128)(2,1)S(1)}, bf16[96,3,16,128]{3,2,1,0:T(8,128)(2,1)}, u32[]{:S(2)}) copy-start(bf16[96,3,16,128]{3,2,1,0:T(8,128)(2,1)} %param.17) | copy-start | bytes 3538948
  27.8 5.3 %copy-start.29 = (f32[8,2,3072]{2,1,0:T(2,128)}, f32[8,2,3072]{2,1,0:T(2,128)S(1)}, u32[]{:S(2)}) copy-start(f32[8,2,3072]{2,1,0:T(2,128)S(1)} %all-to-all-done) | copy-start | bytes 589828
  27.9 5.3 %copy-start.36 = (f32[2,1,16,128]{3,2,0,1:T(8,128)}, f32[2,1,16,128]{3,2,0,1:T(8,128)S(1)}, u32[]{:S(2)}) copy-start(f32[2,1,16,128]{3,2,0,1:T(8,128)S(1)} %stack_reshape_squeeze.3) | copy-start | bytes 49156
  28.5 105.2 %collective-permute-start.3 = (f32[2,16,128]{2,1,0:T(8,128)}, f32[2,16,128]{2,1,0:T(8,128)}, u32[]{:S(2)}, u32[]{:S(2)}) collective-permute-start(f32[2,16,128]{2,1,0:T(8,128)} %fusion.25), channel_id=1, source_target_pairs={{0,1},{1,0},{2,3},{3,2},{4,5},{5,4},{6,7},{7,6},{8,9},{9,8},{10,11... | collective-permute-start | bytes 49160 | tf_op jit(solution)/shard_map/ppermute | solution.py:35
  32.0 1.1 copy-start.26
  36.2 1.3 copy-start.24
  37.4 8.7 %copy-start.31 = (bf16[3072,64]{0,1:T(8,128)(2,1)S(1)}, bf16[3072,64]{0,1:T(8,128)(2,1)}, u32[]{:S(2)}) copy-start(bf16[3072,64]{0,1:T(8,128)(2,1)} %param.21) | copy-start | bytes 1179652
  38.5 7.8 %copy-start.30 = (f32[8,2,3072]{2,1,0:T(2,128)S(1)}, f32[8,2,3072]{2,1,0:T(2,128)}, u32[]{:S(2)}) copy-start(f32[8,2,3072]{2,1,0:T(2,128)} %copy-done.29) | copy-start | bytes 589828
  38.5 10.7 %collective-permute-start = (f32[40,6144]{1,0:T(8,128)}, f32[40,6144]{1,0:T(8,128)}, u32[]{:S(2)}, u32[]{:S(2)}) collective-permute-start(f32[40,6144]{1,0:T(8,128)} %constant_dynamic-slice_fusion), channel_id=1, source_target_pairs={{0,1},{1,0},{2,3},{3,2},{4,5},{5,4},{6,7},{7,6},{8,9},{9,8},{10,11... | collective-permute-start | bytes 2949128 | tf_op jit(solution)/shard_map/ppermute | solution.py:35
  38.5 35.3 %all-to-all-start.1 = ((bf16[32,160,128]{2,1,0:T(8,128)(2,1)}), bf16[32,160,128]{2,1,0:T(8,128)(2,1)}, u32[]{:S(2)}, u32[]{:S(2)}) async-start(bf16[32,160,128]{2,1,0:T(8,128)(2,1)} %pad_maximum_fusion.2), calls=%async_computation.1 | async-start | bytes 2621440 | tf_op jit(solution)/shard_map/all_to_all | solution.py:267
  46.3 1.0 copy-start.40
  47.4 1.8 copy-start.25
  75.8 12.2 %collective-permute-start.1 = (bf16[3072,128]{1,0:T(8,128)(2,1)}, bf16[3072,128]{1,0:T(8,128)(2,1)}, u32[]{:S(2)}, u32[]{:S(2)}) collective-permute-start(bf16[3072,128]{1,0:T(8,128)(2,1)} %bitcast.10), channel_id=1, source_target_pairs={{0,1},{1,0},{2,3},{3,2},{4,5},{5,4},{6,7},{7,6},{8,9},{9,8},{10,11... | collective-permute-start | bytes 2359304 | tf_op jit(solution)/shard_map/ppermute | solution.py:35
  79.6 6.5 %copy-start.32 = (f32[8,3072]{1,0:T(8,128)S(1)}, f32[8,3072]{1,0:T(8,128)}, u32[]{:S(2)}) copy-start(f32[8,3072]{1,0:T(8,128)} %get-tuple-element.64) | copy-start | bytes 294916
  79.6 6.6 %copy-start.33 = (f32[8,3072]{1,0:T(8,128)S(1)}, f32[8,3072]{1,0:T(8,128)}, u32[]{:S(2)}) copy-start(f32[8,3072]{1,0:T(8,128)} %get-tuple-element.65) | copy-start | bytes 294916
  81.8 20.4 %all-to-all-start.2 = ((f32[16,40,384]{2,1,0:T(8,128)}), f32[16,40,384]{2,1,0:T(8,128)}, u32[]{:S(2)}, u32[]{:S(2)}) async-start(f32[16,40,384]{2,1,0:T(8,128)} %bitcast.80), calls=%async_computation.2 | async-start | bytes 1966080 | tf_op jit(solution)/shard_map/all_to_all | solution.py:310
  104.1 8.4 %collective-permute-start.2 = (f32[40,384]{1,0:T(8,128)}, f32[40,384]{1,0:T(8,128)}, u32[]{:S(2)}, u32[]{:S(2)}) collective-permute-start(f32[40,384]{1,0:T(8,128)} %reduce_sum.49), channel_id=1, source_target_pairs={{0,1},{1,0},{2,3},{3,2},{4,5},{5,4},{6,7},{7,6},{8,9},{9,8},{10,11... | collective-permute-start | bytes 184328 | tf_op jit(solution)/shard_map/ppermute | solution.py:35
  108.2 16.7 %all-to-all-start.3 = ((bf16[8,64,256]{2,1,0:T(8,128)(2,1)}), bf16[8,64,256]{2,1,0:T(8,128)(2,1)S(1)}, u32[]{:S(2)}, u32[]{:S(2)}) async-start(bf16[8,64,256]{2,1,0:T(8,128)(2,1)} %bitcast.86), calls=%async_computation.3 | async-start | bytes 524288 | tf_op jit(solution)/shard_map/all_to_all | solution.py:329
  113.4 21.1 %copy-start.20 = (f32[1,384]{1,0:T(1,128)}, f32[1,384]{1,0:T(1,128)S(1)}, u32[]{:S(2)}) copy-start(f32[1,384]{1,0:T(1,128)S(1)} %slice.99.bias_ref) | copy-start | bytes 4612
  124.9 5.3 %copy-start.4 = (bf16[8,64,256]{2,1,0:T(8,128)(2,1)}, bf16[8,64,256]{2,1,0:T(8,128)(2,1)S(1)}, u32[]{:S(2)}) copy-start(bf16[8,64,256]{2,1,0:T(8,128)(2,1)S(1)} %all-to-all-done.3) | copy-start | bytes 786436
  124.9 1.0 copy-start.16
  125.9 0.8 copy-start.18
  130.1 11.8 %all-to-all-start.4 = ((bf16[16,64,128]{2,1,0:T(8,128)(2,1)}), bf16[16,64,128]{2,1,0:T(8,128)(2,1)S(1)}, u32[]{:S(2)}, u32[]{:S(2)}) async-start(bf16[16,64,128]{2,1,0:T(8,128)(2,1)} %copy-done.6), calls=%async_computation.4 | async-start | bytes 524288 | tf_op jit(solution)/shard_map/all_to_all | solution.py:342
  134.5 7.5 %copy-start.35 = (f32[32,128]{1,0:T(8,128)}, f32[32,128]{1,0:T(8,128)S(1)}, u32[]{:S(2)}) copy-start(f32[32,128]{1,0:T(8,128)S(1)} %get-tuple-element.44.start_ref) | copy-start | bytes 49156
  142.0 4.6 %copy-start = (bf16[3072,2048]{1,0:T(8,128)(2,1)S(1)}, bf16[3072,2048]{1,0:T(8,128)(2,1)}, u32[]{:S(2)}) copy-start(bf16[3072,2048]{1,0:T(8,128)(2,1)} %all-gather.2.cloned.1.call-done.w_out_ref) | copy-start | bytes 37748740
  146.6 0.8 copy-start.9
  147.3 0.7 copy-start.10
  148.0 0.7 copy-start.12
  148.7 0.7 copy-start.14
  155.3 11.1 %copy-start.3 = (f32[8,32,128]{2,1,0:T(8,128)}, f32[8,32,128]{2,1,0:T(8,128)S(1)}, u32[]{:S(2)}) copy-start(f32[8,32,128]{2,1,0:T(8,128)S(1)} %output_stage.2.mine_ref) | copy-start | bytes 393220
  178.4 1.0 copy-start.5
  179.3 0.9 copy-start.17
  180.2 0.8 copy-start.19
  185.9 11.0 %all-to-all-start.7 = ((bf16[16,64,128]{2,1,0:T(8,128)(2,1)}), bf16[16,64,128]{2,1,0:T(8,128)(2,1)S(1)}, u32[]{:S(2)}, u32[]{:S(2)}) async-start(bf16[16,64,128]{2,1,0:T(8,128)(2,1)} %copy-done.7), calls=%async_computation.7 | async-start | bytes 524288 | tf_op jit(solution)/shard_map/all_to_all | solution.py:342
  196.9 4.6 %copy-start.1 = (bf16[3072,2048]{1,0:T(8,128)(2,1)S(1)}, bf16[3072,2048]{1,0:T(8,128)(2,1)}, u32[]{:S(2)}) copy-start(bf16[3072,2048]{1,0:T(8,128)(2,1)} %all-gather.2.cloned.1.call-done.w_out_ref) | copy-start | bytes 37748740
  201.5 0.8 copy-start.8
  202.2 0.7 copy-start.11
  202.9 0.7 copy-start.13
  203.7 0.7 copy-start.15
  210.3 11.0 %copy-start.2 = (f32[8,32,128]{2,1,0:T(8,128)}, f32[8,32,128]{2,1,0:T(8,128)S(1)}, u32[]{:S(2)}) copy-start(f32[8,32,128]{2,1,0:T(8,128)S(1)} %output_stage.3.mine_ref) | copy-start | bytes 393220
  223.6 6.7 %collective-permute-start.4 = (f32[1,16,128]{2,1,0:T(8,128)S(1)}, f32[1,16,128]{2,1,0:T(8,128)S(1)}, u32[]{:S(2)}, u32[]{:S(2)}) collective-permute-start(f32[1,16,128]{2,1,0:T(8,128)S(1)} %dynamic-slice_bitcast_fusion), channel_id=1, source_target_pairs={{0,1},{1,0},{2,3},{3,2},{4,5},{5,4},{6,7},{7,6},{8,9},{9,8},{10,11... | collective-permute-start | bytes 24584 | tf_op jit(solution)/shard_map/ppermute | solution.py:35
  (5 other events, 3.4 us)
Sparse Core Ops, SparseCore 0:
  10.1 81.4 all-gather.1

commit v3 on v2

v3 whole, which is shorter than its diff:
```python
import math

import jax
import jax.numpy as jnp
from jax import lax
from jax.experimental import pallas as pl
from jax.experimental.pallas import tpu as pltpu
from jax.sharding import Mesh
from jax.sharding import PartitionSpec as P

ITERS = 2
CHIPS = ("y", "x")
SEQ = ("y", "x", "core")
F32, BF16 = jnp.float32, jnp.bfloat16
NT = (((1,), (1,)), ((), ()))
MIB = 1 << 20
LANES = 128
FREE = pl.CostEstimate(flops=0, bytes_accessed=0, transcendentals=0)


def layer_norm(values):
    centre = values - jnp.mean(values, axis=-1, keepdims=True)
    spread = jnp.mean(centre * centre, axis=-1, keepdims=True)
    return centre * lax.rsqrt(spread + 1e-06)


def rms_scale(values, gains):
    return values * lax.rsqrt(jnp.mean(values * values, axis=-1, keepdims=True) + 1e-06) * gains


def swap_cores(values):
    return lax.ppermute(values, "core", [(0, 1), (1, 0)])


def own_half(values, core):
    kept = lax.dynamic_index_in_dim(values, core, 0, keepdims=False)
    came = swap_cores(lax.dynamic_index_in_dim(values, 1 - core, 0, keepdims=False))
    return jnp.where(core == 0, kept, came), jnp.where(core == 0, came, kept)


def shift_steps(values, by, steps):
    if by % steps == 0:
        return values
    return lax.ppermute(values, "step", [(i, (i + by) % steps) for i in range(steps)])


def fold_kernel(
    place_ref, shifts_ref, w_lat_ref, columns_ref, keep_ref, send_ref, gram_ref
):
    seq, core = place_ref[0], place_ref[1]
    chans, width = w_lat_ref.shape
    heads = keep_ref.shape[0]
    part, hd = columns_ref.shape[1:]
    half = chans // 2
    w_lat = w_lat_ref[...].astype(F32)
    mean = jnp.mean(w_lat, axis=1, keepdims=True)
    centred = w_lat - mean
    gram_ref[...] = (
        lax.dot_general(
            centred, centred, NT, precision=lax.Precision.HIGHEST, preferred_element_type=F32
        )
        / width
    )
    span = 2 * LANES
    first = seq * part
    base = jnp.minimum(first // LANES, (width - span) // LANES) * LANES
    window = pl.ds(pl.multiple_of(base, LANES), span)
    w_window = w_lat_ref[:, window].astype(F32) - mean
    left = jnp.concatenate(
        [
            w_window * (1.0 + shifts_ref[1:2, window]),
            shifts_ref[0:1, window],
            jnp.zeros((7, span), F32),
        ],
        axis=0,
    )
    left = pltpu.roll(left, lax.rem(span - (first - base), span), 1)[:, :part]
    count = left.shape[0]
    high = left.astype(BF16)
    low = (left - high.astype(F32)).astype(BF16)
    stacked = jnp.concatenate([high, low], axis=0)
    for head in range(heads):
        biases = []
        for kind in range(3):
            both = jnp.dot(
                stacked, columns_ref[kind * heads + head], preferred_element_type=F32
            )
            both = both[:count] + both[count:]
            rows = slice(kind * half, (kind + 1) * half)
            top, bottom = both[:half], both[half:chans]
            keep_ref[head, rows] = jnp.where(core == 0, top, bottom)
            send_ref[head, rows] = jnp.where(core == 0, bottom, top)
            biases.append(both[chans : chans + 1])
        biases = jnp.concatenate(biases + [jnp.zeros((5, hd), F32)], axis=0)
        keep_ref[head, 3 * half :] = jnp.where(core == 0, biases, 0.0)
        send_ref[head, 3 * half :] = jnp.where(core == 0, 0.0, biases)


def fold(place, shifts, w_latent, columns, heads):
    chans = w_latent.shape[0]
    hd = columns.shape[2]
    sent = jax.ShapeDtypeStruct((heads, 3 * chans // 2 + 8, hd), F32)
    return pl.pallas_call(
        fold_kernel,
        in_specs=[pl.BlockSpec(memory_space=pltpu.SMEM)]
        + [pl.BlockSpec(memory_space=pltpu.VMEM)] * 3,
        out_shape=(sent, sent, jax.ShapeDtypeStruct((chans, chans), F32)),
        compiler_params=pltpu.CompilerParams(vmem_limit_bytes=40 * MIB),
        cost_estimate=FREE,
        name="fold",
    )(place, shifts, w_latent, columns)


def sum_kernel(parts_ref, out_ref):
    total = parts_ref[0]
    for part in range(1, parts_ref.shape[0]):
        total += parts_ref[part]
    out_ref[...] = total


def sum_parts(parts):
    return pl.pallas_call(
        sum_kernel,
        out_shape=jax.ShapeDtypeStruct(parts.shape[1:], F32),
        cost_estimate=FREE,
        name="sum_parts",
    )(parts)


def text_kernel(
    place_ref, mine_ref, other_ref, mods_ref, gains_ref, out_ref, rows_ref, in_ref
):
    core = place_ref[1]
    sources = mine_ref.shape[0]
    steps, _, width = mods_ref.shape
    hd = gains_ref.shape[1]
    part = width // sources
    chunks = width // hd
    tokens = out_ref.shape[1]
    per = tokens // sources
    rows_ref[...] = mine_ref[:, part : part + per * chunks].astype(F32)
    for chunk in range(chunks):
        cut = slice(chunk * hd, (chunk + 1) * hd)
        text = jnp.concatenate(
            [rows_ref[:, row * chunks + chunk, :] for row in range(per)], axis=0
        )
        for step in range(steps):
            scale = 1.0 + mods_ref[step, 1:2, cut]
            in_ref[step * tokens : (step + 1) * tokens, cut] = (
                text * scale + mods_ref[step, 0:1, cut]
            ).astype(BF16)
    text_in = in_ref[...]
    mine = jnp.dot(
        text_in, mine_ref[:, :part].reshape(width, hd), preferred_element_type=F32
    )
    other = jnp.dot(
        text_in, other_ref[:, :part].reshape(width, hd), preferred_element_type=F32
    )
    keys = rms_scale(jnp.where(core == 0, mine, other), gains_ref[2:3]).astype(BF16)
    values = jnp.where(core == 0, other, mine).astype(BF16)
    out_ref[:, :, :hd] = keys.reshape(steps, tokens, hd)
    out_ref[:, :, hd:] = values.reshape(steps, tokens, hd)


def text_pairs_of(place, mine, other, mods, gains, tokens):
    steps, _, width = mods.shape
    sources, _, hd = mine.shape
    return pl.pallas_call(
        text_kernel,
        in_specs=[pl.BlockSpec(memory_space=pltpu.SMEM)]
        + [pl.BlockSpec(memory_space=pltpu.VMEM)] * 4,
        out_shape=jax.ShapeDtypeStruct((steps, tokens, 2 * hd), BF16),
        scratch_shapes=[
            pltpu.VMEM((sources, tokens // sources * (width // hd), hd), F32),
            pltpu.VMEM((steps * tokens, width), BF16),
        ],
        compiler_params=pltpu.CompilerParams(vmem_limit_bytes=40 * MIB),
        cost_estimate=FREE,
        name="text_pairs",
    )(place, mine, other, mods, gains)


def attention_kernel(
    place_ref, x_ref, mine_ref, theirs_ref, gram_ref, gains_ref, text_ref, out_ref,
    q_ref, k_ref, v_ref
):
    core = place_ref[1]
    hd = gains_ref.shape[1]
    chans = gram_ref.shape[0]
    half_chans = chans // 2
    pairs = x_ref.shape[0]
    text = text_ref.shape[0]
    chips, block, _ = out_ref.shape
    factor = math.log2(math.e) / math.sqrt(hd)
    x = x_ref[...]
    doubled = jnp.concatenate([x, x], axis=1)
    first = jnp.where(core == 0, mine_ref[...], theirs_ref[...])
    second = jnp.where(core == 0, theirs_ref[...], mine_ref[...])
    folded = []
    for kind in range(3):
        rows = slice(kind * half_chans, (kind + 1) * half_chans)
        folded.append(jnp.concatenate([first[rows], second[rows]], axis=0))
    bias = [first[3 * half_chans + kind : 3 * half_chans + kind + 1] for kind in range(3)]
    blank = jnp.zeros((chans, 4 * hd), BF16)
    k_ref[:text] = text_ref[:, :hd]
    v_ref[:text, :hd] = text_ref[:, hd:]
    v_ref[:, hd:] = jnp.ones((v_ref.shape[0], hd), BF16)
    none = jnp.zeros((chans, chans), F32)
    for parity in range(2):
        grams = [gram_ref[...], none] if parity == 0 else [none, gram_ref[...]]
        weights = jnp.concatenate(folded + grams, axis=1)
        high = weights.astype(BF16)
        low = (weights - high.astype(F32)).astype(BF16)
        rows = [high, blank, low, blank] if parity == 0 else [blank, high, blank, low]
        projected = jnp.dot(
            doubled, jnp.concatenate(rows, axis=0), preferred_element_type=F32
        )
        spread = jnp.sum(projected[:, 3 * hd :] * x.astype(F32), axis=1, keepdims=True)
        scale = lax.rsqrt(spread + 1e-06)
        mine = pl.ds(parity * pairs, pairs)
        image = pl.ds(text + parity * pairs, pairs)
        queries = projected[:, :hd] * scale + bias[0]
        image_keys = projected[:, hd : 2 * hd] * scale + bias[1]
        q_ref[mine] = rms_scale(queries, gains_ref[0:1]).astype(BF16)
        k_ref[image] = rms_scale(image_keys, gains_ref[1:2]).astype(BF16)
        v_ref[image, :hd] = (projected[:, 2 * hd : 3 * hd] * scale + bias[2]).astype(BF16)
    half = block // 2
    size = 256
    for start in range(0, 2 * pairs, size):
        scores = lax.dot_general(
            q_ref[start : start + size], k_ref[...], NT, preferred_element_type=F32
        )
        powers = jnp.exp2(scores * factor).astype(BF16)
        both = jnp.dot(powers, v_ref[...], preferred_element_type=F32)
        attended = (both[:, :hd] / both[:, hd:]).astype(BF16)
        parity, begin = divmod(start, pairs)
        out_ref[begin // half : (begin + size) // half, parity * half : (parity + 1) * half] = (
            attended.reshape(size // half, half, hd)
        )


def attention(place, latents, mine, theirs, gram, gains, text_pairs, chips):
    pairs = latents.shape[0]
    text, hd = text_pairs.shape[0], gains.shape[1]
    keys = text + 2 * pairs
    return pl.pallas_call(
        attention_kernel,
        in_specs=[pl.BlockSpec(memory_space=pltpu.SMEM)]
        + [pl.BlockSpec(memory_space=pltpu.VMEM)] * 6,
        out_shape=jax.ShapeDtypeStruct((chips, 2 * pairs // chips, hd), BF16),
        scratch_shapes=[
            pltpu.VMEM((2 * pairs, hd), BF16),
            pltpu.VMEM((keys, hd), BF16),
            pltpu.VMEM((keys, 2 * hd), BF16),
        ],
        compiler_params=pltpu.CompilerParams(vmem_limit_bytes=60 * MIB),
        cost_estimate=pl.CostEstimate(
            flops=8 * pairs * keys * hd, bytes_accessed=2 * MIB, transcendentals=2 * pairs * keys
        ),
        name="attention",
    )(place, latents, mine, theirs, gram, gains, text_pairs)


def output_kernel(
    attended_ref, w_out_ref, x_ref, w_lat_ref, shifts_ref, w_fin_ref, step_ref, added_ref,
    out_ref, rows_ref, w_ref, mixed_ref, sems
):
    heads, tokens, hd = attended_ref.shape
    chunks = sems.shape[0]
    chans, width = w_lat_ref.shape
    size = width // chunks
    half = tokens // 2
    copies = [
        pltpu.make_async_copy(
            w_out_ref.at[pl.ds(c * size, size)], w_ref.at[pl.ds(c * size, size)], sems.at[c]
        )
        for c in range(chunks)
    ]
    for copy in copies:
        copy.start()
    for head in range(heads):
        rows_ref[:, head * hd : (head + 1) * hd] = attended_ref[head]
    x = x_ref[...].astype(F32)
    x = jnp.concatenate([x[:, :chans], x[:, chans:]], axis=0).astype(BF16)
    total = jnp.zeros((tokens, 1), F32)
    for c in range(chunks):
        cut = slice(c * size, (c + 1) * size)
        copies[c].wait()
        mixed = lax.dot_general(rows_ref[...], w_ref[cut], NT, preferred_element_type=F32)
        hidden = jnp.dot(x, w_lat_ref[:, cut], preferred_element_type=F32)
        combined = hidden + shifts_ref[2:3, cut] * mixed
        mixed_ref[c] = combined
        total += jnp.sum(combined, axis=1, keepdims=True)
    mean = total / width
    total = jnp.zeros((tokens, 1), F32)
    for c in range(chunks):
        centre = mixed_ref[c] - mean
        total += jnp.sum(centre * centre, axis=1, keepdims=True)
    scale = lax.rsqrt(total / width + 1e-06)
    drift = jnp.zeros((tokens, chans), F32)
    for c in range(chunks):
        cut = slice(c * size, (c + 1) * size)
        normal = (mixed_ref[c] - mean) * scale
        final_in = (normal * (1.0 + shifts_ref[6:7, cut]) + shifts_ref[5:6, cut]).astype(BF16)
        drift += lax.dot_general(final_in, w_fin_ref[:, cut], NT, preferred_element_type=F32)
    drift = jnp.concatenate([drift[:half], drift[half:]], axis=1)
    contrib = step_ref[0] * drift + added_ref[...]
    out_ref[...] = jnp.broadcast_to(contrib[None], out_ref.shape)


def output_stage(attended, w_out, x, w_lat, shifts, w_fin, step_size, added, steps):
    heads, tokens, hd = attended.shape
    width = w_out.shape[0]
    chunks = 6
    vmem = pl.BlockSpec(memory_space=pltpu.VMEM)
    return pl.pallas_call(
        output_kernel,
        in_specs=[
            vmem,
            pl.BlockSpec(memory_space=pl.ANY),
            vmem,
            vmem,
            vmem,
            vmem,
            pl.BlockSpec(memory_space=pltpu.SMEM),
            vmem,
        ],
        out_shape=jax.ShapeDtypeStruct((steps,) + added.shape, F32),
        scratch_shapes=[
            pltpu.VMEM((tokens, heads * hd), BF16),
            pltpu.VMEM((width, heads * hd), BF16),
            pltpu.VMEM((chunks, tokens, width // chunks), F32),
            pltpu.SemaphoreType.DMA((chunks,)),
        ],
        compiler_params=pltpu.CompilerParams(vmem_limit_bytes=60 * MIB),
        cost_estimate=pl.CostEstimate(
            flops=2 * tokens * width * heads * hd,
            bytes_accessed=2 * width * heads * hd,
            transcendentals=tokens,
        ),
        name="output_stage",
    )(attended, w_out, x, w_lat, shifts, w_fin, step_size, added)


def scan_kernel(place_ref, everyone_ref, mine_ref, start_ref, out_ref, x_ref):
    place = place_ref[0]
    prefix = jnp.zeros(start_ref.shape, F32)
    for step in range(everyone_ref.shape[0]):
        prefix += jnp.where(step < place, everyone_ref[step], 0.0)
    out_ref[...] = prefix + mine_ref[0]
    current = jnp.where(place == 0, start_ref[...], prefix).astype(BF16)
    x_ref[...] = jnp.broadcast_to(current[None], x_ref.shape)


def scan(place, everyone, mine, start, chips):
    return pl.pallas_call(
        scan_kernel,
        in_specs=[pl.BlockSpec(memory_space=pltpu.SMEM)]
        + [pl.BlockSpec(memory_space=pltpu.VMEM)] * 3,
        out_shape=(
            jax.ShapeDtypeStruct(start.shape, F32),
            jax.ShapeDtypeStruct((chips,) + start.shape, BF16),
        ),
        name="scan",
    )(place, everyone, mine, start)


def local(
    trajectory,
    noise,
    step_sizes,
    modulation,
    text_states,
    w_latent,
    w_image_qkv,
    w_text_kv,
    w_out_t,
    qk_gains,
    w_final,
):
    steps = lax.axis_size("step")
    chips = lax.axis_size(CHIPS)
    place, core = lax.axis_index("step"), lax.axis_index("core")
    seq = lax.axis_index(SEQ)
    images, rows, chans = trajectory.shape[1:]
    width = w_latent.shape[1]
    part, heads, hd = w_out_t.shape
    text_rows = text_states.shape[1] // steps
    shifts = modulation[0]

    w_out_mine = w_out_t.reshape(part, heads * hd)
    w_out_mine, text_states, w_text_kv, trajectory, w_image_qkv = lax.optimization_barrier(
        (w_out_mine, text_states, w_text_kv, trajectory, w_image_qkv)
    )
    w_out = lax.all_gather(w_out_mine, SEQ, tiled=True)

    mods = shifts[None, 3:5]
    while mods.shape[0] < steps:
        mods = jnp.concatenate([mods, shift_steps(mods, mods.shape[0], steps)], axis=0)

    text_mine = lax.dynamic_slice_in_dim(text_states, place * text_rows, text_rows, 1)
    text_norm = layer_norm(text_mine.astype(F32)).astype(BF16)
    text_block = jnp.broadcast_to(
        text_norm.reshape(1, images, text_rows * width // hd, hd),
        (chips, images, text_rows * width // hd, hd),
    ).reshape(chips * images, -1, hd)
    weight_block = jnp.transpose(w_text_kv, (2, 1, 0, 3)).reshape(2 * heads, part, hd)
    start_pairs = trajectory[0].reshape(images, rows // 2, 2 * chans)
    latent_block = jnp.broadcast_to(
        start_pairs.astype(BF16)[None], (chips, images, rows // 2, 2 * chans)
    ).reshape(chips * images, rows // 2, 2 * chans)
    packed = jnp.concatenate([weight_block, text_block, latent_block], axis=1)
    columns = jnp.swapaxes(w_image_qkv.reshape(part, 3 * heads, hd), 0, 1)
    packed, w_latent, shifts, columns = lax.optimization_barrier(
        (packed, w_latent, shifts, columns)
    )
    packed = lax.all_to_all(packed, SEQ, 0, 0, tiled=True)

    where = jnp.stack([seq, core]).astype(jnp.int32)
    keep, send, gram = fold(where, shifts, w_latent, columns, heads)
    mine = keep + swap_cores(send)

    mine, packed, mods = lax.optimization_barrier((mine, packed, mods))
    mine = lax.all_to_all(mine, CHIPS, 0, 0, tiled=True)

    text_pairs = text_pairs_of(
        where, packed, swap_cores(packed), mods, qk_gains, text_rows * lax.axis_size(SEQ)
    )
    latents = packed[:, part + text_rows * width // hd :].reshape(-1, 2 * chans)

    text_pairs = jnp.concatenate(
        [shift_steps(text_pairs[k], -k, steps) for k in range(steps)], axis=0
    )
    mine, text_pairs, noise, start_pairs, w_final = lax.optimization_barrier(
        (mine, text_pairs, noise, start_pairs, w_final)
    )
    mine = sum_parts(mine)
    theirs = swap_cores(mine)

    noise_pairs = noise[0].reshape(images, rows // 2, 2 * chans)
    own = jnp.concatenate(
        own_half(jnp.stack([noise_pairs, start_pairs], axis=1), core), axis=1
    )
    own_noise, own_start = own[0], own[1]
    added = own_noise + jnp.where(place == 0, own_start, jnp.zeros_like(own_start))
    w_fin = jnp.swapaxes(w_final, 0, 1)

    place_ref = place.reshape(1).astype(jnp.int32)
    x_own = own_start.astype(BF16)
    result = own_start
    for iteration in range(ITERS):
        attended = attention(where, latents, mine, theirs, gram, qk_gains, text_pairs, chips)
        attended = lax.all_to_all(attended, CHIPS, 0, 0, tiled=True)
        contrib = output_stage(
            attended, w_out, x_own, w_latent, shifts, w_fin, step_sizes, added, steps
        )
        everyone = lax.all_to_all(contrib, "step", 0, 0, tiled=True)
        result, latents = scan(place_ref, everyone, contrib, own_start, chips)
        if iteration + 1 < ITERS:
            x_own = latents[0]
            latents = lax.all_to_all(latents, CHIPS, 0, 0, tiled=True).reshape(-1, 2 * chans)
    first, second = own_half(
        jnp.swapaxes(result.reshape(1, 2, rows // 2, 2 * chans), 0, 1), core
    )
    return jnp.concatenate([first, second], axis=0).reshape(1, images, rows, chans)


def solution(mesh):
    steps = mesh.devices.shape[0]
    fine = Mesh(mesh.devices.reshape(steps, 4, 4, 2), ("step", "y", "x", "core"))
    placed = (
        P("step", None, SEQ, None),
        P("step", None, SEQ, None),
        P("step"),
        P("step", None, None),
        P(None, SEQ, None),
        P(),
        P(SEQ, None, None, None),
        P(SEQ, None, None, None),
        P(SEQ, None, None),
        P(),
        P(),
    )
    return jax.shard_map(
        local,
        mesh=fine,
        in_specs=placed,
        out_specs=P("step", None, SEQ, None),
        check_vma=False,
    )
```

time: 241 us -> 195 us (0.81)
  local copies, waits for them, and re-layouts: 42.6 us -> 9.11 us
  waiting for transfers between devices: 56.7 us -> 31.9 us
  Pallas kernels: 20.5 us -> 38.2 us
  other arithmetic: 20.5 us -> 7.42 us
  starting transfers between devices: 44.3 us -> 56.5 us
  matrix products: 6.86 us -> 0 us
  blocking collectives: 32.4 us -> 36.5 us
    unnamed x86 -> x38, local copies, waits for them, and re-layouts: 27.1 us -> 4.06 us
    ppermute x0 -> x10, starting transfers between devices: none -> 21.1 us  [shift_steps(): lax.ppermute(values, 'step', [(i, (i + by) % steps) for i in range(steps)])]
    all_to_all x1, waiting for transfers between devices: 22.2 us -> 1.91 us  [local(): packed = lax.all_to_all(packed, SEQ, 0, 0, tiled=True)]
    pallas_call x4 -> x7, Pallas kernels: 17.2 us -> 34.9 us  [the longest x2 18.8 us: output_stage(): pl.pallas_call(output_kernel, in_specs=[vmem, pl.BlockSpec(memory_space=p...]
    ppermute x0 -> x10, waiting for transfers between devices: none -> 15 us  [shift_steps(): lax.ppermute(values, 'step', [(i, (i + by) % steps) for i in range(steps)])]
    all_to_all x2 -> x0, starting transfers between devices: 13.3 us -> none  [the longest x1 9.03 us: local(): mods = lax.all_to_all(mods_mine, 'step', 0, 0, tiled=True)]
    all_to_all x2 -> x0, waiting for transfers between devices: 12.1 us -> none  [the longest x1 9.99 us: local(): lax.all_to_all(text_pairs, 'step', 0, 0, tiled=True).reshape(-1, 2 * hd)]
    all_to_all x1, waiting for transfers between devices: 8.58 us -> 0.01 us  [local(): mine = lax.all_to_all(mine, CHIPS, 0, 0, tiled=True)]
  transfers between devices with their start and end apart: 12 -> 20, of which waited for: 7 -> 11; matrix products, arithmetic and copies ran while one was open for 17% -> 5% of each run, Pallas kernels for 1% -> 6%
where the time goes in v3:
time: 195 us; the launch traced here: 194 us
  starting transfers between devices  56.5 us (29%)
  Pallas kernels  38.2 us (20%)
  blocking collectives  36.5 us (19%)
  waiting for transfers between devices  31.9 us (16%)
  between operations  14.4 us (7%)
  local copies, waits for them, and re-layouts  9.11 us (5%)
  other arithmetic  7.42 us (4%)
    all_to_all x2, blocking collectives, local(): everyone = lax.all_to_all(contrib, 'step', 0, 0, tiled=True)  25.5 us
    ppermute x10, starting transfers between devices, shift_steps(): lax.ppermute(values, 'step', [(i, (i + by) % steps) for i in range(steps)])  21.1 us
    pallas_call x2, Pallas kernels, output_stage(): pl.pallas_call(output_kernel, in_specs=[vmem, pl.BlockSpec(memory_space=p...  18.8 us
    ppermute x10, waiting for transfers between devices, shift_steps(): lax.ppermute(values, 'step', [(i, (i + by) % steps) for i in range(steps)])  15 us
    all_to_all x2, waiting for transfers between devices, local(): attended = lax.all_to_all(attended, CHIPS, 0, 0, tiled=True)  13.1 us
    all_to_all x1, blocking collectives, local(): lax.all_to_all(latents, CHIPS, 0, 0, tiled=True).reshape(-1, 2 * chans)  11 us
    ppermute x5, starting transfers between devices, swap_cores(): return lax.ppermute(values, 'core', [(0, 1), (1, 0)])  11 us
    all_to_all x2, starting transfers between devices, local(): attended = lax.all_to_all(attended, CHIPS, 0, 0, tiled=True)  9.71 us
  transfers between devices with their start and end apart: 20, of which 11 were waited for; matrix products, arithmetic and copies ran while one was open for 5% of the time, Pallas kernels for 6%

profile of v3, /device:TPU:1, one launch (start us, length us, event | category | flops | bytes accessed | tf_op | source)
XLA Modules:
  0.0 193.9 jit_solution(5487985389480112935)
XLA Ops:
  6.5 1.9 copy.21
  8.5 0.9 reshape_squeeze.3
  9.4 1.0 convert_reduce_fusion
  10.5 1.1 fusion.2
  11.5 1.0 fusion.3
  13.3 1.1 pad_maximum_fusion
  14.5 8.7 %all-to-all-start = ((bf16[32,160,128]{2,1,0:T(8,128)(2,1)}), bf16[32,160,128]{2,1,0:T(8,128)(2,1)S(1)}, u32[]{:S(2)}, u32[]{:S(2)}) async-start(bf16[32,160,128]{2,1,0:T(8,128)(2,1)} %pad_maximum_fusion), calls=%async_computation | async-start | bytes 2621440 | tf_op jit(solution)/shard_map/all_to_all | solution.py:417
  23.2 1.7 collective-permute-start.1
  25.0 2.4 %fold.1 = (f32[16,104,128]{2,1,0:T(8,128)S(1)}, f32[16,104,128]{2,1,0:T(8,128)S(1)}, f32[64,64]{1,0:T(8,128)S(1)}) custom-call(s32[2]{0:T(128)S(1)} %pad_add_fusion.place_ref, f32[7,3072]{1,0:T(8,128)S(1)} %bitcast.68, bf16[64,3072]{1,0:T(8,128)(2,1)S(1)} %copy-done, bf16[48,96,128]{2,1,0:T(8,128)(2,1)S(1)} %bitcast.67), custom_call_target="tpu_custom_call" | custom-call | tf_op jit(solution)/shard_map/fold/pallas_call | solution.py:103
  28.1 2.3 %collective-permute-done.1 = f32[1,2,3072]{2,1,0:T(2,128)S(1)} collective-permute-done((f32[1,2,3072]{2,1,0:T(2,128)S(1)}, f32[1,2,3072]{2,1,0:T(2,128)S(1)}, u32[]{:S(2)}, u32[]{:S(2)}) %collective-permute-start.1) | collective-permute-done | bytes 24608 | tf_op jit(solution)/shard_map/ppermute | solution.py:44
  30.4 0.7 collective-permute-start.2
  31.2 5.2 %collective-permute-done.2 = f32[2,2,3072]{2,1,0:T(2,128)S(1)} collective-permute-done((f32[2,2,3072]{2,1,0:T(2,128)S(1)}, f32[2,2,3072]{2,1,0:T(2,128)S(1)}, u32[]{:S(2)}, u32[]{:S(2)}) %collective-permute-start.2) | collective-permute-done | bytes 49184 | tf_op jit(solution)/shard_map/ppermute | solution.py:44
  36.4 4.5 %collective-permute-start.3 = (f32[4,2,3072]{2,1,0:T(2,128)S(1)}, f32[4,2,3072]{2,1,0:T(2,128)S(1)}, u32[]{:S(2)}, u32[]{:S(2)}) collective-permute-start(f32[4,2,3072]{2,1,0:T(2,128)S(1)} %pad_maximum_fusion.2), channel_id=1, source_target_pairs={{0,128},{32,160},{64,192},{96,224},{128,0},{160,32},{192,64},{224,... | collective-permute-start | bytes 294920 | tf_op jit(solution)/shard_map/ppermute | solution.py:44
  40.9 4.1 %collective-permute-done.3 = f32[4,2,3072]{2,1,0:T(2,128)S(1)} collective-permute-done((f32[4,2,3072]{2,1,0:T(2,128)S(1)}, f32[4,2,3072]{2,1,0:T(2,128)S(1)}, u32[]{:S(2)}, u32[]{:S(2)}) %collective-permute-start.3) | collective-permute-done | bytes 98336 | tf_op jit(solution)/shard_map/ppermute | solution.py:44
  45.1 1.0 add.38
  46.1 1.9 all-to-all-done.mine_ref
  48.0 1.5 collective-permute-start.4
  50.8 6.0 %all-to-all-start.1 = ((f32[16,104,128]{2,1,0:T(8,128)}), f32[16,104,128]{2,1,0:T(8,128)}, u32[]{:S(2)}, u32[]{:S(2)}) async-start(f32[16,104,128]{2,1,0:T(8,128)} %add.38), calls=%async_computation.1 | async-start | bytes 1703936 | tf_op jit(solution)/shard_map/all_to_all | solution.py:424
  56.8 2.5 %text_pairs.1 = bf16[8,64,256]{2,1,0:T(8,128)(2,1)S(1)} custom-call(s32[2]{0:T(128)S(1)} %pad_add_fusion.place_ref, bf16[32,160,128]{2,1,0:T(8,128)(2,1)S(1)} %all-to-all-done.mine_ref, bf16[32,160,128]{2,1,0:T(8,128)(2,1)S(1)} %collective-permute-done.4.other_ref, f32[8,2,3072]{2,1,0:T(2,128)S(1)} %pad_maximum_fusion.1.mods_ref, f32[3,128]{1,0:T(4,128)S(1)} %copy-done.3), custom_call_target="tpu_custom_call" | custom-call | tf_op jit(solution)/shard_map/text_pairs/pallas_call | solution.py:168
  59.4 4.5 %collective-permute-start.5 = (bf16[64,256]{1,0:T(8,128)(2,1)S(1)}, bf16[64,256]{1,0:T(8,128)(2,1)S(1)}, u32[]{:S(2)}, u32[]{:S(2)}) collective-permute-start(bf16[64,256]{1,0:T(8,128)(2,1)S(1)} %get-tuple-element.57), channel_id=1, source_target_pairs={{0,224},{32,0},{64,32},{96,64},{128,96},{160,128},{192,160},{224,1... | collective-permute-start | bytes 98312 | tf_op jit(solution)/shard_map/ppermute | solution.py:44
  63.8 1.3 collective-permute-start.6
  65.5 4.4 %collective-permute-start.8 = (bf16[64,256]{1,0:T(8,128)(2,1)S(1)}, bf16[64,256]{1,0:T(8,128)(2,1)S(1)}, u32[]{:S(2)}, u32[]{:S(2)}) collective-permute-start(bf16[64,256]{1,0:T(8,128)(2,1)S(1)} %get-tuple-element.54), channel_id=1, source_target_pairs={{0,128},{32,160},{64,192},{96,224},{128,0},{160,32},{192,64},{224,... | collective-permute-start | bytes 98312 | tf_op jit(solution)/shard_map/ppermute | solution.py:44
  70.0 2.2 %collective-permute-start.10 = (bf16[64,256]{1,0:T(8,128)(2,1)S(1)}, bf16[64,256]{1,0:T(8,128)(2,1)S(1)}, u32[]{:S(2)}, u32[]{:S(2)}) collective-permute-start(bf16[64,256]{1,0:T(8,128)(2,1)S(1)} %get-tuple-element.52), channel_id=1, source_target_pairs={{0,64},{32,96},{64,128},{96,160},{128,192},{160,224},{192,0},{224,... | collective-permute-start | bytes 98312 | tf_op jit(solution)/shard_map/ppermute | solution.py:44
  72.2 1.4 collective-permute-start.11
  73.6 2.1 %collective-permute-done.9 = bf16[64,256]{1,0:T(8,128)(2,1)S(1)} collective-permute-done((bf16[64,256]{1,0:T(8,128)(2,1)S(1)}, bf16[64,256]{1,0:T(8,128)(2,1)S(1)}, u32[]{:S(2)}, u32[]{:S(2)}) %collective-permute-start.9) | collective-permute-done | bytes 32800 | tf_op jit(solution)/shard_map/ppermute | solution.py:44
  75.7 1.0 collective-permute-done.10
  77.0 1.9 sum_parts.1.mine_ref
  78.9 2.5 %collective-permute-start.12 = (f32[104,128]{1,0:T(8,128)}, f32[104,128]{1,0:T(8,128)S(1)}, u32[]{:S(2)}, u32[]{:S(2)}) collective-permute-start(f32[104,128]{1,0:T(8,128)} %sum_parts.1.mine_ref), channel_id=1, source_target_pairs={{0,1},{1,0},{2,3},{3,2},{4,5},{5,4},{6,7},{7,6},{8,9},{9,8},{10,11... | collective-permute-start | bytes 159752 | tf_op jit(solution)/shard_map/ppermute | solution.py:32
  81.5 1.0 collective-permute-done.12.theirs_ref
  83.1 4.7 %attention.2 = bf16[16,64,128]{2,1,0:T(8,128)(2,1)} custom-call(s32[2]{0:T(128)} %copy-done.2, bf16[512,128]{1,0:T(8,128)(2,1)} %bitcast.83, f32[104,128]{1,0:T(8,128)} %sum_parts.1.mine_ref, f32[104,128]{1,0:T(8,128)} %copy-done.13, f32[64,64]{1,0:T(8,128)} %copy-done.4, f32[3,128]{1,0:T(4,128)} %gains_ref.5, bf16[512,256]{1,0:T(8,128)(2,1)} %copy-done.12), custom_call_target="tpu_custom_call" | custom-call | flops 805306368 | bytes 2097152 | tf_op jit(solution)/shard_map/attention/pallas_call | solution.py:246
  87.9 6.2 %all-to-all-start.2 = ((bf16[16,64,128]{2,1,0:T(8,128)(2,1)}), bf16[16,64,128]{2,1,0:T(8,128)(2,1)S(1)}, u32[]{:S(2)}, u32[]{:S(2)}) async-start(bf16[16,64,128]{2,1,0:T(8,128)(2,1)} %attention.2), calls=%async_computation.2 | async-start | bytes 524288 | tf_op jit(solution)/shard_map/all_to_all | solution.py:453
  95.3 6.9 %all-to-all-done.2.attended_ref = bf16[16,64,128]{2,1,0:T(8,128)(2,1)S(1)} async-done(((bf16[16,64,128]{2,1,0:T(8,128)(2,1)}), bf16[16,64,128]{2,1,0:T(8,128)(2,1)S(1)}, u32[]{:S(2)}, u32[]{:S(2)}) %all-to-all-start.2) | async-done | bytes 262176 | tf_op jit(solution)/shard_map/all_to_all | solution.py:453
  102.2 0.7 copy-done.6
  102.9 9.4 %output_stage.2.mine_ref = f32[8,32,128]{2,1,0:T(8,128)} custom-call(bf16[16,64,128]{2,1,0:T(8,128)(2,1)} %copy-done.6, bf16[3072,2048]{1,0:T(8,128)(2,1)} %all-gather.2.cloned.1.call-done.w_out_ref, bf16[32,128]{1,0:T(8,128)(2,1)} %convert_element_type.19.x_ref, bf16[64,3072]{1,0:T(8,128)(2,1)} %w_lat_ref.2, f32[7,3072]{1,0:T(8,128)} %bitcast.69, ...), custom_call_target="tpu_custom_call" | custom-call | flops 805306368 | bytes 12582912 | tf_op jit(solution)/shard_map/output_stage/pallas_call | solution.py:316
  112.3 13.6 %all_to_all.35.everyone_ref = f32[8,32,128]{2,1,0:T(8,128)} all-to-all(f32[8,32,128]{2,1,0:T(8,128)} %output_stage.2.mine_ref), channel_id=1, replica_groups=mesh['step'=8,'y'=4,'x'=4,'core'=2] {'step'}, dimensions={0} | all-to-all | bytes 262144 | tf_op jit(solution)/shard_map/all_to_all | solution.py:457
  125.8 1.6 scan.2
  127.5 11.0 %all_to_all.36 = bf16[16,32,128]{2,1,0:T(8,128)(2,1)} all-to-all(bf16[16,32,128]{2,1,0:T(8,128)(2,1)} %get-tuple-element.47), channel_id=1, replica_groups=mesh['step'=8,'y'=4,'x'=4,'core'=2] {'y','x'}, dimensions={0} | all-to-all | bytes 262144 | tf_op jit(solution)/shard_map/all_to_all | solution.py:461
  138.5 4.6 %attention.3 = bf16[16,64,128]{2,1,0:T(8,128)(2,1)} custom-call(s32[2]{0:T(128)} %copy-done.2, bf16[512,128]{1,0:T(8,128)(2,1)} %bitcast.84, f32[104,128]{1,0:T(8,128)} %sum_parts.1.mine_ref, f32[104,128]{1,0:T(8,128)} %copy-done.13, f32[64,64]{1,0:T(8,128)} %copy-done.4, f32[3,128]{1,0:T(4,128)} %gains_ref.5, bf16[512,256]{1,0:T(8,128)(2,1)} %copy-done.12), custom_call_target="tpu_custom_call" | custom-call | flops 805306368 | bytes 2097152 | tf_op jit(solution)/shard_map/attention/pallas_call | solution.py:246
  143.1 3.5 %all-to-all-start.5 = ((bf16[16,64,128]{2,1,0:T(8,128)(2,1)}), bf16[16,64,128]{2,1,0:T(8,128)(2,1)S(1)}, u32[]{:S(2)}, u32[]{:S(2)}) async-start(bf16[16,64,128]{2,1,0:T(8,128)(2,1)} %attention.3), calls=%async_computation.5 | async-start | bytes 524288 | tf_op jit(solution)/shard_map/all_to_all | solution.py:453
  146.6 1.3 slice_bitcast_fusion.8.x_ref
  147.9 6.2 %all-to-all-done.5.attended_ref = bf16[16,64,128]{2,1,0:T(8,128)(2,1)S(1)} async-done(((bf16[16,64,128]{2,1,0:T(8,128)(2,1)}), bf16[16,64,128]{2,1,0:T(8,128)(2,1)S(1)}, u32[]{:S(2)}, u32[]{:S(2)}) %all-to-all-start.5) | async-done | bytes 262176 | tf_op jit(solution)/shard_map/all_to_all | solution.py:453
  154.1 0.7 copy-done.7
  154.8 9.4 %output_stage.3.mine_ref = f32[8,32,128]{2,1,0:T(8,128)} custom-call(bf16[16,64,128]{2,1,0:T(8,128)(2,1)} %copy-done.7, bf16[3072,2048]{1,0:T(8,128)(2,1)} %all-gather.2.cloned.1.call-done.w_out_ref, bf16[32,128]{1,0:T(8,128)(2,1)} %slice_bitcast_fusion.8.x_ref, bf16[64,3072]{1,0:T(8,128)(2,1)} %w_lat_ref.2, f32[7,3072]{1,0:T(8,128)} %bitcast.70, ...), custom_call_target="tpu_custom_call" | custom-call | flops 805306368 | bytes 12582912 | tf_op jit(solution)/shard_map/output_stage/pallas_call | solution.py:316
  164.2 11.9 %all_to_all.37.everyone_ref = f32[8,32,128]{2,1,0:T(8,128)} all-to-all(f32[8,32,128]{2,1,0:T(8,128)} %output_stage.3.mine_ref), channel_id=1, replica_groups=mesh['step'=8,'y'=4,'x'=4,'core'=2] {'step'}, dimensions={0} | all-to-all | bytes 262144 | tf_op jit(solution)/shard_map/all_to_all | solution.py:457
  176.1 1.6 scan.3
  178.5 6.4 %collective-permute-start.14 = (f32[1,16,128]{2,1,0:T(8,128)S(1)}, f32[1,16,128]{2,1,0:T(8,128)S(1)}, u32[]{:S(2)}, u32[]{:S(2)}) collective-permute-start(f32[1,16,128]{2,1,0:T(8,128)S(1)} %dynamic-slice_bitcast_fusion), channel_id=1, source_target_pairs={{0,1},{1,0},{2,3},{3,2},{4,5},{5,4},{6,7},{7,6},{8,9},{9,8},{10,11... | collective-permute-start | bytes 24584 | tf_op jit(solution)/shard_map/ppermute | solution.py:32
  184.8 0.8 collective-permute-done.14
  185.7 0.7 bitcast_select_fusion.1
  (76 shorter events, 6.4 us)
Async XLA Ops:
  6.5 6.0 %copy-start.8 = (bf16[96,2,16,128]{3,2,1,0:T(8,128)(2,1)S(1)}, bf16[96,2,16,128]{3,2,1,0:T(8,128)(2,1)}, u32[]{:S(2)}) copy-start(bf16[96,2,16,128]{3,2,1,0:T(8,128)(2,1)} %param.18) | copy-start | bytes 2359300
  6.5 95.6 %all-gather.2.cloned.1.call-start = ((), (), s32[]{:S(2)}) async-start(), calls=%async_computation.7 | async-start | bytes 12976128 | tf_op jit(solution)/shard_map/all_gather | solution.py:395
  6.5 6.3 %copy-start.10 = (f32[1,7,3072]{2,0,1:T(1,128)S(1)}, f32[1,7,3072]{2,0,1:T(1,128)}, u32[]{:S(2)}) copy-start(f32[1,7,3072]{2,0,1:T(1,128)} %param.14) | copy-start | bytes 258052
  8.5 4.5 %copy-start.5 = (bf16[96,3,16,128]{3,2,1,0:T(8,128)(2,1)S(1)}, bf16[96,3,16,128]{3,2,1,0:T(8,128)(2,1)}, u32[]{:S(2)}) copy-start(bf16[96,3,16,128]{3,2,1,0:T(8,128)(2,1)} %param.17) | copy-start | bytes 3538948
  12.9 12.1 %copy-start.1 = (f32[1,7,3072]{2,1,0:T(8,128)}, f32[1,7,3072]{2,1,0:T(8,128)S(1)}, u32[]{:S(2)}) copy-start(f32[1,7,3072]{2,1,0:T(8,128)S(1)} %copy.22) | copy-start | bytes 258052
  14.5 8.7 %slice-start = ((f32[1,7,3072]{2,0,1:T(1,128)}), f32[1,2,3072]{2,0,1:T(1,128)S(1)}, s32[]{:S(2)}) async-start(f32[1,7,3072]{2,0,1:T(1,128)} %param.14), calls=%async_computation.8 | async-start | bytes 49152 | tf_op jit(solution)/shard_map/slice | solution.py:397
  14.5 10.6 %copy-start = (bf16[64,3072]{1,0:T(8,128)(2,1)S(1)}, bf16[64,3072]{1,0:T(8,128)(2,1)}, u32[]{:S(2)}) copy-start(bf16[64,3072]{1,0:T(8,128)(2,1)} %w_lat_ref.2) | copy-start | bytes 1179652
  14.5 33.5 %all-to-all-start = ((bf16[32,160,128]{2,1,0:T(8,128)(2,1)}), bf16[32,160,128]{2,1,0:T(8,128)(2,1)S(1)}, u32[]{:S(2)}, u32[]{:S(2)}) async-start(bf16[32,160,128]{2,1,0:T(8,128)(2,1)} %pad_maximum_fusion), calls=%async_computation | async-start | bytes 2621440 | tf_op jit(solution)/shard_map/all_to_all | solution.py:417
  23.2 7.2 %collective-permute-start.1 = (f32[1,2,3072]{2,1,0:T(2,128)S(1)}, f32[1,2,3072]{2,1,0:T(2,128)S(1)}, u32[]{:S(2)}, u32[]{:S(2)}) collective-permute-start(f32[1,2,3072]{2,1,0:T(2,128)S(1)} %copy.17), channel_id=1, source_target_pairs={{0,32},{32,64},{64,96},{96,128},{128,160},{160,192},{192,224},{224... | collective-permute-start | bytes 73736 | tf_op jit(solution)/shard_map/ppermute | solution.py:44
  25.0 31.7 %copy-start.2 = (s32[2]{0:T(128)}, s32[2]{0:T(128)S(1)}, u32[]{:S(2)}) copy-start(s32[2]{0:T(128)S(1)} %pad_add_fusion.place_ref) | copy-start | bytes 28
  27.5 17.6 %copy-start.4 = (f32[64,64]{1,0:T(8,128)}, f32[64,64]{1,0:T(8,128)S(1)}, u32[]{:S(2)}) copy-start(f32[64,64]{1,0:T(8,128)S(1)} %get-tuple-element.41.gram_ref) | copy-start | bytes 49156
  27.5 17.6 %collective-permute-start = (f32[16,104,128]{2,1,0:T(8,128)S(1)}, f32[16,104,128]{2,1,0:T(8,128)S(1)}, u32[]{:S(2)}, u32[]{:S(2)}) collective-permute-start(f32[16,104,128]{2,1,0:T(8,128)S(1)} %get-tuple-element.35), channel_id=1, source_target_pairs={{0,1},{1,0},{2,3},{3,2},{4,5},{5,4},{6,7},{7,6},{8,9},{9,8},{10,11... | collective-permute-start | bytes 2555912 | tf_op jit(solution)/shard_map/ppermute | solution.py:32
  30.4 5.9 %collective-permute-start.2 = (f32[2,2,3072]{2,1,0:T(2,128)S(1)}, f32[2,2,3072]{2,1,0:T(2,128)S(1)}, u32[]{:S(2)}, u32[]{:S(2)}) collective-permute-start(f32[2,2,3072]{2,1,0:T(2,128)S(1)} %pad_maximum_fusion.3), channel_id=1, source_target_pairs={{0,64},{32,96},{64,128},{96,160},{128,192},{160,224},{192,0},{224,... | collective-permute-start | bytes 147464 | tf_op jit(solution)/shard_map/ppermute | solution.py:44
  36.4 8.5 %collective-permute-start.3 = (f32[4,2,3072]{2,1,0:T(2,128)S(1)}, f32[4,2,3072]{2,1,0:T(2,128)S(1)}, u32[]{:S(2)}, u32[]{:S(2)}) collective-permute-start(f32[4,2,3072]{2,1,0:T(2,128)S(1)} %pad_maximum_fusion.2), channel_id=1, source_target_pairs={{0,128},{32,160},{64,192},{96,224},{128,0},{160,32},{192,64},{224,... | collective-permute-start | bytes 294920 | tf_op jit(solution)/shard_map/ppermute | solution.py:44
  46.1 10.7 %copy-start.3 = (f32[3,128]{1,0:T(4,128)S(1)}, f32[3,128]{1,0:T(4,128)}, u32[]{:S(2)}) copy-start(f32[3,128]{1,0:T(4,128)} %gains_ref.5) | copy-start | bytes 4612
  48.0 8.8 %collective-permute-start.4 = (bf16[32,160,128]{2,1,0:T(8,128)(2,1)S(1)}, bf16[32,160,128]{2,1,0:T(8,128)(2,1)S(1)}, u32[]{:S(2)}, u32[]{:S(2)}) collective-permute-start(bf16[32,160,128]{2,1,0:T(8,128)(2,1)S(1)} %all-to-all-done.mine_ref), channel_id=1, source_target_pairs={{0,1},{1,0},{2,3},{3,2},{4,5},{5,4},{6,7},{7,6},{8,9},{9,8},{10,11... | collective-permute-start | bytes 3932168 | tf_op jit(solution)/shard_map/ppermute | solution.py:32
  50.8 26.2 %all-to-all-start.1 = ((f32[16,104,128]{2,1,0:T(8,128)}), f32[16,104,128]{2,1,0:T(8,128)}, u32[]{:S(2)}, u32[]{:S(2)}) async-start(f32[16,104,128]{2,1,0:T(8,128)} %add.38), calls=%async_computation.1 | async-start | bytes 1703936 | tf_op jit(solution)/shard_map/all_to_all | solution.py:424
  59.3 22.0 %copy-start.11 = (f32[1,2,32,64]{3,2,1,0:T(8,128)S(1)}, f32[1,2,32,64]{3,2,1,0:T(8,128)}, u32[]{:S(2)}) copy-start(f32[1,2,32,64]{3,2,1,0:T(8,128)} %param.12) | copy-start | bytes 49156
  59.4 10.6 %collective-permute-start.5 = (bf16[64,256]{1,0:T(8,128)(2,1)S(1)}, bf16[64,256]{1,0:T(8,128)(2,1)S(1)}, u32[]{:S(2)}, u32[]{:S(2)}) collective-permute-start(bf16[64,256]{1,0:T(8,128)(2,1)S(1)} %get-tuple-element.57), channel_id=1, source_target_pairs={{0,224},{32,0},{64,32},{96,64},{128,96},{160,128},{192,160},{224,1... | collective-permute-start | bytes 98312 | tf_op jit(solution)/shard_map/ppermute | solution.py:44
  63.8 8.4 %collective-permute-start.6 = (bf16[64,256]{1,0:T(8,128)(2,1)S(1)}, bf16[64,256]{1,0:T(8,128)(2,1)S(1)}, u32[]{:S(2)}, u32[]{:S(2)}) collective-permute-start(bf16[64,256]{1,0:T(8,128)(2,1)S(1)} %get-tuple-element.56), channel_id=1, source_target_pairs={{0,192},{32,224},{64,0},{96,32},{128,64},{160,96},{192,128},{224,1... | collective-permute-start | bytes 98312 | tf_op jit(solution)/shard_map/ppermute | solution.py:44
  65.1 8.5 %collective-permute-start.7 = (bf16[64,256]{1,0:T(8,128)(2,1)S(1)}, bf16[64,256]{1,0:T(8,128)(2,1)S(1)}, u32[]{:S(2)}, u32[]{:S(2)}) collective-permute-start(bf16[64,256]{1,0:T(8,128)(2,1)S(1)} %get-tuple-element.55), channel_id=1, source_target_pairs={{0,160},{32,192},{64,224},{96,0},{128,32},{160,64},{192,96},{224,1... | collective-permute-start | bytes 98312 | tf_op jit(solution)/shard_map/ppermute | solution.py:44
  65.5 8.0 %collective-permute-start.8 = (bf16[64,256]{1,0:T(8,128)(2,1)S(1)}, bf16[64,256]{1,0:T(8,128)(2,1)S(1)}, u32[]{:S(2)}, u32[]{:S(2)}) collective-permute-start(bf16[64,256]{1,0:T(8,128)(2,1)S(1)} %get-tuple-element.54), channel_id=1, source_target_pairs={{0,128},{32,160},{64,192},{96,224},{128,0},{160,32},{192,64},{224,... | collective-permute-start | bytes 98312 | tf_op jit(solution)/shard_map/ppermute | solution.py:44
  70.0 5.8 %collective-permute-start.9 = (bf16[64,256]{1,0:T(8,128)(2,1)S(1)}, bf16[64,256]{1,0:T(8,128)(2,1)S(1)}, u32[]{:S(2)}, u32[]{:S(2)}) collective-permute-start(bf16[64,256]{1,0:T(8,128)(2,1)S(1)} %get-tuple-element.53), channel_id=1, source_target_pairs={{0,96},{32,128},{64,160},{96,192},{128,224},{160,0},{192,32},{224,... | collective-permute-start | bytes 98312 | tf_op jit(solution)/shard_map/ppermute | solution.py:44
  70.0 6.7 %collective-permute-start.10 = (bf16[64,256]{1,0:T(8,128)(2,1)S(1)}, bf16[64,256]{1,0:T(8,128)(2,1)S(1)}, u32[]{:S(2)}, u32[]{:S(2)}) collective-permute-start(bf16[64,256]{1,0:T(8,128)(2,1)S(1)} %get-tuple-element.52), channel_id=1, source_target_pairs={{0,64},{32,96},{64,128},{96,160},{128,192},{160,224},{192,0},{224,... | collective-permute-start | bytes 98312 | tf_op jit(solution)/shard_map/ppermute | solution.py:44
  72.2 4.7 %collective-permute-start.11 = (bf16[64,256]{1,0:T(8,128)(2,1)S(1)}, bf16[64,256]{1,0:T(8,128)(2,1)S(1)}, u32[]{:S(2)}, u32[]{:S(2)}) collective-permute-start(bf16[64,256]{1,0:T(8,128)(2,1)S(1)} %get-tuple-element.51), channel_id=1, source_target_pairs={{0,32},{32,64},{64,96},{96,128},{128,160},{160,192},{192,224},{224... | collective-permute-start | bytes 98312 | tf_op jit(solution)/shard_map/ppermute | solution.py:44
  76.9 5.6 %copy-start.12 = (bf16[512,256]{1,0:T(8,128)(2,1)}, bf16[512,256]{1,0:T(8,128)(2,1)S(1)}, u32[]{:S(2)}) copy-start(bf16[512,256]{1,0:T(8,128)(2,1)S(1)} %constant_dynamic-update-slice_fusion.text_ref) | copy-start | bytes 786436
  78.9 3.6 %collective-permute-start.12 = (f32[104,128]{1,0:T(8,128)}, f32[104,128]{1,0:T(8,128)S(1)}, u32[]{:S(2)}, u32[]{:S(2)}) collective-permute-start(f32[104,128]{1,0:T(8,128)} %sum_parts.1.mine_ref), channel_id=1, source_target_pairs={{0,1},{1,0},{2,3},{3,2},{4,5},{5,4},{6,7},{7,6},{8,9},{9,8},{10,11... | collective-permute-start | bytes 159752 | tf_op jit(solution)/shard_map/ppermute | solution.py:32
  81.4 12.6 %collective-permute-start.13 = (f32[2,16,128]{2,1,0:T(8,128)S(1)}, f32[2,16,128]{2,1,0:T(8,128)S(1)}, u32[]{:S(2)}, u32[]{:S(2)}) collective-permute-start(f32[2,16,128]{2,1,0:T(8,128)S(1)} %fusion.8), channel_id=1, source_target_pairs={{0,1},{1,0},{2,3},{3,2},{4,5},{5,4},{6,7},{7,6},{8,9},{9,8},{10,11... | collective-permute-start | bytes 49160 | tf_op jit(solution)/shard_map/ppermute | solution.py:32
  82.5 0.6 copy-start.13
  87.9 14.3 %all-to-all-start.2 = ((bf16[16,64,128]{2,1,0:T(8,128)(2,1)}), bf16[16,64,128]{2,1,0:T(8,128)(2,1)S(1)}, u32[]{:S(2)}, u32[]{:S(2)}) async-start(bf16[16,64,128]{2,1,0:T(8,128)(2,1)} %attention.2), calls=%async_computation.2 | async-start | bytes 524288 | tf_op jit(solution)/shard_map/all_to_all | solution.py:453
  94.7 17.6 %copy-start.9 = (f32[32,128]{1,0:T(8,128)}, f32[32,128]{1,0:T(8,128)S(1)}, u32[]{:S(2)}) copy-start(f32[32,128]{1,0:T(8,128)S(1)} %get-tuple-element.50.start_ref) | copy-start | bytes 49156
  102.2 0.7 copy-start.6
  143.1 11.0 %all-to-all-start.5 = ((bf16[16,64,128]{2,1,0:T(8,128)(2,1)}), bf16[16,64,128]{2,1,0:T(8,128)(2,1)S(1)}, u32[]{:S(2)}, u32[]{:S(2)}) async-start(bf16[16,64,128]{2,1,0:T(8,128)(2,1)} %attention.3), calls=%async_computation.5 | async-start | bytes 524288 | tf_op jit(solution)/shard_map/all_to_all | solution.py:453
  154.1 0.7 copy-start.7
  178.5 7.2 %collective-permute-start.14 = (f32[1,16,128]{2,1,0:T(8,128)S(1)}, f32[1,16,128]{2,1,0:T(8,128)S(1)}, u32[]{:S(2)}, u32[]{:S(2)}) collective-permute-start(f32[1,16,128]{2,1,0:T(8,128)S(1)} %dynamic-slice_bitcast_fusion), channel_id=1, source_target_pairs={{0,1},{1,0},{2,3},{3,2},{4,5},{5,4},{6,7},{7,6},{8,9},{9,8},{10,11... | collective-permute-start | bytes 24584 | tf_op jit(solution)/shard_map/ppermute | solution.py:32
Sparse Core Ops, SparseCore 0:
  9.9 87.6 all-gather.1

commit v4 on v3

--- a/solution.py
+++ b/solution.py
@@ -15,6 +15,7 @@
 NT = (((1,), (1,)), ((), ()))
 MIB = 1 << 20
 LANES = 128
+VMEM_LIMIT = 28 * MIB
 FREE = pl.CostEstimate(flops=0, bytes_accessed=0, transcendentals=0)
 
 
@@ -49,7 +50,7 @@
 ):
     seq, core = place_ref[0], place_ref[1]
     chans, width = w_lat_ref.shape
-    heads = keep_ref.shape[0]
+    heads, sent = keep_ref.shape[:2]
     part, hd = columns_ref.shape[1:]
     half = chans // 2
     w_lat = w_lat_ref[...].astype(F32)
@@ -91,7 +92,8 @@
             keep_ref[head, rows] = jnp.where(core == 0, top, bottom)
             send_ref[head, rows] = jnp.where(core == 0, bottom, top)
             biases.append(both[chans : chans + 1])
-        biases = jnp.concatenate(biases + [jnp.zeros((5, hd), F32)], axis=0)
+        biases.append(jnp.zeros((sent - 3 * half - 3, hd), F32))
+        biases = jnp.concatenate(biases, axis=0)
         keep_ref[head, 3 * half :] = jnp.where(core == 0, biases, 0.0)
         send_ref[head, 3 * half :] = jnp.where(core == 0, 0.0, biases)
 
@@ -99,22 +101,35 @@
 def fold(place, shifts, w_latent, columns, heads):
     chans = w_latent.shape[0]
     hd = columns.shape[2]
-    sent = jax.ShapeDtypeStruct((heads, 3 * chans // 2 + 8, hd), F32)
+    sent = jax.ShapeDtypeStruct((heads, 3 * chans // 2 + 16, hd), F32)
     return pl.pallas_call(
         fold_kernel,
         in_specs=[pl.BlockSpec(memory_space=pltpu.SMEM)]
         + [pl.BlockSpec(memory_space=pltpu.VMEM)] * 3,
         out_shape=(sent, sent, jax.ShapeDtypeStruct((chans, chans), F32)),
-        compiler_params=pltpu.CompilerParams(vmem_limit_bytes=40 * MIB),
+        compiler_params=pltpu.CompilerParams(vmem_limit_bytes=24 * MIB),
         cost_estimate=FREE,
         name="fold",
     )(place, shifts, w_latent, columns)
 
 
+def add_kernel(one_ref, other_ref, out_ref):
+    out_ref[...] = (one_ref[...] + other_ref[...]).astype(BF16)
+
+
+def add_parts(one, other):
+    return pl.pallas_call(
+        add_kernel,
+        out_shape=jax.ShapeDtypeStruct(one.shape, BF16),
+        cost_estimate=FREE,
+        name="add_parts",
+    )(one, other)
+
+
 def sum_kernel(parts_ref, out_ref):
-    total = parts_ref[0]
+    total = parts_ref[0].astype(F32)
     for part in range(1, parts_ref.shape[0]):
-        total += parts_ref[part]
+        total += parts_ref[part].astype(F32)
     out_ref[...] = total
 
 
@@ -174,7 +189,7 @@
             pltpu.VMEM((sources, tokens // sources * (width // hd), hd), F32),
             pltpu.VMEM((steps * tokens, width), BF16),
         ],
-        compiler_params=pltpu.CompilerParams(vmem_limit_bytes=40 * MIB),
+        compiler_params=pltpu.CompilerParams(vmem_limit_bytes=24 * MIB),
         cost_estimate=FREE,
         name="text_pairs",
     )(place, mine, other, mods, gains)
@@ -253,7 +268,7 @@
             pltpu.VMEM((keys, hd), BF16),
             pltpu.VMEM((keys, 2 * hd), BF16),
         ],
-        compiler_params=pltpu.CompilerParams(vmem_limit_bytes=60 * MIB),
+        compiler_params=pltpu.CompilerParams(vmem_limit_bytes=VMEM_LIMIT),
         cost_estimate=pl.CostEstimate(
             flops=8 * pairs * keys * hd, bytes_accessed=2 * MIB, transcendentals=2 * pairs * keys
         ),
@@ -263,21 +278,13 @@
 
 def output_kernel(
     attended_ref, w_out_ref, x_ref, w_lat_ref, shifts_ref, w_fin_ref, step_ref, added_ref,
-    out_ref, rows_ref, w_ref, mixed_ref, sems
+    out_ref, rows_ref, mixed_ref
 ):
     heads, tokens, hd = attended_ref.shape
-    chunks = sems.shape[0]
+    chunks = mixed_ref.shape[0]
     chans, width = w_lat_ref.shape
     size = width // chunks
     half = tokens // 2
-    copies = [
-        pltpu.make_async_copy(
-            w_out_ref.at[pl.ds(c * size, size)], w_ref.at[pl.ds(c * size, size)], sems.at[c]
-        )
-        for c in range(chunks)
-    ]
-    for copy in copies:
-        copy.start()
     for head in range(heads):
         rows_ref[:, head * hd : (head + 1) * hd] = attended_ref[head]
     x = x_ref[...].astype(F32)
@@ -285,8 +292,7 @@
     total = jnp.zeros((tokens, 1), F32)
     for c in range(chunks):
         cut = slice(c * size, (c + 1) * size)
-        copies[c].wait()
-        mixed = lax.dot_general(rows_ref[...], w_ref[cut], NT, preferred_element_type=F32)
+        mixed = lax.dot_general(rows_ref[...], w_out_ref[cut], NT, preferred_element_type=F32)
         hidden = jnp.dot(x, w_lat_ref[:, cut], preferred_element_type=F32)
         combined = hidden + shifts_ref[2:3, cut] * mixed
         mixed_ref[c] = combined
@@ -317,7 +323,7 @@
         output_kernel,
         in_specs=[
             vmem,
-            pl.BlockSpec(memory_space=pl.ANY),
+            vmem,
             vmem,
             vmem,
             vmem,
@@ -328,11 +334,9 @@
         out_shape=jax.ShapeDtypeStruct((steps,) + added.shape, F32),
         scratch_shapes=[
             pltpu.VMEM((tokens, heads * hd), BF16),
-            pltpu.VMEM((width, heads * hd), BF16),
             pltpu.VMEM((chunks, tokens, width // chunks), F32),
-            pltpu.SemaphoreType.DMA((chunks,)),
         ],
-        compiler_params=pltpu.CompilerParams(vmem_limit_bytes=60 * MIB),
+        compiler_params=pltpu.CompilerParams(vmem_limit_bytes=VMEM_LIMIT),
         cost_estimate=pl.CostEstimate(
             flops=2 * tokens * width * heads * hd,
             bytes_accessed=2 * width * heads * hd,
@@ -342,27 +346,51 @@
     )(attended, w_out, x, w_lat, shifts, w_fin, step_size, added)
 
 
-def scan_kernel(place_ref, everyone_ref, mine_ref, start_ref, out_ref, x_ref):
-    place = place_ref[0]
-    prefix = jnp.zeros(start_ref.shape, F32)
+def prefix_of(place, everyone_ref):
+    prefix = jnp.zeros(everyone_ref.shape[1:], F32)
     for step in range(everyone_ref.shape[0]):
         prefix += jnp.where(step < place, everyone_ref[step], 0.0)
-    out_ref[...] = prefix + mine_ref[0]
-    current = jnp.where(place == 0, start_ref[...], prefix).astype(BF16)
-    x_ref[...] = jnp.broadcast_to(current[None], x_ref.shape)
-
-
-def scan(place, everyone, mine, start, chips):
+    return prefix
+
+
+def scan_kernel(place_ref, everyone_ref, start_ref, x_ref):
+    place = place_ref[2]
+    current = jnp.where(place == 0, start_ref[...], prefix_of(place, everyone_ref))
+    x_ref[...] = jnp.broadcast_to(current.astype(BF16)[None], x_ref.shape)
+
+
+def scan(place, everyone, start, chips):
     return pl.pallas_call(
         scan_kernel,
         in_specs=[pl.BlockSpec(memory_space=pltpu.SMEM)]
-        + [pl.BlockSpec(memory_space=pltpu.VMEM)] * 3,
-        out_shape=(
-            jax.ShapeDtypeStruct(start.shape, F32),
-            jax.ShapeDtypeStruct((chips,) + start.shape, BF16),
-        ),
+        + [pl.BlockSpec(memory_space=pltpu.VMEM)] * 2,
+        out_shape=jax.ShapeDtypeStruct((chips,) + start.shape, BF16),
         name="scan",
-    )(place, everyone, mine, start)
+    )(place, everyone, start)
+
+
+def total_kernel(place_ref, everyone_ref, mine_ref, keep_ref, send_ref):
+    core, place = place_ref[1], place_ref[2]
+    total = prefix_of(place, everyone_ref) + mine_ref[0]
+    half, chans = total.shape[0] // 2, keep_ref.shape[1]
+    top, bottom = total[:half], total[half:]
+    for ref, pairs in (
+        (keep_ref, jnp.where(core == 0, top, bottom)),
+        (send_ref, jnp.where(core == 0, bottom, top)),
+    ):
+        ref[pl.ds(0, half, stride=2), :] = pairs[:, :chans]
+        ref[pl.ds(1, half, stride=2), :] = pairs[:, chans:]
+
+
+def total_rows(place, everyone, mine, rows, chans):
+    half = jax.ShapeDtypeStruct((rows, chans), F32)
+    return pl.pallas_call(
+        total_kernel,
+        in_specs=[pl.BlockSpec(memory_space=pltpu.SMEM)]
+        + [pl.BlockSpec(memory_space=pltpu.VMEM)] * 2,
+        out_shape=(half, half),
+        name="total_rows",
+    )(place, everyone, mine)
 
 
 def local(
@@ -392,11 +420,13 @@
     w_out_mine, text_states, w_text_kv, trajectory, w_image_qkv = lax.optimization_barrier(
         (w_out_mine, text_states, w_text_kv, trajectory, w_image_qkv)
     )
-    w_out = lax.all_gather(w_out_mine, SEQ, tiled=True)
-
     mods = shifts[None, 3:5]
-    while mods.shape[0] < steps:
-        mods = jnp.concatenate([mods, shift_steps(mods, mods.shape[0], steps)], axis=0)
+    back = shift_steps(mods, 1, steps)
+    near = jnp.concatenate([mods, back])
+    back = shift_steps(near, 2, steps)
+    ahead = shift_steps(near, -2, steps)
+    across = shift_steps(near, 4, steps)
+    mods = jnp.concatenate([near, back, across, ahead])
 
     text_mine = lax.dynamic_slice_in_dim(text_states, place * text_rows, text_rows, 1)
     text_norm = layer_norm(text_mine.astype(F32)).astype(BF16)
@@ -411,14 +441,15 @@
     ).reshape(chips * images, rows // 2, 2 * chans)
     packed = jnp.concatenate([weight_block, text_block, latent_block], axis=1)
     columns = jnp.swapaxes(w_image_qkv.reshape(part, 3 * heads, hd), 0, 1)
-    packed, w_latent, shifts, columns = lax.optimization_barrier(
-        (packed, w_latent, shifts, columns)
-    )
+    packed, w_latent, shifts, columns, w_out_mine = lax.optimization_barrier(
+        (packed, w_latent, shifts, columns, w_out_mine)
+    )
+    w_out = lax.all_gather(w_out_mine, SEQ, tiled=True)
     packed = lax.all_to_all(packed, SEQ, 0, 0, tiled=True)
 
-    where = jnp.stack([seq, core]).astype(jnp.int32)
+    where = jnp.stack([seq, core, place]).astype(jnp.int32)
     keep, send, gram = fold(where, shifts, w_latent, columns, heads)
-    mine = keep + swap_cores(send)
+    mine = add_parts(keep, swap_cores(send))
 
     mine, packed, mods = lax.optimization_barrier((mine, packed, mods))
     mine = lax.all_to_all(mine, CHIPS, 0, 0, tiled=True)
@@ -428,12 +459,11 @@
     )
     latents = packed[:, part + text_rows * width // hd :].reshape(-1, 2 * chans)
 
-    text_pairs = jnp.concatenate(
-        [shift_steps(text_pairs[k], -k, steps) for k in range(steps)], axis=0
-    )
-    mine, text_pairs, noise, start_pairs, w_final = lax.optimization_barrier(
-        (mine, text_pairs, noise, start_pairs, w_final)
-    )
+    received = [shift_steps(text_pairs[k], -k, steps) for k in (0, 1, 7, 2, 6, 3, 5, 4)]
+    mine, received[:4], noise, start_pairs, w_final = lax.optimization_barrier(
+        (mine, received[:4], noise, start_pairs, w_final)
+    )
+    text_pairs = jnp.concatenate(received, axis=0)
     mine = sum_parts(mine)
     theirs = swap_cores(mine)
 
@@ -445,9 +475,7 @@
     added = own_noise + jnp.where(place == 0, own_start, jnp.zeros_like(own_start))
     w_fin = jnp.swapaxes(w_final, 0, 1)
 
-    place_ref = place.reshape(1).astype(jnp.int32)
     x_own = own_start.astype(BF16)
-    result = own_start
     for iteration in range(ITERS):
         attended = attention(where, latents, mine, theirs, gram, qk_gains, text_pairs, chips)
         attended = lax.all_to_all(attended, CHIPS, 0, 0, tiled=True)
@@ -455,14 +483,13 @@
             attended, w_out, x_own, w_latent, shifts, w_fin, step_sizes, added, steps
         )
         everyone = lax.all_to_all(contrib, "step", 0, 0, tiled=True)
-        result, latents = scan(place_ref, everyone, contrib, own_start, chips)
         if iteration + 1 < ITERS:
+            latents = scan(where, everyone, own_start, chips)
             x_own = latents[0]
             latents = lax.all_to_all(latents, CHIPS, 0, 0, tiled=True).reshape(-1, 2 * chans)
-    first, second = own_half(
-        jnp.swapaxes(result.reshape(1, 2, rows // 2, 2 * chans), 0, 1), core
-    )
-    return jnp.concatenate([first, second], axis=0).reshape(1, images, rows, chans)
+    kept, sent = total_rows(where, everyone, contrib, rows, chans)
+    came = swap_cores(sent)
+    return jnp.where(core == 0, jnp.stack([kept, came]), jnp.stack([came, kept]))[None]
 
 
 def solution(mesh):

time: 195 us -> 189 us (0.969)
  waiting for transfers between devices: 31.9 us -> 22.7 us
  local copies, waits for them, and re-layouts: 9.11 us -> 17.2 us
  Pallas kernels: 38.2 us -> 30.2 us
  starting transfers between devices: 56.5 us -> 60.9 us
    ppermute x10 -> x11, waiting for transfers between devices: 15 us -> 2.71 us  [shift_steps(): lax.ppermute(values, 'step', [(i, (i + by) % steps) for i in range(steps)])]
    unnamed x38 -> x46, local copies, waits for them, and re-layouts: 4.06 us -> 14.8 us
    ppermute x10 -> x11, starting transfers between devices: 21.1 us -> 26.8 us  [shift_steps(): lax.ppermute(values, 'step', [(i, (i + by) % steps) for i in range(steps)])]
    pallas_call x2 -> x4, Pallas kernels: 18.8 us -> 13.2 us  [the longest x2 9.22 us: output_stage(): pl.pallas_call(output_kernel, in_specs=[vmem, vmem, vmem, vmem, vmem, vme...]
    all_to_all x1, starting transfers between devices: 5.96 us -> 3.56 us  [local(): mine = lax.all_to_all(mine, CHIPS, 0, 0, tiled=True)]
    all_to_all x1, waiting for transfers between devices: 1.91 us -> 3.91 us  [local(): packed = lax.all_to_all(packed, SEQ, 0, 0, tiled=True)]
  transfers between devices with their start and end apart: 20 -> 21, of which waited for: 11 -> 7; matrix products, arithmetic and copies ran while one was open for 5% -> 1% of each run, Pallas kernels for 6% -> 7%
where the time goes in v4:
time: 189 us; the launch traced here: 188 us
  starting transfers between devices  60.9 us (32%)
  blocking collectives  36.4 us (19%)
  Pallas kernels  30.2 us (16%)
  waiting for transfers between devices  22.7 us (12%)
  local copies, waits for them, and re-layouts  17.2 us (9%)
  between operations  14.5 us (8%)
  other arithmetic  5.78 us (3%)
    ppermute x11, starting transfers between devices, shift_steps(): lax.ppermute(values, 'step', [(i, (i + by) % steps) for i in range(steps)])  26.8 us
    all_to_all x2, blocking collectives, local(): everyone = lax.all_to_all(contrib, 'step', 0, 0, tiled=True)  26.1 us
    unnamed x46, local copies, waits for them, and re-layouts  14.8 us
    all_to_all x2, waiting for transfers between devices, local(): attended = lax.all_to_all(attended, CHIPS, 0, 0, tiled=True)  14.3 us
    ppermute x5, starting transfers between devices, swap_cores(): return lax.ppermute(values, 'core', [(0, 1), (1, 0)])  12 us
    all_to_all x2, starting transfers between devices, local(): attended = lax.all_to_all(attended, CHIPS, 0, 0, tiled=True)  10.5 us
    all_to_all x1, blocking collectives, local(): lax.all_to_all(latents, CHIPS, 0, 0, tiled=True).reshape(-1, 2 * chans)  10.3 us
    pallas_call x2, Pallas kernels, output_stage(): pl.pallas_call(output_kernel, in_specs=[vmem, vmem, vmem, vmem, vmem, vme...  9.22 us
  transfers between devices with their start and end apart: 21, of which 7 were waited for; matrix products, arithmetic and copies ran while one was open for 1% of the time, Pallas kernels for 7%

profile of v4, /device:TPU:1, one launch (start us, length us, event | category | flops | bytes accessed | tf_op | source)
XLA Modules:
  0.0 187.6 jit_solution(12276393812656457423)
XLA Ops:
  6.5 2.0 %copy.24 = bf16[12,8,16,128]{3,1,2,0:T(8,128)(2,1)} copy(bf16[12,8,16,128]{3,2,1,0:T(8,128)(2,1)} %bitcast.74) | data formatting | bytes 786432
  8.5 0.8 reshape_squeeze.3
  9.4 1.0 convert_reduce_fusion
  10.4 1.1 fusion.2
  11.5 1.0 fusion.3
  13.3 1.1 pad_maximum_fusion
  14.5 2.5 %collective-permute-start.1 = (f32[1,2,3072]{2,1,0:T(2,128)S(1)}, f32[1,2,3072]{2,1,0:T(2,128)S(1)}, u32[]{:S(2)}, u32[]{:S(2)}) collective-permute-start(f32[1,2,3072]{2,1,0:T(2,128)S(1)} %get-tuple-element.73), channel_id=1, source_target_pairs={{0,32},{32,64},{64,96},{96,128},{128,160},{160,192},{192,224},{224... | collective-permute-start | bytes 73736 | tf_op jit(solution)/shard_map/ppermute | solution.py:45
  17.1 8.0 %all-to-all-start = ((bf16[32,160,128]{2,1,0:T(8,128)(2,1)}), bf16[32,160,128]{2,1,0:T(8,128)(2,1)S(1)}, u32[]{:S(2)}, u32[]{:S(2)}) async-start(bf16[32,160,128]{2,1,0:T(8,128)(2,1)} %pad_maximum_fusion), calls=%async_computation | async-start | bytes 2621440 | tf_op jit(solution)/shard_map/all_to_all | solution.py:448
  25.1 3.1 %collective-permute-start.2 = (f32[2,2,3072]{2,1,0:T(2,128)S(1)}, f32[2,2,3072]{2,1,0:T(2,128)S(1)}, u32[]{:S(2)}, u32[]{:S(2)}) collective-permute-start(f32[2,2,3072]{2,1,0:T(2,128)S(1)} %get-tuple-element.69), channel_id=1, source_target_pairs={{0,64},{32,96},{64,128},{96,160},{128,192},{160,224},{192,0},{224,... | collective-permute-start | bytes 147464 | tf_op jit(solution)/shard_map/ppermute | solution.py:45
  28.3 2.4 %fold.1 = (f32[16,112,128]{2,1,0:T(8,128)S(1)}, f32[16,112,128]{2,1,0:T(8,128)S(1)}, f32[64,64]{1,0:T(8,128)S(1)}) custom-call(s32[3]{0:T(128)S(1)} %pad_add_fusion.place_ref, f32[7,3072]{1,0:T(8,128)S(1)} %bitcast.62, bf16[64,3072]{1,0:T(8,128)(2,1)S(1)} %copy-done.2, bf16[48,96,128]{2,1,0:T(8,128)(2,1)S(1)} %bitcast.61), custom_call_target="tpu_custom_call" | custom-call | tf_op jit(solution)/shard_map/fold/pallas_call | solution.py:105
  30.7 0.9 copy-done.5
  32.1 4.2 %collective-permute-start.3 = (f32[2,2,3072]{2,1,0:T(2,128)S(1)}, f32[2,2,3072]{2,1,0:T(2,128)S(1)}, u32[]{:S(2)}, u32[]{:S(2)}) collective-permute-start(f32[2,2,3072]{2,1,0:T(2,128)S(1)} %get-tuple-element.69), channel_id=1, source_target_pairs={{0,128},{32,160},{64,192},{96,224},{128,0},{160,32},{192,64},{224,... | collective-permute-start | bytes 147464 | tf_op jit(solution)/shard_map/ppermute | solution.py:45
  36.4 2.4 %collective-permute-start.4 = (f32[2,2,3072]{2,1,0:T(2,128)S(1)}, f32[2,2,3072]{2,1,0:T(2,128)S(1)}, u32[]{:S(2)}, u32[]{:S(2)}) collective-permute-start(f32[2,2,3072]{2,1,0:T(2,128)S(1)} %get-tuple-element.69), channel_id=1, source_target_pairs={{0,192},{32,224},{64,0},{96,32},{128,64},{160,96},{192,128},{224,1... | collective-permute-start | bytes 147464 | tf_op jit(solution)/shard_map/ppermute | solution.py:45
  39.4 2.0 %collective-permute-done.4 = f32[2,2,3072]{2,1,0:T(2,128)S(1)} collective-permute-done((f32[2,2,3072]{2,1,0:T(2,128)S(1)}, f32[2,2,3072]{2,1,0:T(2,128)S(1)}, u32[]{:S(2)}, u32[]{:S(2)}) %collective-permute-start.4) | collective-permute-done | bytes 49184 | tf_op jit(solution)/shard_map/ppermute | solution.py:45
  41.5 1.0 copy-done.12
  42.4 2.3 %add_parts.1 = bf16[16,112,128]{2,1,0:T(8,128)(2,1)} custom-call(f32[16,112,128]{2,1,0:T(8,128)} %copy-done.5, f32[16,112,128]{2,1,0:T(8,128)} %copy-done.12), custom_call_target="tpu_custom_call" | custom-call | tf_op jit(solution)/shard_map/add_parts/pallas_call | solution.py:121
  44.8 3.9 %all-to-all-done.mine_ref = bf16[32,160,128]{2,1,0:T(8,128)(2,1)S(1)} async-done(((bf16[32,160,128]{2,1,0:T(8,128)(2,1)}), bf16[32,160,128]{2,1,0:T(8,128)(2,1)S(1)}, u32[]{:S(2)}, u32[]{:S(2)}) %all-to-all-start) | async-done | bytes 1310752 | tf_op jit(solution)/shard_map/all_to_all | solution.py:448
  48.7 1.7 collective-permute-start.5
  50.4 3.6 %all-to-all-start.1 = ((bf16[16,112,128]{2,1,0:T(8,128)(2,1)}), bf16[16,112,128]{2,1,0:T(8,128)(2,1)S(1)}, u32[]{:S(2)}, u32[]{:S(2)}) async-start(bf16[16,112,128]{2,1,0:T(8,128)(2,1)} %add_parts.1), calls=%async_computation.1 | async-start | bytes 917504 | tf_op jit(solution)/shard_map/all_to_all | solution.py:455
  54.0 3.3 %text_pairs.1 = bf16[8,64,256]{2,1,0:T(8,128)(2,1)S(1)} custom-call(s32[3]{0:T(128)S(1)} %pad_add_fusion.place_ref, bf16[32,160,128]{2,1,0:T(8,128)(2,1)S(1)} %all-to-all-done.mine_ref, bf16[32,160,128]{2,1,0:T(8,128)(2,1)} %collective-permute-done.5.other_ref, f32[8,2,3072]{2,1,0:T(2,128)S(1)} %constant_dynamic-update-slice_fusion.2.mods_ref, ...), custom_call_target="tpu_custom_call" | custom-call | tf_op jit(solution)/shard_map/text_pairs/pallas_call | solution.py:183
  57.3 4.2 %collective-permute-start.6 = (bf16[64,256]{1,0:T(8,128)(2,1)S(1)}, bf16[64,256]{1,0:T(8,128)(2,1)S(1)}, u32[]{:S(2)}, u32[]{:S(2)}) collective-permute-start(bf16[64,256]{1,0:T(8,128)(2,1)S(1)} %get-tuple-element.65), channel_id=1, source_target_pairs={{0,224},{32,0},{64,32},{96,64},{128,96},{160,128},{192,160},{224,1... | collective-permute-start | bytes 98312 | tf_op jit(solution)/shard_map/ppermute | solution.py:45
  61.6 2.9 %collective-permute-start.8 = (bf16[64,256]{1,0:T(8,128)(2,1)S(1)}, bf16[64,256]{1,0:T(8,128)(2,1)S(1)}, u32[]{:S(2)}, u32[]{:S(2)}) collective-permute-start(bf16[64,256]{1,0:T(8,128)(2,1)S(1)} %get-tuple-element.63), channel_id=1, source_target_pairs={{0,192},{32,224},{64,0},{96,32},{128,64},{160,96},{192,128},{224,1... | collective-permute-start | bytes 98312 | tf_op jit(solution)/shard_map/ppermute | solution.py:45
  65.2 4.5 %collective-permute-start.11 = (bf16[64,256]{1,0:T(8,128)(2,1)S(1)}, bf16[64,256]{1,0:T(8,128)(2,1)S(1)}, u32[]{:S(2)}, u32[]{:S(2)}) collective-permute-start(bf16[64,256]{1,0:T(8,128)(2,1)S(1)} %get-tuple-element.61), channel_id=1, source_target_pairs={{0,160},{32,192},{64,224},{96,0},{128,32},{160,64},{192,96},{224,1... | collective-permute-start | bytes 98312 | tf_op jit(solution)/shard_map/ppermute | solution.py:45
  69.7 1.1 collective-permute-start.12
  70.8 1.8 collective-permute-start.13
  72.6 0.8 copy-done.10
  73.4 1.7 sum_parts.1.mine_ref
  75.1 2.5 %collective-permute-start.9 = (f32[112,128]{1,0:T(8,128)}, f32[112,128]{1,0:T(8,128)S(1)}, u32[]{:S(2)}, u32[]{:S(2)}) collective-permute-start(f32[112,128]{1,0:T(8,128)} %sum_parts.1.mine_ref), channel_id=1, source_target_pairs={{0,1},{1,0},{2,3},{3,2},{4,5},{5,4},{6,7},{7,6},{8,9},{9,8},{10,11... | collective-permute-start | bytes 172040 | tf_op jit(solution)/shard_map/ppermute | solution.py:33
  77.9 0.8 collective-permute-done.9.theirs_ref
  78.7 0.8 copy-done.6
  79.5 4.0 %attention.2 = bf16[16,64,128]{2,1,0:T(8,128)(2,1)} custom-call(s32[3]{0:T(128)S(1)} %pad_add_fusion.place_ref, bf16[512,128]{1,0:T(8,128)(2,1)S(1)} %bitcast.67, f32[112,128]{1,0:T(8,128)S(1)} %copy-done.6, f32[112,128]{1,0:T(8,128)S(1)} %collective-permute-done.9.theirs_ref, f32[64,64]{1,0:T(8,128)S(1)} %get-tuple-element.46.gram_ref, ...), custom_call_target="tpu_custom_call" | custom-call | flops 805306368 | bytes 2097152 | tf_op jit(solution)/shard_map/attention/pallas_call | solution.py:261
  83.5 6.9 %all-to-all-start.2 = ((bf16[16,64,128]{2,1,0:T(8,128)(2,1)}), bf16[16,64,128]{2,1,0:T(8,128)(2,1)S(1)}, u32[]{:S(2)}, u32[]{:S(2)}) async-start(bf16[16,64,128]{2,1,0:T(8,128)(2,1)} %attention.2), calls=%async_computation.2 | async-start | bytes 524288 | tf_op jit(solution)/shard_map/all_to_all | solution.py:481
  90.5 7.5 %all-to-all-done.2.attended_ref = bf16[16,64,128]{2,1,0:T(8,128)(2,1)S(1)} async-done(((bf16[16,64,128]{2,1,0:T(8,128)(2,1)}), bf16[16,64,128]{2,1,0:T(8,128)(2,1)S(1)}, u32[]{:S(2)}, u32[]{:S(2)}) %all-to-all-start.2) | async-done | bytes 262176 | tf_op jit(solution)/shard_map/all_to_all | solution.py:481
  98.0 4.6 %copy-done = bf16[3072,2048]{1,0:T(8,128)(2,1)S(1)} copy-done((bf16[3072,2048]{1,0:T(8,128)(2,1)S(1)}, bf16[3072,2048]{1,0:T(8,128)(2,1)}, u32[]{:S(2)}) %copy-start) | copy-done | bytes 12582936
  102.6 4.6 %output_stage.2 = f32[8,32,128]{2,1,0:T(8,128)S(1)} custom-call(bf16[16,64,128]{2,1,0:T(8,128)(2,1)S(1)} %all-to-all-done.2.attended_ref, bf16[3072,2048]{1,0:T(8,128)(2,1)S(1)} %copy-done, bf16[32,128]{1,0:T(8,128)(2,1)S(1)} %convert_element_type.19.x_ref, bf16[64,3072]{1,0:T(8,128)(2,1)S(1)} %copy-done.2, f32[7,3072]{1,0:T(8,128)S(1)} %bitcast.63, ...), custom_call_target="tpu_custom_call" | custom-call | flops 805306368 | bytes 12582912 | tf_op jit(solution)/shard_map/output_stage/pallas_call | solution.py:322
  107.2 15.1 %all_to_all.35.everyone_ref = f32[8,32,128]{2,1,0:T(8,128)} all-to-all(f32[8,32,128]{2,1,0:T(8,128)S(1)} %output_stage.2), channel_id=1, replica_groups=mesh['step'=8,'y'=4,'x'=4,'core'=2] {'step'}, dimensions={0} | all-to-all | bytes 262144 | tf_op jit(solution)/shard_map/all_to_all | solution.py:485
  122.3 1.6 scan.1
  123.9 10.3 %all_to_all.36 = bf16[16,32,128]{2,1,0:T(8,128)(2,1)S(1)} all-to-all(bf16[16,32,128]{2,1,0:T(8,128)(2,1)} %scan.1), channel_id=1, replica_groups=mesh['step'=8,'y'=4,'x'=4,'core'=2] {'y','x'}, dimensions={0} | all-to-all | bytes 262144 | tf_op jit(solution)/shard_map/all_to_all | solution.py:489
  134.2 4.0 %attention.3 = bf16[16,64,128]{2,1,0:T(8,128)(2,1)} custom-call(s32[3]{0:T(128)S(1)} %copy-done.8, bf16[512,128]{1,0:T(8,128)(2,1)S(1)} %bitcast.68, f32[112,128]{1,0:T(8,128)S(1)} %copy-done.6, f32[112,128]{1,0:T(8,128)S(1)} %collective-permute-done.9.theirs_ref, f32[64,64]{1,0:T(8,128)S(1)} %get-tuple-element.46.gram_ref, f32[3,128]{1,0:T(4,128)S(1)} %copy-done.9, ...), custom_call_target="tpu_custom_call" | custom-call | flops 805306368 | bytes 2097152 | tf_op jit(solution)/shard_map/attention/pallas_call | solution.py:261
  138.2 3.5 %all-to-all-start.5 = ((bf16[16,64,128]{2,1,0:T(8,128)(2,1)}), bf16[16,64,128]{2,1,0:T(8,128)(2,1)S(1)}, u32[]{:S(2)}, u32[]{:S(2)}) async-start(bf16[16,64,128]{2,1,0:T(8,128)(2,1)} %attention.3), calls=%async_computation.5 | async-start | bytes 524288 | tf_op jit(solution)/shard_map/all_to_all | solution.py:481
  142.4 6.8 %all-to-all-done.5.attended_ref = bf16[16,64,128]{2,1,0:T(8,128)(2,1)S(1)} async-done(((bf16[16,64,128]{2,1,0:T(8,128)(2,1)}), bf16[16,64,128]{2,1,0:T(8,128)(2,1)S(1)}, u32[]{:S(2)}, u32[]{:S(2)}) %all-to-all-start.5) | async-done | bytes 262176 | tf_op jit(solution)/shard_map/all_to_all | solution.py:481
  149.2 4.6 %copy-done.1 = bf16[3072,2048]{1,0:T(8,128)(2,1)S(1)} copy-done((bf16[3072,2048]{1,0:T(8,128)(2,1)S(1)}, bf16[3072,2048]{1,0:T(8,128)(2,1)}, u32[]{:S(2)}) %copy-start.1) | copy-done | bytes 12582936
  153.8 4.6 %output_stage.3.mine_ref = f32[8,32,128]{2,1,0:T(8,128)S(1)} custom-call(bf16[16,64,128]{2,1,0:T(8,128)(2,1)S(1)} %all-to-all-done.5.attended_ref, bf16[3072,2048]{1,0:T(8,128)(2,1)S(1)} %copy-done.1, bf16[32,128]{1,0:T(8,128)(2,1)S(1)} %slice_bitcast_fusion.8.x_ref, bf16[64,3072]{1,0:T(8,128)(2,1)S(1)} %copy-done.2, f32[7,3072]{1,0:T(8,128)S(1)} %bitcast.64, ...), custom_call_target="tpu_custom_call" | custom-call | flops 805306368 | bytes 12582912 | tf_op jit(solution)/shard_map/output_stage/pallas_call | solution.py:322
  158.4 11.0 %all_to_all.37.everyone_ref = f32[8,32,128]{2,1,0:T(8,128)} all-to-all(f32[8,32,128]{2,1,0:T(8,128)S(1)} %output_stage.3.mine_ref), channel_id=1, replica_groups=mesh['step'=8,'y'=4,'x'=4,'core'=2] {'step'}, dimensions={0} | all-to-all | bytes 262144 | tf_op jit(solution)/shard_map/all_to_all | solution.py:485
  169.4 1.7 total_rows.1
  171.1 7.2 %collective-permute-start.15 = (f32[32,64]{1,0:T(8,128)}, f32[32,64]{1,0:T(8,128)S(1)}, u32[]{:S(2)}, u32[]{:S(2)}) collective-permute-start(f32[32,64]{1,0:T(8,128)} %get-tuple-element.56), channel_id=1, source_target_pairs={{0,1},{1,0},{2,3},{3,2},{4,5},{5,4},{6,7},{7,6},{8,9},{9,8},{10,11... | collective-permute-start | bytes 24584 | tf_op jit(solution)/shard_map/ppermute | solution.py:33
  178.3 1.0 collective-permute-done.15
  179.4 1.4 maximum_select_fusion
  (82 shorter events, 3.3 us)
Async XLA Ops:
  6.5 6.0 %copy-start.13 = (bf16[96,2,16,128]{3,2,1,0:T(8,128)(2,1)S(1)}, bf16[96,2,16,128]{3,2,1,0:T(8,128)(2,1)}, u32[]{:S(2)}) copy-start(bf16[96,2,16,128]{3,2,1,0:T(8,128)(2,1)} %param.18) | copy-start | bytes 2359300
  6.5 6.3 %copy-start.15 = (f32[1,7,3072]{2,0,1:T(1,128)S(1)}, f32[1,7,3072]{2,0,1:T(1,128)}, u32[]{:S(2)}) copy-start(f32[1,7,3072]{2,0,1:T(1,128)} %param.14) | copy-start | bytes 258052
  6.5 91.5 %all-gather.2.cloned.1.call-start = ((), (), s32[]{:S(2)}) async-start(), calls=%async_computation.7 | async-start | bytes 12976128 | tf_op jit(solution)/shard_map/all_gather | solution.py:447
  6.5 6.3 %copy-start.11 = (bf16[96,3,16,128]{3,2,1,0:T(8,128)(2,1)S(1)}, bf16[96,3,16,128]{3,2,1,0:T(8,128)(2,1)}, u32[]{:S(2)}) copy-start(bf16[96,3,16,128]{3,2,1,0:T(8,128)(2,1)} %param.17) | copy-start | bytes 3538948
  13.3 1.2 slice-start
  14.5 13.8 %copy-start.2 = (bf16[64,3072]{1,0:T(8,128)(2,1)S(1)}, bf16[64,3072]{1,0:T(8,128)(2,1)}, u32[]{:S(2)}) copy-start(bf16[64,3072]{1,0:T(8,128)(2,1)} %w_lat_ref.2) | copy-start | bytes 1179652
  14.5 10.6 %collective-permute-start.1 = (f32[1,2,3072]{2,1,0:T(2,128)S(1)}, f32[1,2,3072]{2,1,0:T(2,128)S(1)}, u32[]{:S(2)}, u32[]{:S(2)}) collective-permute-start(f32[1,2,3072]{2,1,0:T(2,128)S(1)} %get-tuple-element.73), channel_id=1, source_target_pairs={{0,32},{32,64},{64,96},{96,128},{128,160},{160,192},{192,224},{224... | collective-permute-start | bytes 73736 | tf_op jit(solution)/shard_map/ppermute | solution.py:45
  17.1 31.6 %all-to-all-start = ((bf16[32,160,128]{2,1,0:T(8,128)(2,1)}), bf16[32,160,128]{2,1,0:T(8,128)(2,1)S(1)}, u32[]{:S(2)}, u32[]{:S(2)}) async-start(bf16[32,160,128]{2,1,0:T(8,128)(2,1)} %pad_maximum_fusion), calls=%async_computation | async-start | bytes 2621440 | tf_op jit(solution)/shard_map/all_to_all | solution.py:448
  25.1 13.6 %collective-permute-start.2 = (f32[2,2,3072]{2,1,0:T(2,128)S(1)}, f32[2,2,3072]{2,1,0:T(2,128)S(1)}, u32[]{:S(2)}, u32[]{:S(2)}) collective-permute-start(f32[2,2,3072]{2,1,0:T(2,128)S(1)} %get-tuple-element.69), channel_id=1, source_target_pairs={{0,64},{32,96},{64,128},{96,160},{128,192},{160,224},{192,0},{224,... | collective-permute-start | bytes 147464 | tf_op jit(solution)/shard_map/ppermute | solution.py:45
  28.3 50.4 %copy-start.7 = (s32[3]{0:T(128)}, s32[3]{0:T(128)S(1)}, u32[]{:S(2)}) copy-start(s32[3]{0:T(128)S(1)} %pad_add_fusion.place_ref) | copy-start | bytes 40
  30.7 0.9 copy-start.5
  31.6 9.8 %collective-permute-start = (f32[16,112,128]{2,1,0:T(8,128)S(1)}, f32[16,112,128]{2,1,0:T(8,128)S(1)}, u32[]{:S(2)}, u32[]{:S(2)}) collective-permute-start(f32[16,112,128]{2,1,0:T(8,128)S(1)} %get-tuple-element.40), channel_id=1, source_target_pairs={{0,1},{1,0},{2,3},{3,2},{4,5},{5,4},{6,7},{7,6},{8,9},{9,8},{10,11... | collective-permute-start | bytes 2752520 | tf_op jit(solution)/shard_map/ppermute | solution.py:33
  32.1 7.3 %collective-permute-start.3 = (f32[2,2,3072]{2,1,0:T(2,128)S(1)}, f32[2,2,3072]{2,1,0:T(2,128)S(1)}, u32[]{:S(2)}, u32[]{:S(2)}) collective-permute-start(f32[2,2,3072]{2,1,0:T(2,128)S(1)} %get-tuple-element.69), channel_id=1, source_target_pairs={{0,128},{32,160},{64,192},{96,224},{128,0},{160,32},{192,64},{224,... | collective-permute-start | bytes 147464 | tf_op jit(solution)/shard_map/ppermute | solution.py:45
  36.4 5.1 %collective-permute-start.4 = (f32[2,2,3072]{2,1,0:T(2,128)S(1)}, f32[2,2,3072]{2,1,0:T(2,128)S(1)}, u32[]{:S(2)}, u32[]{:S(2)}) collective-permute-start(f32[2,2,3072]{2,1,0:T(2,128)S(1)} %get-tuple-element.69), channel_id=1, source_target_pairs={{0,192},{32,224},{64,0},{96,32},{128,64},{160,96},{192,128},{224,1... | collective-permute-start | bytes 147464 | tf_op jit(solution)/shard_map/ppermute | solution.py:45
  41.5 1.0 copy-start.12
  42.4 11.5 %copy-start.9 = (f32[3,128]{1,0:T(4,128)S(1)}, f32[3,128]{1,0:T(4,128)}, u32[]{:S(2)}) copy-start(f32[3,128]{1,0:T(4,128)} %gains_ref.5) | copy-start | bytes 4612
  48.7 5.2 %collective-permute-start.5 = (bf16[32,160,128]{2,1,0:T(8,128)(2,1)S(1)}, bf16[32,160,128]{2,1,0:T(8,128)(2,1)}, u32[]{:S(2)}, u32[]{:S(2)}) collective-permute-start(bf16[32,160,128]{2,1,0:T(8,128)(2,1)S(1)} %all-to-all-done.mine_ref), channel_id=1, source_target_pairs={{0,1},{1,0},{2,3},{3,2},{4,5},{5,4},{6,7},{7,6},{8,9},{9,8},{10,11... | collective-permute-start | bytes 3932168 | tf_op jit(solution)/shard_map/ppermute | solution.py:33
  50.4 22.3 %all-to-all-start.1 = ((bf16[16,112,128]{2,1,0:T(8,128)(2,1)}), bf16[16,112,128]{2,1,0:T(8,128)(2,1)S(1)}, u32[]{:S(2)}, u32[]{:S(2)}) async-start(bf16[16,112,128]{2,1,0:T(8,128)(2,1)} %add_parts.1), calls=%async_computation.1 | async-start | bytes 917504 | tf_op jit(solution)/shard_map/all_to_all | solution.py:455
  57.3 20.3 %copy-start.16 = (f32[1,2,32,64]{3,2,1,0:T(8,128)S(1)}, f32[1,2,32,64]{3,2,1,0:T(8,128)}, u32[]{:S(2)}) copy-start(f32[1,2,32,64]{3,2,1,0:T(8,128)} %param.12) | copy-start | bytes 49156
  57.3 12.4 %collective-permute-start.6 = (bf16[64,256]{1,0:T(8,128)(2,1)S(1)}, bf16[64,256]{1,0:T(8,128)(2,1)S(1)}, u32[]{:S(2)}, u32[]{:S(2)}) collective-permute-start(bf16[64,256]{1,0:T(8,128)(2,1)S(1)} %get-tuple-element.65), channel_id=1, source_target_pairs={{0,224},{32,0},{64,32},{96,64},{128,96},{160,128},{192,160},{224,1... | collective-permute-start | bytes 98312 | tf_op jit(solution)/shard_map/ppermute | solution.py:45
  61.6 9.3 %collective-permute-start.7 = (bf16[64,256]{1,0:T(8,128)(2,1)S(1)}, bf16[64,256]{1,0:T(8,128)(2,1)S(1)}, u32[]{:S(2)}, u32[]{:S(2)}) collective-permute-start(bf16[64,256]{1,0:T(8,128)(2,1)S(1)} %get-tuple-element.64), channel_id=1, source_target_pairs={{0,32},{32,64},{64,96},{96,128},{128,160},{160,192},{192,224},{224... | collective-permute-start | bytes 98312 | tf_op jit(solution)/shard_map/ppermute | solution.py:45
  61.6 11.1 %collective-permute-start.8 = (bf16[64,256]{1,0:T(8,128)(2,1)S(1)}, bf16[64,256]{1,0:T(8,128)(2,1)S(1)}, u32[]{:S(2)}, u32[]{:S(2)}) collective-permute-start(bf16[64,256]{1,0:T(8,128)(2,1)S(1)} %get-tuple-element.63), channel_id=1, source_target_pairs={{0,192},{32,224},{64,0},{96,32},{128,64},{160,96},{192,128},{224,1... | collective-permute-start | bytes 98312 | tf_op jit(solution)/shard_map/ppermute | solution.py:45
  65.1 12.6 %collective-permute-start.10 = (bf16[64,256]{1,0:T(8,128)(2,1)S(1)}, bf16[64,256]{1,0:T(8,128)(2,1)S(1)}, u32[]{:S(2)}, u32[]{:S(2)}) collective-permute-start(bf16[64,256]{1,0:T(8,128)(2,1)S(1)} %get-tuple-element.62), channel_id=1, source_target_pairs={{0,64},{32,96},{64,128},{96,160},{128,192},{160,224},{192,0},{224,... | collective-permute-start | bytes 98312 | tf_op jit(solution)/shard_map/ppermute | solution.py:45
  65.2 12.6 %collective-permute-start.11 = (bf16[64,256]{1,0:T(8,128)(2,1)S(1)}, bf16[64,256]{1,0:T(8,128)(2,1)S(1)}, u32[]{:S(2)}, u32[]{:S(2)}) collective-permute-start(bf16[64,256]{1,0:T(8,128)(2,1)S(1)} %get-tuple-element.61), channel_id=1, source_target_pairs={{0,160},{32,192},{64,224},{96,0},{128,32},{160,64},{192,96},{224,1... | collective-permute-start | bytes 98312 | tf_op jit(solution)/shard_map/ppermute | solution.py:45
  69.7 8.1 %collective-permute-start.12 = (bf16[64,256]{1,0:T(8,128)(2,1)S(1)}, bf16[64,256]{1,0:T(8,128)(2,1)S(1)}, u32[]{:S(2)}, u32[]{:S(2)}) collective-permute-start(bf16[64,256]{1,0:T(8,128)(2,1)S(1)} %get-tuple-element.60), channel_id=1, source_target_pairs={{0,96},{32,128},{64,160},{96,192},{128,224},{160,0},{192,32},{224,... | collective-permute-start | bytes 98312 | tf_op jit(solution)/shard_map/ppermute | solution.py:45
  70.8 7.1 %collective-permute-start.13 = (bf16[64,256]{1,0:T(8,128)(2,1)S(1)}, bf16[64,256]{1,0:T(8,128)(2,1)S(1)}, u32[]{:S(2)}, u32[]{:S(2)}) collective-permute-start(bf16[64,256]{1,0:T(8,128)(2,1)S(1)} %get-tuple-element.59), channel_id=1, source_target_pairs={{0,128},{32,160},{64,192},{96,224},{128,0},{160,32},{192,64},{224,... | collective-permute-start | bytes 98312 | tf_op jit(solution)/shard_map/ppermute | solution.py:45
  72.6 0.8 copy-start.10
  75.1 3.6 %collective-permute-start.9 = (f32[112,128]{1,0:T(8,128)}, f32[112,128]{1,0:T(8,128)S(1)}, u32[]{:S(2)}, u32[]{:S(2)}) collective-permute-start(f32[112,128]{1,0:T(8,128)} %sum_parts.1.mine_ref), channel_id=1, source_target_pairs={{0,1},{1,0},{2,3},{3,2},{4,5},{5,4},{6,7},{7,6},{8,9},{9,8},{10,11... | collective-permute-start | bytes 172040 | tf_op jit(solution)/shard_map/ppermute | solution.py:33
  77.7 12.7 %collective-permute-start.14 = (f32[2,16,128]{2,1,0:T(8,128)S(1)}, f32[2,16,128]{2,1,0:T(8,128)S(1)}, u32[]{:S(2)}, u32[]{:S(2)}) collective-permute-start(f32[2,16,128]{2,1,0:T(8,128)S(1)} %fusion.7), channel_id=1, source_target_pairs={{0,1},{1,0},{2,3},{3,2},{4,5},{5,4},{6,7},{7,6},{8,9},{9,8},{10,11... | collective-permute-start | bytes 49160 | tf_op jit(solution)/shard_map/ppermute | solution.py:33
  78.7 0.8 copy-start.6
  79.5 18.5 %copy-start.3 = (bf16[3072,64]{0,1:T(8,128)(2,1)S(1)}, bf16[3072,64]{0,1:T(8,128)(2,1)}, u32[]{:S(2)}) copy-start(bf16[3072,64]{0,1:T(8,128)(2,1)} %param.21) | copy-start | bytes 1179652
  83.5 14.5 %all-to-all-start.2 = ((bf16[16,64,128]{2,1,0:T(8,128)(2,1)}), bf16[16,64,128]{2,1,0:T(8,128)(2,1)S(1)}, u32[]{:S(2)}, u32[]{:S(2)}) async-start(bf16[16,64,128]{2,1,0:T(8,128)(2,1)} %attention.2), calls=%async_computation.2 | async-start | bytes 524288 | tf_op jit(solution)/shard_map/all_to_all | solution.py:481
  90.5 16.7 %copy-start.14 = (f32[32,128]{1,0:T(8,128)}, f32[32,128]{1,0:T(8,128)S(1)}, u32[]{:S(2)}) copy-start(f32[32,128]{1,0:T(8,128)S(1)} %get-tuple-element.58.start_ref) | copy-start | bytes 49156
  98.0 4.6 %copy-start = (bf16[3072,2048]{1,0:T(8,128)(2,1)S(1)}, bf16[3072,2048]{1,0:T(8,128)(2,1)}, u32[]{:S(2)}) copy-start(bf16[3072,2048]{1,0:T(8,128)(2,1)} %all-gather.2.cloned.1.call-done.w_out_ref) | copy-start | bytes 37748740
  102.6 31.6 %copy-start.8 = (s32[3]{0:T(128)S(1)}, s32[3]{0:T(128)}, u32[]{:S(2)}) copy-start(s32[3]{0:T(128)} %copy-done.7) | copy-start | bytes 40
  138.2 11.0 %all-to-all-start.5 = ((bf16[16,64,128]{2,1,0:T(8,128)(2,1)}), bf16[16,64,128]{2,1,0:T(8,128)(2,1)S(1)}, u32[]{:S(2)}, u32[]{:S(2)}) async-start(bf16[16,64,128]{2,1,0:T(8,128)(2,1)} %attention.3), calls=%async_computation.5 | async-start | bytes 524288 | tf_op jit(solution)/shard_map/all_to_all | solution.py:481
  149.2 4.6 %copy-start.1 = (bf16[3072,2048]{1,0:T(8,128)(2,1)S(1)}, bf16[3072,2048]{1,0:T(8,128)(2,1)}, u32[]{:S(2)}) copy-start(bf16[3072,2048]{1,0:T(8,128)(2,1)} %all-gather.2.cloned.1.call-done.w_out_ref) | copy-start | bytes 37748740
  158.4 11.0 %copy-start.4 = (f32[8,32,128]{2,1,0:T(8,128)}, f32[8,32,128]{2,1,0:T(8,128)S(1)}, u32[]{:S(2)}) copy-start(f32[8,32,128]{2,1,0:T(8,128)S(1)} %output_stage.3.mine_ref) | copy-start | bytes 393220
  171.1 8.3 %collective-permute-start.15 = (f32[32,64]{1,0:T(8,128)}, f32[32,64]{1,0:T(8,128)S(1)}, u32[]{:S(2)}, u32[]{:S(2)}) collective-permute-start(f32[32,64]{1,0:T(8,128)} %get-tuple-element.56), channel_id=1, source_target_pairs={{0,1},{1,0},{2,3},{3,2},{4,5},{5,4},{6,7},{7,6},{8,9},{9,8},{10,11... | collective-permute-start | bytes 24584 | tf_op jit(solution)/shard_map/ppermute | solution.py:33
Sparse Core Ops, SparseCore 0:
  14.6 78.5 all-gather.1

commit v5 on v4

--- a/solution.py
+++ b/solution.py
@@ -121,6 +121,7 @@
     return pl.pallas_call(
         add_kernel,
         out_shape=jax.ShapeDtypeStruct(one.shape, BF16),
+        compiler_params=pltpu.CompilerParams(vmem_limit_bytes=8 * MIB),
         cost_estimate=FREE,
         name="add_parts",
     )(one, other)
@@ -137,6 +138,7 @@
     return pl.pallas_call(
         sum_kernel,
         out_shape=jax.ShapeDtypeStruct(parts.shape[1:], F32),
+        compiler_params=pltpu.CompilerParams(vmem_limit_bytes=8 * MIB),
         cost_estimate=FREE,
         name="sum_parts",
     )(parts)
@@ -365,32 +367,35 @@
         in_specs=[pl.BlockSpec(memory_space=pltpu.SMEM)]
         + [pl.BlockSpec(memory_space=pltpu.VMEM)] * 2,
         out_shape=jax.ShapeDtypeStruct((chips,) + start.shape, BF16),
+        compiler_params=pltpu.CompilerParams(vmem_limit_bytes=8 * MIB),
         name="scan",
     )(place, everyone, start)
 
 
-def total_kernel(place_ref, everyone_ref, mine_ref, keep_ref, send_ref):
-    core, place = place_ref[1], place_ref[2]
-    total = prefix_of(place, everyone_ref) + mine_ref[0]
-    half, chans = total.shape[0] // 2, keep_ref.shape[1]
-    top, bottom = total[:half], total[half:]
-    for ref, pairs in (
-        (keep_ref, jnp.where(core == 0, top, bottom)),
-        (send_ref, jnp.where(core == 0, bottom, top)),
-    ):
-        ref[pl.ds(0, half, stride=2), :] = pairs[:, :chans]
-        ref[pl.ds(1, half, stride=2), :] = pairs[:, chans:]
-
-
-def total_rows(place, everyone, mine, rows, chans):
-    half = jax.ShapeDtypeStruct((rows, chans), F32)
+def total_kernel(place_ref, everyone_ref, out_ref):
+    place = place_ref[2]
+    images, chans = out_ref.shape[0], out_ref.shape[2]
+    pairs = everyone_ref.shape[1]
+    for image in range(images):
+        total = jnp.zeros(everyone_ref.shape[1:], F32)
+        for step in range(everyone_ref.shape[0] // images):
+            part = everyone_ref[step * images + image]
+            total += jnp.where(step <= place, part, 0.0)
+        out_ref[image, pl.ds(0, pairs, stride=2), :] = total[:, :chans]
+        out_ref[image, pl.ds(1, pairs, stride=2), :] = total[:, chans:]
+
+
+def total_rows(place, everyone, images, rows, chans):
     return pl.pallas_call(
         total_kernel,
-        in_specs=[pl.BlockSpec(memory_space=pltpu.SMEM)]
-        + [pl.BlockSpec(memory_space=pltpu.VMEM)] * 2,
-        out_shape=(half, half),
+        in_specs=[
+            pl.BlockSpec(memory_space=pltpu.SMEM),
+            pl.BlockSpec(memory_space=pltpu.VMEM),
+        ],
+        out_shape=jax.ShapeDtypeStruct((images, rows, chans), F32),
+        compiler_params=pltpu.CompilerParams(vmem_limit_bytes=8 * MIB),
         name="total_rows",
-    )(place, everyone, mine)
+    )(place, everyone)
 
 
 def local(
@@ -416,10 +421,6 @@
     text_rows = text_states.shape[1] // steps
     shifts = modulation[0]
 
-    w_out_mine = w_out_t.reshape(part, heads * hd)
-    w_out_mine, text_states, w_text_kv, trajectory, w_image_qkv = lax.optimization_barrier(
-        (w_out_mine, text_states, w_text_kv, trajectory, w_image_qkv)
-    )
     mods = shifts[None, 3:5]
     back = shift_steps(mods, 1, steps)
     near = jnp.concatenate([mods, back])
@@ -441,10 +442,10 @@
     ).reshape(chips * images, rows // 2, 2 * chans)
     packed = jnp.concatenate([weight_block, text_block, latent_block], axis=1)
     columns = jnp.swapaxes(w_image_qkv.reshape(part, 3 * heads, hd), 0, 1)
-    packed, w_latent, shifts, columns, w_out_mine = lax.optimization_barrier(
-        (packed, w_latent, shifts, columns, w_out_mine)
-    )
-    w_out = lax.all_gather(w_out_mine, SEQ, tiled=True)
+    packed, w_latent, shifts, columns, w_out_t = lax.optimization_barrier(
+        (packed, w_latent, shifts, columns, w_out_t)
+    )
+    w_out = lax.all_gather(w_out_t.reshape(part, heads * hd), SEQ, tiled=True)
     packed = lax.all_to_all(packed, SEQ, 0, 0, tiled=True)
 
     where = jnp.stack([seq, core, place]).astype(jnp.int32)
@@ -482,14 +483,14 @@
         contrib = output_stage(
             attended, w_out, x_own, w_latent, shifts, w_fin, step_sizes, added, steps
         )
-        everyone = lax.all_to_all(contrib, "step", 0, 0, tiled=True)
         if iteration + 1 < ITERS:
+            everyone = lax.all_to_all(contrib, "step", 0, 0, tiled=True)
             latents = scan(where, everyone, own_start, chips)
             x_own = latents[0]
             latents = lax.all_to_all(latents, CHIPS, 0, 0, tiled=True).reshape(-1, 2 * chans)
-    kept, sent = total_rows(where, everyone, contrib, rows, chans)
-    came = swap_cores(sent)
-    return jnp.where(core == 0, jnp.stack([kept, came]), jnp.stack([came, kept]))[None]
+    contrib = contrib.reshape(steps * images, rows // 2, 2 * chans)
+    everyone = lax.all_to_all(contrib, ("step", "core"), 0, 0, tiled=True)
+    return total_rows(where, everyone, images, rows, chans)[None]
 
 
 def solution(mesh):

time: 189 us -> 183 us (0.968)
  starting transfers between devices: 60.9 us -> 53.3 us
  blocking collectives: 36.4 us -> 43.7 us
  waiting for transfers between devices: 22.7 us -> 27.2 us
  Pallas kernels: 30.2 us -> 25.8 us
  local copies, waits for them, and re-layouts: 17.2 us -> 13 us
    all_to_all x0 -> x1, blocking collectives: none -> 19.5 us  [local(): everyone = lax.all_to_all(contrib, ('step', 'core'), 0, 0, tiled=True)]
    all_to_all x2 -> x1, blocking collectives: 26.1 us -> 13.4 us  [local(): everyone = lax.all_to_all(contrib, 'step', 0, 0, tiled=True)]
    ppermute x5 -> x4, starting transfers between devices: 12 us -> 4.6 us  [swap_cores(): return lax.ppermute(values, 'core', [(0, 1), (1, 0)])]
    unnamed x46 -> x31, local copies, waits for them, and re-layouts: 14.8 us -> 10.4 us
    all_to_all x1, waiting for transfers between devices: 3.91 us -> 7.63 us  [local(): packed = lax.all_to_all(packed, SEQ, 0, 0, tiled=True)]
    ppermute x11, waiting for transfers between devices: 2.71 us -> 4.61 us  [shift_steps(): lax.ppermute(values, 'step', [(i, (i + by) % steps) for i in range(steps)])]
  transfers between devices with their start and end apart: 21 -> 20, of which waited for: 7 -> 6; matrix products, arithmetic and copies ran while one was open for 1% -> 0% of each run, Pallas kernels for 7% -> 6%
where the time goes in v5:
time: 183 us; the launch traced here: 182 us
  starting transfers between devices  53.3 us (29%)
  blocking collectives  43.7 us (24%)
  waiting for transfers between devices  27.2 us (15%)
  Pallas kernels  25.8 us (14%)
  between operations  14.4 us (8%)
  local copies, waits for them, and re-layouts  13 us (7%)
  other arithmetic  4.35 us (2%)
    ppermute x11, starting transfers between devices, shift_steps(): lax.ppermute(values, 'step', [(i, (i + by) % steps) for i in range(steps)])  26.8 us
    all_to_all x1, blocking collectives, local(): everyone = lax.all_to_all(contrib, ('step', 'core'), 0, 0, tiled=True)  19.5 us
    all_to_all x2, waiting for transfers between devices, local(): attended = lax.all_to_all(attended, CHIPS, 0, 0, tiled=True)  15 us
    all_to_all x1, blocking collectives, local(): everyone = lax.all_to_all(contrib, 'step', 0, 0, tiled=True)  13.4 us
    all_to_all x1, blocking collectives, local(): lax.all_to_all(latents, CHIPS, 0, 0, tiled=True).reshape(-1, 2 * chans)  10.8 us
    unnamed x31, local copies, waits for them, and re-layouts  10.4 us
    all_to_all x2, starting transfers between devices, local(): attended = lax.all_to_all(attended, CHIPS, 0, 0, tiled=True)  10.2 us
    pallas_call x2, Pallas kernels, output_stage(): pl.pallas_call(output_kernel, in_specs=[vmem, vmem, vmem, vmem, vmem, vme...  9.26 us
  transfers between devices with their start and end apart: 20, of which 6 were waited for; matrix products, arithmetic and copies ran while one was open for 0% of the time, Pallas kernels for 6%

profile of v5, /device:TPU:1, one launch (start us, length us, event | category | flops | bytes accessed | tf_op | source)
XLA Modules:
  0.0 181.9 jit_solution(14391379678461596084)
XLA Ops:
  6.5 0.9 reshape_squeeze.3
  7.5 1.0 convert_reduce_fusion
  8.5 1.1 fusion.2
  9.6 1.0 fusion.3
  10.6 1.4 copy.12
  12.1 0.3 copy.13
  12.5 1.1 pad_maximum_fusion
  13.7 0.8 copy.24
  14.6 2.5 %collective-permute-start.1 = (f32[1,2,3072]{2,1,0:T(2,128)S(1)}, f32[1,2,3072]{2,1,0:T(2,128)S(1)}, u32[]{:S(2)}, u32[]{:S(2)}) collective-permute-start(f32[1,2,3072]{2,1,0:T(2,128)S(1)} %get-tuple-element.59), channel_id=1, source_target_pairs={{0,32},{32,64},{64,96},{96,128},{128,160},{160,192},{192,224},{224... | collective-permute-start | bytes 73736 | tf_op jit(solution)/shard_map/ppermute | solution.py:45
  17.1 8.0 %all-to-all-start = ((bf16[32,160,128]{2,1,0:T(8,128)(2,1)}), bf16[32,160,128]{2,1,0:T(8,128)(2,1)S(1)}, u32[]{:S(2)}, u32[]{:S(2)}) async-start(bf16[32,160,128]{2,1,0:T(8,128)(2,1)} %pad_maximum_fusion), calls=%async_computation | async-start | bytes 2621440 | tf_op jit(solution)/shard_map/all_to_all | solution.py:449
  25.2 3.1 %collective-permute-start.2 = (f32[2,2,3072]{2,1,0:T(2,128)S(1)}, f32[2,2,3072]{2,1,0:T(2,128)S(1)}, u32[]{:S(2)}, u32[]{:S(2)}) collective-permute-start(f32[2,2,3072]{2,1,0:T(2,128)S(1)} %get-tuple-element.55), channel_id=1, source_target_pairs={{0,64},{32,96},{64,128},{96,160},{128,192},{160,224},{192,0},{224,... | collective-permute-start | bytes 147464 | tf_op jit(solution)/shard_map/ppermute | solution.py:45
  28.3 0.1 pad_add_fusion.place_ref
  28.4 2.4 %fold.1 = (f32[16,112,128]{2,1,0:T(8,128)S(1)}, f32[16,112,128]{2,1,0:T(8,128)S(1)}, f32[64,64]{1,0:T(8,128)S(1)}) custom-call(s32[3]{0:T(128)S(1)} %pad_add_fusion.place_ref, f32[7,3072]{1,0:T(8,128)S(1)} %bitcast.62, bf16[64,3072]{1,0:T(8,128)(2,1)S(1)} %copy-done.2, bf16[48,96,128]{2,1,0:T(8,128)(2,1)S(1)} %bitcast.61), custom_call_target="tpu_custom_call" | custom-call | tf_op jit(solution)/shard_map/fold/pallas_call | solution.py:105
  30.8 0.6 collective-permute-start
  31.4 4.2 %collective-permute-start.3 = (f32[2,2,3072]{2,1,0:T(2,128)S(1)}, f32[2,2,3072]{2,1,0:T(2,128)S(1)}, u32[]{:S(2)}, u32[]{:S(2)}) collective-permute-start(f32[2,2,3072]{2,1,0:T(2,128)S(1)} %get-tuple-element.55), channel_id=1, source_target_pairs={{0,128},{32,160},{64,192},{96,224},{128,0},{160,32},{192,64},{224,... | collective-permute-start | bytes 147464 | tf_op jit(solution)/shard_map/ppermute | solution.py:45
  35.6 2.4 %collective-permute-start.4 = (f32[2,2,3072]{2,1,0:T(2,128)S(1)}, f32[2,2,3072]{2,1,0:T(2,128)S(1)}, u32[]{:S(2)}, u32[]{:S(2)}) collective-permute-start(f32[2,2,3072]{2,1,0:T(2,128)S(1)} %get-tuple-element.55), channel_id=1, source_target_pairs={{0,192},{32,224},{64,0},{96,32},{128,64},{160,96},{192,128},{224,1... | collective-permute-start | bytes 147464 | tf_op jit(solution)/shard_map/ppermute | solution.py:45
  38.0 0.2 collective-permute-done.3
  38.3 2.2 %collective-permute-done.4 = f32[2,2,3072]{2,1,0:T(2,128)S(1)} collective-permute-done((f32[2,2,3072]{2,1,0:T(2,128)S(1)}, f32[2,2,3072]{2,1,0:T(2,128)S(1)}, u32[]{:S(2)}, u32[]{:S(2)}) %collective-permute-start.4) | collective-permute-done | bytes 49184 | tf_op jit(solution)/shard_map/ppermute | solution.py:45
  40.5 0.9 add_parts.1
  41.5 7.6 %all-to-all-done.mine_ref = bf16[32,160,128]{2,1,0:T(8,128)(2,1)S(1)} async-done(((bf16[32,160,128]{2,1,0:T(8,128)(2,1)}), bf16[32,160,128]{2,1,0:T(8,128)(2,1)S(1)}, u32[]{:S(2)}, u32[]{:S(2)}) %all-to-all-start) | async-done | bytes 1310752 | tf_op jit(solution)/shard_map/all_to_all | solution.py:449
  49.1 1.4 collective-permute-start.5
  50.4 3.6 %all-to-all-start.1 = ((bf16[16,112,128]{2,1,0:T(8,128)(2,1)}), bf16[16,112,128]{2,1,0:T(8,128)(2,1)S(1)}, u32[]{:S(2)}, u32[]{:S(2)}) async-start(bf16[16,112,128]{2,1,0:T(8,128)(2,1)} %add_parts.1), calls=%async_computation.1 | async-start | bytes 917504 | tf_op jit(solution)/shard_map/all_to_all | solution.py:456
  54.0 3.3 %text_pairs.1 = bf16[8,64,256]{2,1,0:T(8,128)(2,1)S(1)} custom-call(s32[3]{0:T(128)S(1)} %pad_add_fusion.place_ref, bf16[32,160,128]{2,1,0:T(8,128)(2,1)S(1)} %all-to-all-done.mine_ref, bf16[32,160,128]{2,1,0:T(8,128)(2,1)} %collective-permute-done.5.other_ref, f32[8,2,3072]{2,1,0:T(2,128)S(1)} %constant_dynamic-update-slice_fusion.2.mods_ref, ...), custom_call_target="tpu_custom_call" | custom-call | tf_op jit(solution)/shard_map/text_pairs/pallas_call | solution.py:185
  57.4 4.2 %collective-permute-start.6 = (bf16[64,256]{1,0:T(8,128)(2,1)S(1)}, bf16[64,256]{1,0:T(8,128)(2,1)S(1)}, u32[]{:S(2)}, u32[]{:S(2)}) collective-permute-start(bf16[64,256]{1,0:T(8,128)(2,1)S(1)} %get-tuple-element.51), channel_id=1, source_target_pairs={{0,224},{32,0},{64,32},{96,64},{128,96},{160,128},{192,160},{224,1... | collective-permute-start | bytes 98312 | tf_op jit(solution)/shard_map/ppermute | solution.py:45
  61.6 2.9 %collective-permute-start.8 = (bf16[64,256]{1,0:T(8,128)(2,1)S(1)}, bf16[64,256]{1,0:T(8,128)(2,1)S(1)}, u32[]{:S(2)}, u32[]{:S(2)}) collective-permute-start(bf16[64,256]{1,0:T(8,128)(2,1)S(1)} %get-tuple-element.49), channel_id=1, source_target_pairs={{0,192},{32,224},{64,0},{96,32},{128,64},{160,96},{192,128},{224,1... | collective-permute-start | bytes 98312 | tf_op jit(solution)/shard_map/ppermute | solution.py:45
  65.2 0.1 collective-permute-start.10
  65.3 4.5 %collective-permute-start.11 = (bf16[64,256]{1,0:T(8,128)(2,1)S(1)}, bf16[64,256]{1,0:T(8,128)(2,1)S(1)}, u32[]{:S(2)}, u32[]{:S(2)}) collective-permute-start(bf16[64,256]{1,0:T(8,128)(2,1)S(1)} %get-tuple-element.47), channel_id=1, source_target_pairs={{0,160},{32,192},{64,224},{96,0},{128,32},{160,64},{192,96},{224,1... | collective-permute-start | bytes 98312 | tf_op jit(solution)/shard_map/ppermute | solution.py:45
  69.8 1.1 collective-permute-start.12
  70.9 1.8 collective-permute-start.13
  72.8 2.5 %collective-permute-start.9 = (f32[112,128]{1,0:T(8,128)S(1)}, f32[112,128]{1,0:T(8,128)S(1)}, u32[]{:S(2)}, u32[]{:S(2)}) collective-permute-start(f32[112,128]{1,0:T(8,128)S(1)} %sum_parts.1.mine_ref), channel_id=1, source_target_pairs={{0,1},{1,0},{2,3},{3,2},{4,5},{5,4},{6,7},{7,6},{8,9},{9,8},{10,11... | collective-permute-start | bytes 172040 | tf_op jit(solution)/shard_map/ppermute | solution.py:33
  75.3 0.1 stack_reshape_squeeze.3
  75.5 0.1 collective-permute-start.14
  75.6 2.1 %collective-permute-done.13 = bf16[64,256]{1,0:T(8,128)(2,1)S(1)} collective-permute-done((bf16[64,256]{1,0:T(8,128)(2,1)S(1)}, bf16[64,256]{1,0:T(8,128)(2,1)S(1)}, u32[]{:S(2)}, u32[]{:S(2)}) %collective-permute-start.13) | collective-permute-done | bytes 32800 | tf_op jit(solution)/shard_map/ppermute | solution.py:45
  77.8 4.0 %attention.2 = bf16[16,64,128]{2,1,0:T(8,128)(2,1)} custom-call(s32[3]{0:T(128)S(1)} %pad_add_fusion.place_ref, bf16[512,128]{1,0:T(8,128)(2,1)S(1)} %bitcast.68, f32[112,128]{1,0:T(8,128)S(1)} %sum_parts.1.mine_ref, f32[112,128]{1,0:T(8,128)S(1)} %collective-permute-done.9.theirs_ref, f32[64,64]{1,0:T(8,128)S(1)} %get-tuple-element.34.gram_ref, ...), custom_call_target="tpu_custom_call" | custom-call | flops 805306368 | bytes 2097152 | tf_op jit(solution)/shard_map/attention/pallas_call | solution.py:263
  81.8 6.7 %all-to-all-start.2 = ((bf16[16,64,128]{2,1,0:T(8,128)(2,1)}), bf16[16,64,128]{2,1,0:T(8,128)(2,1)S(1)}, u32[]{:S(2)}, u32[]{:S(2)}) async-start(bf16[16,64,128]{2,1,0:T(8,128)(2,1)} %attention.2), calls=%async_computation.2 | async-start | bytes 524288 | tf_op jit(solution)/shard_map/all_to_all | solution.py:482
  88.5 7.5 %all-to-all-done.2.attended_ref = bf16[16,64,128]{2,1,0:T(8,128)(2,1)S(1)} async-done(((bf16[16,64,128]{2,1,0:T(8,128)(2,1)}), bf16[16,64,128]{2,1,0:T(8,128)(2,1)S(1)}, u32[]{:S(2)}, u32[]{:S(2)}) %all-to-all-start.2) | async-done | bytes 262176 | tf_op jit(solution)/shard_map/all_to_all | solution.py:482
  96.0 4.6 %copy-done = bf16[3072,2048]{1,0:T(8,128)(2,1)S(1)} copy-done((bf16[3072,2048]{1,0:T(8,128)(2,1)S(1)}, bf16[3072,2048]{1,0:T(8,128)(2,1)}, u32[]{:S(2)}) %copy-start) | copy-done | bytes 12582936
  100.6 4.6 %output_stage.2 = f32[8,32,128]{2,1,0:T(8,128)S(1)} custom-call(bf16[16,64,128]{2,1,0:T(8,128)(2,1)S(1)} %all-to-all-done.2.attended_ref, bf16[3072,2048]{1,0:T(8,128)(2,1)S(1)} %copy-done, bf16[32,128]{1,0:T(8,128)(2,1)S(1)} %convert_element_type.19.x_ref, bf16[64,3072]{1,0:T(8,128)(2,1)S(1)} %copy-done.2, f32[7,3072]{1,0:T(8,128)S(1)} %bitcast.63, ...), custom_call_target="tpu_custom_call" | custom-call | flops 805306368 | bytes 12582912 | tf_op jit(solution)/shard_map/output_stage/pallas_call | solution.py:324
  105.2 13.4 %all_to_all.35.everyone_ref = f32[8,32,128]{2,1,0:T(8,128)S(1)} all-to-all(f32[8,32,128]{2,1,0:T(8,128)S(1)} %output_stage.2), channel_id=1, replica_groups=mesh['step'=8,'y'=4,'x'=4,'core'=2] {'step'}, dimensions={0} | all-to-all | bytes 262144 | tf_op jit(solution)/shard_map/all_to_all | solution.py:487
  118.7 0.6 scan.1
  119.3 10.8 %all_to_all.36 = bf16[16,32,128]{2,1,0:T(8,128)(2,1)S(1)} all-to-all(bf16[16,32,128]{2,1,0:T(8,128)(2,1)S(1)} %scan.1), channel_id=1, replica_groups=mesh['step'=8,'y'=4,'x'=4,'core'=2] {'y','x'}, dimensions={0} | all-to-all | bytes 262144 | tf_op jit(solution)/shard_map/all_to_all | solution.py:490
  130.0 4.0 %attention.3 = bf16[16,64,128]{2,1,0:T(8,128)(2,1)} custom-call(s32[3]{0:T(128)S(1)} %pad_add_fusion.place_ref, bf16[512,128]{1,0:T(8,128)(2,1)S(1)} %bitcast.69, f32[112,128]{1,0:T(8,128)S(1)} %sum_parts.1.mine_ref, f32[112,128]{1,0:T(8,128)S(1)} %collective-permute-done.9.theirs_ref, f32[64,64]{1,0:T(8,128)S(1)} %get-tuple-element.34.gram_ref, ...), custom_call_target="tpu_custom_call" | custom-call | flops 805306368 | bytes 2097152 | tf_op jit(solution)/shard_map/attention/pallas_call | solution.py:263
  134.0 3.5 %all-to-all-start.5 = ((bf16[16,64,128]{2,1,0:T(8,128)(2,1)}), bf16[16,64,128]{2,1,0:T(8,128)(2,1)S(1)}, u32[]{:S(2)}, u32[]{:S(2)}) async-start(bf16[16,64,128]{2,1,0:T(8,128)(2,1)} %attention.3), calls=%async_computation.5 | async-start | bytes 524288 | tf_op jit(solution)/shard_map/all_to_all | solution.py:482
  137.6 7.5 %all-to-all-done.5.attended_ref = bf16[16,64,128]{2,1,0:T(8,128)(2,1)S(1)} async-done(((bf16[16,64,128]{2,1,0:T(8,128)(2,1)}), bf16[16,64,128]{2,1,0:T(8,128)(2,1)S(1)}, u32[]{:S(2)}, u32[]{:S(2)}) %all-to-all-start.5) | async-done | bytes 262176 | tf_op jit(solution)/shard_map/all_to_all | solution.py:482
  145.1 4.6 %copy-done.1 = bf16[3072,2048]{1,0:T(8,128)(2,1)S(1)} copy-done((bf16[3072,2048]{1,0:T(8,128)(2,1)S(1)}, bf16[3072,2048]{1,0:T(8,128)(2,1)}, u32[]{:S(2)}) %copy-start.1) | copy-done | bytes 12582936
  149.7 4.6 %output_stage.3 = f32[8,32,128]{2,1,0:T(8,128)S(1)} custom-call(bf16[16,64,128]{2,1,0:T(8,128)(2,1)S(1)} %all-to-all-done.5.attended_ref, bf16[3072,2048]{1,0:T(8,128)(2,1)S(1)} %copy-done.1, bf16[32,128]{1,0:T(8,128)(2,1)S(1)} %slice_bitcast_fusion.8.x_ref, bf16[64,3072]{1,0:T(8,128)(2,1)S(1)} %copy-done.2, f32[7,3072]{1,0:T(8,128)S(1)} %bitcast.64, ...), custom_call_target="tpu_custom_call" | custom-call | flops 805306368 | bytes 12582912 | tf_op jit(solution)/shard_map/output_stage/pallas_call | solution.py:324
  154.3 19.5 %all_to_all.37.everyone_ref = f32[16,16,128]{2,1,0:T(8,128)S(1)} all-to-all(f32[16,16,128]{2,1,0:T(8,128)S(1)} %bitcast.67), channel_id=1, replica_groups=mesh['step'=8,'y'=4,'x'=4,'core'=2] {'step','core'}, dimensions={0} | all-to-all | bytes 262144 | tf_op jit(solution)/shard_map/all_to_all | solution.py:492
  173.8 1.2 total_rows.1
  (63 shorter events, 0.5 us)
Async XLA Ops:
  6.5 5.5 %copy-start.7 = (f32[1,7,3072]{2,0,1:T(1,128)S(1)}, f32[1,7,3072]{2,0,1:T(1,128)}, u32[]{:S(2)}) copy-start(f32[1,7,3072]{2,0,1:T(1,128)} %param.14) | copy-start | bytes 258052
  6.5 5.6 %copy-start.5 = (bf16[96,3,16,128]{3,2,1,0:T(8,128)(2,1)S(1)}, bf16[96,3,16,128]{3,2,1,0:T(8,128)(2,1)}, u32[]{:S(2)}) copy-start(bf16[96,3,16,128]{3,2,1,0:T(8,128)(2,1)} %param.17) | copy-start | bytes 3538948
  6.5 89.5 %all-gather.2.cloned.1.call-start = ((), (), s32[]{:S(2)}) async-start(), calls=%async_computation.7 | async-start | bytes 12976128 | tf_op jit(solution)/shard_map/all_gather | solution.py:448
  12.5 1.2 copy-start.6
  12.5 2.0 %slice-start = ((f32[1,7,3072]{2,0,1:T(1,128)}), f32[1,2,3072]{2,0,1:T(1,128)S(1)}, s32[]{:S(2)}) async-start(f32[1,7,3072]{2,0,1:T(1,128)} %param.14), calls=%async_computation.8 | async-start | bytes 49152 | tf_op jit(solution)/shard_map/slice | solution.py:424
  14.6 13.8 %copy-start.2 = (bf16[64,3072]{1,0:T(8,128)(2,1)S(1)}, bf16[64,3072]{1,0:T(8,128)(2,1)}, u32[]{:S(2)}) copy-start(bf16[64,3072]{1,0:T(8,128)(2,1)} %w_lat_ref.2) | copy-start | bytes 1179652
  14.6 10.6 %collective-permute-start.1 = (f32[1,2,3072]{2,1,0:T(2,128)S(1)}, f32[1,2,3072]{2,1,0:T(2,128)S(1)}, u32[]{:S(2)}, u32[]{:S(2)}) collective-permute-start(f32[1,2,3072]{2,1,0:T(2,128)S(1)} %get-tuple-element.59), channel_id=1, source_target_pairs={{0,32},{32,64},{64,96},{96,128},{128,160},{160,192},{192,224},{224... | collective-permute-start | bytes 73736 | tf_op jit(solution)/shard_map/ppermute | solution.py:45
  17.1 32.0 %all-to-all-start = ((bf16[32,160,128]{2,1,0:T(8,128)(2,1)}), bf16[32,160,128]{2,1,0:T(8,128)(2,1)S(1)}, u32[]{:S(2)}, u32[]{:S(2)}) async-start(bf16[32,160,128]{2,1,0:T(8,128)(2,1)} %pad_maximum_fusion), calls=%async_computation | async-start | bytes 2621440 | tf_op jit(solution)/shard_map/all_to_all | solution.py:449
  25.2 12.8 %collective-permute-start.2 = (f32[2,2,3072]{2,1,0:T(2,128)S(1)}, f32[2,2,3072]{2,1,0:T(2,128)S(1)}, u32[]{:S(2)}, u32[]{:S(2)}) collective-permute-start(f32[2,2,3072]{2,1,0:T(2,128)S(1)} %get-tuple-element.55), channel_id=1, source_target_pairs={{0,64},{32,96},{64,128},{96,160},{128,192},{160,224},{192,0},{224,... | collective-permute-start | bytes 147464 | tf_op jit(solution)/shard_map/ppermute | solution.py:45
  30.8 9.7 %collective-permute-start = (f32[16,112,128]{2,1,0:T(8,128)S(1)}, f32[16,112,128]{2,1,0:T(8,128)S(1)}, u32[]{:S(2)}, u32[]{:S(2)}) collective-permute-start(f32[16,112,128]{2,1,0:T(8,128)S(1)} %get-tuple-element.28), channel_id=1, source_target_pairs={{0,1},{1,0},{2,3},{3,2},{4,5},{5,4},{6,7},{7,6},{8,9},{9,8},{10,11... | collective-permute-start | bytes 2752520 | tf_op jit(solution)/shard_map/ppermute | solution.py:33
  31.4 6.9 %collective-permute-start.3 = (f32[2,2,3072]{2,1,0:T(2,128)S(1)}, f32[2,2,3072]{2,1,0:T(2,128)S(1)}, u32[]{:S(2)}, u32[]{:S(2)}) collective-permute-start(f32[2,2,3072]{2,1,0:T(2,128)S(1)} %get-tuple-element.55), channel_id=1, source_target_pairs={{0,128},{32,160},{64,192},{96,224},{128,0},{160,32},{192,64},{224,... | collective-permute-start | bytes 147464 | tf_op jit(solution)/shard_map/ppermute | solution.py:45
  35.6 4.9 %collective-permute-start.4 = (f32[2,2,3072]{2,1,0:T(2,128)S(1)}, f32[2,2,3072]{2,1,0:T(2,128)S(1)}, u32[]{:S(2)}, u32[]{:S(2)}) collective-permute-start(f32[2,2,3072]{2,1,0:T(2,128)S(1)} %get-tuple-element.55), channel_id=1, source_target_pairs={{0,192},{32,224},{64,0},{96,32},{128,64},{160,96},{192,128},{224,1... | collective-permute-start | bytes 147464 | tf_op jit(solution)/shard_map/ppermute | solution.py:45
  40.5 13.5 %copy-start.4 = (f32[3,128]{1,0:T(4,128)S(1)}, f32[3,128]{1,0:T(4,128)}, u32[]{:S(2)}) copy-start(f32[3,128]{1,0:T(4,128)} %gains_ref.5) | copy-start | bytes 4612
  49.1 4.9 %collective-permute-start.5 = (bf16[32,160,128]{2,1,0:T(8,128)(2,1)S(1)}, bf16[32,160,128]{2,1,0:T(8,128)(2,1)}, u32[]{:S(2)}, u32[]{:S(2)}) collective-permute-start(bf16[32,160,128]{2,1,0:T(8,128)(2,1)S(1)} %all-to-all-done.mine_ref), channel_id=1, source_target_pairs={{0,1},{1,0},{2,3},{3,2},{4,5},{5,4},{6,7},{7,6},{8,9},{9,8},{10,11... | collective-permute-start | bytes 3932168 | tf_op jit(solution)/shard_map/ppermute | solution.py:33
  50.4 22.3 %all-to-all-start.1 = ((bf16[16,112,128]{2,1,0:T(8,128)(2,1)}), bf16[16,112,128]{2,1,0:T(8,128)(2,1)S(1)}, u32[]{:S(2)}, u32[]{:S(2)}) async-start(bf16[16,112,128]{2,1,0:T(8,128)(2,1)} %add_parts.1), calls=%async_computation.1 | async-start | bytes 917504 | tf_op jit(solution)/shard_map/all_to_all | solution.py:456
  57.4 18.0 %copy-start.8 = (f32[1,2,32,64]{3,2,1,0:T(8,128)S(1)}, f32[1,2,32,64]{3,2,1,0:T(8,128)}, u32[]{:S(2)}) copy-start(f32[1,2,32,64]{3,2,1,0:T(8,128)} %param.12) | copy-start | bytes 49156
  57.4 12.4 %collective-permute-start.6 = (bf16[64,256]{1,0:T(8,128)(2,1)S(1)}, bf16[64,256]{1,0:T(8,128)(2,1)S(1)}, u32[]{:S(2)}, u32[]{:S(2)}) collective-permute-start(bf16[64,256]{1,0:T(8,128)(2,1)S(1)} %get-tuple-element.51), channel_id=1, source_target_pairs={{0,224},{32,0},{64,32},{96,64},{128,96},{160,128},{192,160},{224,1... | collective-permute-start | bytes 98312 | tf_op jit(solution)/shard_map/ppermute | solution.py:45
  61.6 9.3 %collective-permute-start.7 = (bf16[64,256]{1,0:T(8,128)(2,1)S(1)}, bf16[64,256]{1,0:T(8,128)(2,1)S(1)}, u32[]{:S(2)}, u32[]{:S(2)}) collective-permute-start(bf16[64,256]{1,0:T(8,128)(2,1)S(1)} %get-tuple-element.50), channel_id=1, source_target_pairs={{0,32},{32,64},{64,96},{96,128},{128,160},{160,192},{192,224},{224... | collective-permute-start | bytes 98312 | tf_op jit(solution)/shard_map/ppermute | solution.py:45
  61.6 11.1 %collective-permute-start.8 = (bf16[64,256]{1,0:T(8,128)(2,1)S(1)}, bf16[64,256]{1,0:T(8,128)(2,1)S(1)}, u32[]{:S(2)}, u32[]{:S(2)}) collective-permute-start(bf16[64,256]{1,0:T(8,128)(2,1)S(1)} %get-tuple-element.49), channel_id=1, source_target_pairs={{0,192},{32,224},{64,0},{96,32},{128,64},{160,96},{192,128},{224,1... | collective-permute-start | bytes 98312 | tf_op jit(solution)/shard_map/ppermute | solution.py:45
  65.2 10.2 %collective-permute-start.10 = (bf16[64,256]{1,0:T(8,128)(2,1)S(1)}, bf16[64,256]{1,0:T(8,128)(2,1)S(1)}, u32[]{:S(2)}, u32[]{:S(2)}) collective-permute-start(bf16[64,256]{1,0:T(8,128)(2,1)S(1)} %get-tuple-element.48), channel_id=1, source_target_pairs={{0,64},{32,96},{64,128},{96,160},{128,192},{160,224},{192,0},{224,... | collective-permute-start | bytes 98312 | tf_op jit(solution)/shard_map/ppermute | solution.py:45
  65.3 10.3 %collective-permute-start.11 = (bf16[64,256]{1,0:T(8,128)(2,1)S(1)}, bf16[64,256]{1,0:T(8,128)(2,1)S(1)}, u32[]{:S(2)}, u32[]{:S(2)}) collective-permute-start(bf16[64,256]{1,0:T(8,128)(2,1)S(1)} %get-tuple-element.47), channel_id=1, source_target_pairs={{0,160},{32,192},{64,224},{96,0},{128,32},{160,64},{192,96},{224,1... | collective-permute-start | bytes 98312 | tf_op jit(solution)/shard_map/ppermute | solution.py:45
  69.8 5.8 %collective-permute-start.12 = (bf16[64,256]{1,0:T(8,128)(2,1)S(1)}, bf16[64,256]{1,0:T(8,128)(2,1)S(1)}, u32[]{:S(2)}, u32[]{:S(2)}) collective-permute-start(bf16[64,256]{1,0:T(8,128)(2,1)S(1)} %get-tuple-element.46), channel_id=1, source_target_pairs={{0,96},{32,128},{64,160},{96,192},{128,224},{160,0},{192,32},{224,... | collective-permute-start | bytes 98312 | tf_op jit(solution)/shard_map/ppermute | solution.py:45
  70.9 6.8 %collective-permute-start.13 = (bf16[64,256]{1,0:T(8,128)(2,1)S(1)}, bf16[64,256]{1,0:T(8,128)(2,1)S(1)}, u32[]{:S(2)}, u32[]{:S(2)}) collective-permute-start(bf16[64,256]{1,0:T(8,128)(2,1)S(1)} %get-tuple-element.45), channel_id=1, source_target_pairs={{0,128},{32,160},{64,192},{96,224},{128,0},{160,32},{192,64},{224,... | collective-permute-start | bytes 98312 | tf_op jit(solution)/shard_map/ppermute | solution.py:45
  72.8 5.0 %collective-permute-start.9 = (f32[112,128]{1,0:T(8,128)S(1)}, f32[112,128]{1,0:T(8,128)S(1)}, u32[]{:S(2)}, u32[]{:S(2)}) collective-permute-start(f32[112,128]{1,0:T(8,128)S(1)} %sum_parts.1.mine_ref), channel_id=1, source_target_pairs={{0,1},{1,0},{2,3},{3,2},{4,5},{5,4},{6,7},{7,6},{8,9},{9,8},{10,11... | collective-permute-start | bytes 172040 | tf_op jit(solution)/shard_map/ppermute | solution.py:33
  75.5 13.0 %collective-permute-start.14 = (f32[2,16,128]{2,1,0:T(8,128)S(1)}, f32[2,16,128]{2,1,0:T(8,128)S(1)}, u32[]{:S(2)}, u32[]{:S(2)}) collective-permute-start(f32[2,16,128]{2,1,0:T(8,128)S(1)} %fusion.7), channel_id=1, source_target_pairs={{0,1},{1,0},{2,3},{3,2},{4,5},{5,4},{6,7},{7,6},{8,9},{9,8},{10,11... | collective-permute-start | bytes 49160 | tf_op jit(solution)/shard_map/ppermute | solution.py:33
  77.8 18.3 %copy-start.3 = (bf16[3072,64]{0,1:T(8,128)(2,1)S(1)}, bf16[3072,64]{0,1:T(8,128)(2,1)}, u32[]{:S(2)}) copy-start(bf16[3072,64]{0,1:T(8,128)(2,1)} %param.21) | copy-start | bytes 1179652
  81.8 14.3 %all-to-all-start.2 = ((bf16[16,64,128]{2,1,0:T(8,128)(2,1)}), bf16[16,64,128]{2,1,0:T(8,128)(2,1)S(1)}, u32[]{:S(2)}, u32[]{:S(2)}) async-start(bf16[16,64,128]{2,1,0:T(8,128)(2,1)} %attention.2), calls=%async_computation.2 | async-start | bytes 524288 | tf_op jit(solution)/shard_map/all_to_all | solution.py:482
  96.0 4.6 %copy-start = (bf16[3072,2048]{1,0:T(8,128)(2,1)S(1)}, bf16[3072,2048]{1,0:T(8,128)(2,1)}, u32[]{:S(2)}) copy-start(bf16[3072,2048]{1,0:T(8,128)(2,1)} %all-gather.2.cloned.1.call-done.w_out_ref) | copy-start | bytes 37748740
  134.0 11.0 %all-to-all-start.5 = ((bf16[16,64,128]{2,1,0:T(8,128)(2,1)}), bf16[16,64,128]{2,1,0:T(8,128)(2,1)S(1)}, u32[]{:S(2)}, u32[]{:S(2)}) async-start(bf16[16,64,128]{2,1,0:T(8,128)(2,1)} %attention.3), calls=%async_computation.5 | async-start | bytes 524288 | tf_op jit(solution)/shard_map/all_to_all | solution.py:482
  145.1 4.6 %copy-start.1 = (bf16[3072,2048]{1,0:T(8,128)(2,1)S(1)}, bf16[3072,2048]{1,0:T(8,128)(2,1)}, u32[]{:S(2)}) copy-start(bf16[3072,2048]{1,0:T(8,128)(2,1)} %all-gather.2.cloned.1.call-done.w_out_ref) | copy-start | bytes 37748740
Sparse Core Ops, SparseCore 0:
  14.7 78.5 all-gather.1

commit v6 on v5

--- a/solution.py
+++ b/solution.py
@@ -113,31 +113,41 @@
     )(place, shifts, w_latent, columns)
 
 
-def add_kernel(one_ref, other_ref, out_ref):
-    out_ref[...] = (one_ref[...] + other_ref[...]).astype(BF16)
-
-
-def add_parts(one, other):
+def add_kernel(one_ref, other_ref, x_ref, out_ref):
+    count = one_ref.shape[1]
+    out_ref[:, :count] = (one_ref[...] + other_ref[...]).astype(BF16)
+    for chip in range(out_ref.shape[0]):
+        out_ref[chip, count:] = x_ref[...].astype(BF16)
+
+
+def add_parts(one, other, x):
+    chips, count, hd = one.shape
     return pl.pallas_call(
         add_kernel,
-        out_shape=jax.ShapeDtypeStruct(one.shape, BF16),
+        out_shape=jax.ShapeDtypeStruct((chips, count + x.shape[0], hd), BF16),
         compiler_params=pltpu.CompilerParams(vmem_limit_bytes=8 * MIB),
         cost_estimate=FREE,
         name="add_parts",
-    )(one, other)
-
-
-def sum_kernel(parts_ref, out_ref):
-    total = parts_ref[0].astype(F32)
+    )(one, other, x)
+
+
+def sum_kernel(parts_ref, out_ref, x_ref):
+    count = out_ref.shape[0]
+    total = parts_ref[0, :count].astype(F32)
     for part in range(1, parts_ref.shape[0]):
-        total += parts_ref[part].astype(F32)
+        total += parts_ref[part, :count].astype(F32)
     out_ref[...] = total
-
-
-def sum_parts(parts):
+    x_ref[...] = parts_ref[:, count:]
+
+
+def sum_parts(parts, below):
+    chips, count, hd = parts.shape
     return pl.pallas_call(
         sum_kernel,
-        out_shape=jax.ShapeDtypeStruct(parts.shape[1:], F32),
+        out_shape=(
+            jax.ShapeDtypeStruct((count - below, hd), F32),
+            jax.ShapeDtypeStruct((chips, below, hd), BF16),
+        ),
         compiler_params=pltpu.CompilerParams(vmem_limit_bytes=8 * MIB),
         cost_estimate=FREE,
         name="sum_parts",
@@ -242,7 +252,7 @@
         k_ref[image] = rms_scale(image_keys, gains_ref[1:2]).astype(BF16)
         v_ref[image, :hd] = (projected[:, 2 * hd : 3 * hd] * scale + bias[2]).astype(BF16)
     half = block // 2
-    size = 256
+    size = 128
     for start in range(0, 2 * pairs, size):
         scores = lax.dot_general(
             q_ref[start : start + size], k_ref[...], NT, preferred_element_type=F32
@@ -319,7 +329,7 @@
 def output_stage(attended, w_out, x, w_lat, shifts, w_fin, step_size, added, steps):
     heads, tokens, hd = attended.shape
     width = w_out.shape[0]
-    chunks = 6
+    chunks = 12
     vmem = pl.BlockSpec(memory_space=pltpu.VMEM)
     return pl.pallas_call(
         output_kernel,
@@ -437,10 +447,7 @@
     ).reshape(chips * images, -1, hd)
     weight_block = jnp.transpose(w_text_kv, (2, 1, 0, 3)).reshape(2 * heads, part, hd)
     start_pairs = trajectory[0].reshape(images, rows // 2, 2 * chans)
-    latent_block = jnp.broadcast_to(
-        start_pairs.astype(BF16)[None], (chips, images, rows // 2, 2 * chans)
-    ).reshape(chips * images, rows // 2, 2 * chans)
-    packed = jnp.concatenate([weight_block, text_block, latent_block], axis=1)
+    packed = jnp.concatenate([weight_block, text_block], axis=1)
     columns = jnp.swapaxes(w_image_qkv.reshape(part, 3 * heads, hd), 0, 1)
     packed, w_latent, shifts, columns, w_out_t = lax.optimization_barrier(
         (packed, w_latent, shifts, columns, w_out_t)
@@ -450,29 +457,26 @@
 
     where = jnp.stack([seq, core, place]).astype(jnp.int32)
     keep, send, gram = fold(where, shifts, w_latent, columns, heads)
-    mine = add_parts(keep, swap_cores(send))
-
-    mine, packed, mods = lax.optimization_barrier((mine, packed, mods))
-    mine = lax.all_to_all(mine, CHIPS, 0, 0, tiled=True)
-
-    text_pairs = text_pairs_of(
-        where, packed, swap_cores(packed), mods, qk_gains, text_rows * lax.axis_size(SEQ)
-    )
-    latents = packed[:, part + text_rows * width // hd :].reshape(-1, 2 * chans)
-
-    received = [shift_steps(text_pairs[k], -k, steps) for k in (0, 1, 7, 2, 6, 3, 5, 4)]
-    mine, received[:4], noise, start_pairs, w_final = lax.optimization_barrier(
-        (mine, received[:4], noise, start_pairs, w_final)
-    )
-    text_pairs = jnp.concatenate(received, axis=0)
-    mine = sum_parts(mine)
-    theirs = swap_cores(mine)
-
     noise_pairs = noise[0].reshape(images, rows // 2, 2 * chans)
     own = jnp.concatenate(
         own_half(jnp.stack([noise_pairs, start_pairs], axis=1), core), axis=1
     )
     own_noise, own_start = own[0], own[1]
+    mine = add_parts(keep, swap_cores(send), own_start)
+
+    mine, packed, mods = lax.optimization_barrier((mine, packed, mods))
+    mine = lax.all_to_all(mine, CHIPS, 0, 0, tiled=True)
+
+    text_pairs = text_pairs_of(
+        where, packed, swap_cores(packed), mods, qk_gains, text_rows * lax.axis_size(SEQ)
+    )
+    received = [shift_steps(text_pairs[k], -k, steps) for k in (0, 1, 7, 2, 6, 3, 5, 4)]
+    mine, received[:4], w_final = lax.optimization_barrier((mine, received[:4], w_final))
+    text_pairs = jnp.concatenate(received, axis=0)
+    mine, latents = sum_parts(mine, rows)
+    latents = latents.reshape(-1, 2 * chans)
+    theirs = swap_cores(mine)
+
     added = own_noise + jnp.where(place == 0, own_start, jnp.zeros_like(own_start))
     w_fin = jnp.swapaxes(w_final, 0, 1)
 

time: 183 us -> 181 us (0.989)
  starting transfers between devices: 53.3 us -> 51.4 us
    ppermute x11, waiting for transfers between devices: 4.61 us -> 9.39 us  [shift_steps(): lax.ppermute(values, 'step', [(i, (i + by) % steps) for i in range(steps)])]
    all_to_all x1, waiting for transfers between devices: 7.63 us -> 3.74 us  [local(): packed = lax.all_to_all(packed, SEQ, 0, 0, tiled=True)]
    all_to_all x1, blocking collectives: 19.5 us -> 16.7 us  [local(): everyone = lax.all_to_all(contrib, ('step', 'core'), 0, 0, tiled=True)]
    all_to_all x1, starting transfers between devices: 8.04 us -> 5.85 us  [local(): packed = lax.all_to_all(packed, SEQ, 0, 0, tiled=True)]
    unnamed x31 -> x37, local copies, waits for them, and re-layouts: 10.4 us -> 11.4 us
  transfers between devices with their start and end apart: 20 -> 20, of which waited for: 6 -> 7; matrix products, arithmetic and copies ran while one was open for 0% -> 0% of each run, Pallas kernels for 6% -> 7%
where the time goes in v6:
time: 181 us; the launch traced here: 180 us
  starting transfers between devices  51.4 us (28%)
  blocking collectives  42.9 us (24%)
  waiting for transfers between devices  27.7 us (15%)
  Pallas kernels  26.6 us (15%)
  between operations  14.4 us (8%)
  local copies, waits for them, and re-layouts  13.1 us (7%)
  other arithmetic  4.4 us (2%)
    ppermute x11, starting transfers between devices, shift_steps(): lax.ppermute(values, 'step', [(i, (i + by) % steps) for i in range(steps)])  25.5 us
    all_to_all x1, blocking collectives, local(): everyone = lax.all_to_all(contrib, ('step', 'core'), 0, 0, tiled=True)  16.7 us
    all_to_all x1, blocking collectives, local(): everyone = lax.all_to_all(contrib, 'step', 0, 0, tiled=True)  15.1 us
    all_to_all x2, waiting for transfers between devices, local(): attended = lax.all_to_all(attended, CHIPS, 0, 0, tiled=True)  14.5 us
    unnamed x37, local copies, waits for them, and re-layouts  11.4 us
    all_to_all x1, blocking collectives, local(): lax.all_to_all(latents, CHIPS, 0, 0, tiled=True).reshape(-1, 2 * chans)  11.1 us
    all_to_all x2, starting transfers between devices, local(): attended = lax.all_to_all(attended, CHIPS, 0, 0, tiled=True)  10 us
    ppermute x11, waiting for transfers between devices, shift_steps(): lax.ppermute(values, 'step', [(i, (i + by) % steps) for i in range(steps)])  9.39 us
  transfers between devices with their start and end apart: 20, of which 7 were waited for; matrix products, arithmetic and copies ran while one was open for 0% of the time, Pallas kernels for 7%

profile of v6, /device:TPU:1, one launch (start us, length us, event | category | flops | bytes accessed | tf_op | source)
XLA Modules:
  0.0 180.4 jit_solution(16441276223172301769)
XLA Ops:
  6.5 1.1 convert_reduce_fusion
  7.7 1.1 fusion.2
  8.8 1.0 fusion.3
  9.8 1.4 copy.12
  11.3 0.3 copy.13
  11.7 1.1 pad_maximum_fusion
  12.8 0.8 copy.25
  13.6 0.1 pad_add_fusion.place_ref
  13.7 3.3 %fold.1 = (f32[16,112,128]{2,1,0:T(8,128)S(1)}, f32[16,112,128]{2,1,0:T(8,128)}, f32[64,64]{1,0:T(8,128)S(1)}) custom-call(s32[3]{0:T(128)S(1)} %pad_add_fusion.place_ref, f32[7,3072]{1,0:T(8,128)S(1)} %bitcast.61, bf16[64,3072]{1,0:T(8,128)(2,1)S(1)} %copy-done.2, bf16[48,96,128]{2,1,0:T(8,128)(2,1)S(1)} %bitcast.60), custom_call_target="tpu_custom_call" | custom-call | tf_op jit(solution)/shard_map/fold/pallas_call | solution.py:105
  17.1 3.2 %collective-permute-start = (f32[16,112,128]{2,1,0:T(8,128)}, f32[16,112,128]{2,1,0:T(8,128)}, u32[]{:S(2)}, u32[]{:S(2)}) collective-permute-start(f32[16,112,128]{2,1,0:T(8,128)} %get-tuple-element.28), channel_id=1, source_target_pairs={{0,1},{1,0},{2,3},{3,2},{4,5},{5,4},{6,7},{7,6},{8,9},{9,8},{10,11... | collective-permute-start | bytes 2752520 | tf_op jit(solution)/shard_map/ppermute | solution.py:33
  20.3 0.1 stack_reshape_squeeze.6
  20.5 5.8 %all-to-all-start = ((bf16[32,144,128]{2,1,0:T(8,128)(2,1)}), bf16[32,144,128]{2,1,0:T(8,128)(2,1)S(1)}, u32[]{:S(2)}, u32[]{:S(2)}) async-start(bf16[32,144,128]{2,1,0:T(8,128)(2,1)} %pad_maximum_fusion), calls=%async_computation | async-start | bytes 2359296 | tf_op jit(solution)/shard_map/all_to_all | solution.py:456
  26.4 1.7 collective-permute-start.2
  28.2 5.4 %collective-permute-done.2 = f32[1,2,3072]{2,1,0:T(2,128)S(1)} collective-permute-done((f32[1,2,3072]{2,1,0:T(2,128)S(1)}, f32[1,2,3072]{2,1,0:T(2,128)S(1)}, u32[]{:S(2)}, u32[]{:S(2)}) %collective-permute-start.2) | collective-permute-done | bytes 24608 | tf_op jit(solution)/shard_map/ppermute | solution.py:45
  33.6 0.1 collective-permute-start.3
  33.7 4.1 %collective-permute-start.4 = (f32[2,2,3072]{2,1,0:T(2,128)S(1)}, f32[2,2,3072]{2,1,0:T(2,128)S(1)}, u32[]{:S(2)}, u32[]{:S(2)}) collective-permute-start(f32[2,2,3072]{2,1,0:T(2,128)S(1)} %get-tuple-element.55), channel_id=1, source_target_pairs={{0,128},{32,160},{64,192},{96,224},{128,0},{160,32},{192,64},{224,... | collective-permute-start | bytes 147464 | tf_op jit(solution)/shard_map/ppermute | solution.py:45
  37.8 3.5 %collective-permute-start.5 = (f32[2,2,3072]{2,1,0:T(2,128)S(1)}, f32[2,2,3072]{2,1,0:T(2,128)S(1)}, u32[]{:S(2)}, u32[]{:S(2)}) collective-permute-start(f32[2,2,3072]{2,1,0:T(2,128)S(1)} %get-tuple-element.55), channel_id=1, source_target_pairs={{0,192},{32,224},{64,0},{96,32},{128,64},{160,96},{192,128},{224,1... | collective-permute-start | bytes 147464 | tf_op jit(solution)/shard_map/ppermute | solution.py:45
  41.3 0.7 collective-permute-done.4
  42.0 1.3 collective-permute-done.5
  43.3 2.2 %add_parts.1 = bf16[16,144,128]{2,1,0:T(8,128)(2,1)} custom-call(f32[16,112,128]{2,1,0:T(8,128)S(1)} %get-tuple-element.27.one_ref, f32[16,112,128]{2,1,0:T(8,128)} %collective-permute-done.other_ref, f32[32,128]{1,0:T(8,128)S(1)} %get-tuple-element.44.x_ref.start_ref), custom_call_target="tpu_custom_call" | custom-call | tf_op jit(solution)/shard_map/add_parts/pallas_call | solution.py:125
  45.5 3.7 %all-to-all-done.mine_ref = bf16[32,144,128]{2,1,0:T(8,128)(2,1)S(1)} async-done(((bf16[32,144,128]{2,1,0:T(8,128)(2,1)}), bf16[32,144,128]{2,1,0:T(8,128)(2,1)S(1)}, u32[]{:S(2)}, u32[]{:S(2)}) %all-to-all-start) | async-done | bytes 1179680 | tf_op jit(solution)/shard_map/all_to_all | solution.py:456
  49.2 1.2 collective-permute-start.6
  50.4 3.7 %all-to-all-start.1 = ((bf16[16,144,128]{2,1,0:T(8,128)(2,1)}), bf16[16,144,128]{2,1,0:T(8,128)(2,1)S(1)}, u32[]{:S(2)}, u32[]{:S(2)}) async-start(bf16[16,144,128]{2,1,0:T(8,128)(2,1)} %add_parts.1), calls=%async_computation.1 | async-start | bytes 1179648 | tf_op jit(solution)/shard_map/all_to_all | solution.py:468
  54.1 0.9 copy-done.5
  55.1 2.5 %text_pairs.1 = bf16[8,64,256]{2,1,0:T(8,128)(2,1)S(1)} custom-call(s32[3]{0:T(128)S(1)} %pad_add_fusion.place_ref, bf16[32,144,128]{2,1,0:T(8,128)(2,1)S(1)} %all-to-all-done.mine_ref, bf16[32,144,128]{2,1,0:T(8,128)(2,1)S(1)} %collective-permute-done.6.other_ref, f32[8,2,3072]{2,1,0:T(2,128)S(1)} %copy-done.5, f32[3,128]{1,0:T(4,128)S(1)} %copy-done.6), custom_call_target="tpu_custom_call" | custom-call | tf_op jit(solution)/shard_map/text_pairs/pallas_call | solution.py:195
  57.6 6.9 %collective-permute-start.7 = (bf16[64,256]{1,0:T(8,128)(2,1)S(1)}, bf16[64,256]{1,0:T(8,128)(2,1)S(1)}, u32[]{:S(2)}, u32[]{:S(2)}) collective-permute-start(bf16[64,256]{1,0:T(8,128)(2,1)S(1)} %get-tuple-element.51), channel_id=1, source_target_pairs={{0,224},{32,0},{64,32},{96,64},{128,96},{160,128},{192,160},{224,1... | collective-permute-start | bytes 98312 | tf_op jit(solution)/shard_map/ppermute | solution.py:45
  64.5 1.9 %collective-permute-start.9 = (bf16[64,256]{1,0:T(8,128)(2,1)S(1)}, bf16[64,256]{1,0:T(8,128)(2,1)S(1)}, u32[]{:S(2)}, u32[]{:S(2)}) collective-permute-start(bf16[64,256]{1,0:T(8,128)(2,1)S(1)} %get-tuple-element.49), channel_id=1, source_target_pairs={{0,192},{32,224},{64,0},{96,32},{128,64},{160,96},{192,128},{224,1... | collective-permute-start | bytes 98312 | tf_op jit(solution)/shard_map/ppermute | solution.py:45
  66.4 0.4 collective-permute-start.11
  66.9 2.4 %collective-permute-start.12 = (bf16[64,256]{1,0:T(8,128)(2,1)S(1)}, bf16[64,256]{1,0:T(8,128)(2,1)S(1)}, u32[]{:S(2)}, u32[]{:S(2)}) collective-permute-start(bf16[64,256]{1,0:T(8,128)(2,1)S(1)} %get-tuple-element.47), channel_id=1, source_target_pairs={{0,160},{32,192},{64,224},{96,0},{128,32},{160,64},{192,96},{224,1... | collective-permute-start | bytes 98312 | tf_op jit(solution)/shard_map/ppermute | solution.py:45
  69.3 0.9 collective-permute-start.13
  70.1 3.6 %collective-permute-start.14 = (bf16[64,256]{1,0:T(8,128)(2,1)S(1)}, bf16[64,256]{1,0:T(8,128)(2,1)S(1)}, u32[]{:S(2)}, u32[]{:S(2)}) collective-permute-start(bf16[64,256]{1,0:T(8,128)(2,1)S(1)} %get-tuple-element.45), channel_id=1, source_target_pairs={{0,128},{32,160},{64,192},{96,224},{128,0},{160,32},{192,64},{224,... | collective-permute-start | bytes 98312 | tf_op jit(solution)/shard_map/ppermute | solution.py:45
  73.8 1.8 %collective-permute-start.10 = (f32[112,128]{1,0:T(8,128)S(1)}, f32[112,128]{1,0:T(8,128)S(1)}, u32[]{:S(2)}, u32[]{:S(2)}) collective-permute-start(f32[112,128]{1,0:T(8,128)S(1)} %get-tuple-element.35.mine_ref), channel_id=1, source_target_pairs={{0,1},{1,0},{2,3},{3,2},{4,5},{5,4},{6,7},{7,6},{8,9},{9,8},{10,11... | collective-permute-start | bytes 172040 | tf_op jit(solution)/shard_map/ppermute | solution.py:33
  75.8 2.0 %collective-permute-done.14 = bf16[64,256]{1,0:T(8,128)(2,1)S(1)} collective-permute-done((bf16[64,256]{1,0:T(8,128)(2,1)S(1)}, bf16[64,256]{1,0:T(8,128)(2,1)S(1)}, u32[]{:S(2)}, u32[]{:S(2)}) %collective-permute-start.14) | collective-permute-done | bytes 32800 | tf_op jit(solution)/shard_map/ppermute | solution.py:45
  77.8 3.9 %attention.2 = bf16[16,64,128]{2,1,0:T(8,128)(2,1)} custom-call(s32[3]{0:T(128)S(1)} %pad_add_fusion.place_ref, bf16[512,128]{1,0:T(8,128)(2,1)S(1)} %bitcast.68, f32[112,128]{1,0:T(8,128)S(1)} %get-tuple-element.35.mine_ref, f32[112,128]{1,0:T(8,128)S(1)} %collective-permute-done.10.theirs_ref, f32[64,64]{1,0:T(8,128)S(1)} %get-tuple-element.36.gram_ref, ...), custom_call_target="tpu_custom_call" | custom-call | flops 805306368 | bytes 2097152 | tf_op jit(solution)/shard_map/attention/pallas_call | solution.py:273
  81.7 6.5 %all-to-all-start.2 = ((bf16[16,64,128]{2,1,0:T(8,128)(2,1)}), bf16[16,64,128]{2,1,0:T(8,128)(2,1)S(1)}, u32[]{:S(2)}, u32[]{:S(2)}) async-start(bf16[16,64,128]{2,1,0:T(8,128)(2,1)} %attention.2), calls=%async_computation.2 | async-start | bytes 524288 | tf_op jit(solution)/shard_map/all_to_all | solution.py:486
  88.8 7.0 %all-to-all-done.2.attended_ref = bf16[16,64,128]{2,1,0:T(8,128)(2,1)S(1)} async-done(((bf16[16,64,128]{2,1,0:T(8,128)(2,1)}), bf16[16,64,128]{2,1,0:T(8,128)(2,1)S(1)}, u32[]{:S(2)}, u32[]{:S(2)}) %all-to-all-start.2) | async-done | bytes 262176 | tf_op jit(solution)/shard_map/all_to_all | solution.py:486
  95.9 4.6 %copy-done = bf16[3072,2048]{1,0:T(8,128)(2,1)S(1)} copy-done((bf16[3072,2048]{1,0:T(8,128)(2,1)S(1)}, bf16[3072,2048]{1,0:T(8,128)(2,1)}, u32[]{:S(2)}) %copy-start) | copy-done | bytes 12582936
  100.4 4.4 %output_stage.2 = f32[8,32,128]{2,1,0:T(8,128)S(1)} custom-call(bf16[16,64,128]{2,1,0:T(8,128)(2,1)S(1)} %all-to-all-done.2.attended_ref, bf16[3072,2048]{1,0:T(8,128)(2,1)S(1)} %copy-done, bf16[32,128]{1,0:T(8,128)(2,1)S(1)} %convert_element_type.11.x_ref, bf16[64,3072]{1,0:T(8,128)(2,1)S(1)} %copy-done.2, f32[7,3072]{1,0:T(8,128)S(1)} %bitcast.62, ...), custom_call_target="tpu_custom_call" | custom-call | flops 805306368 | bytes 12582912 | tf_op jit(solution)/shard_map/output_stage/pallas_call | solution.py:334
  104.9 15.1 %all_to_all.35.everyone_ref = f32[8,32,128]{2,1,0:T(8,128)S(1)} all-to-all(f32[8,32,128]{2,1,0:T(8,128)S(1)} %output_stage.2), channel_id=1, replica_groups=mesh['step'=8,'y'=4,'x'=4,'core'=2] {'step'}, dimensions={0} | all-to-all | bytes 262144 | tf_op jit(solution)/shard_map/all_to_all | solution.py:491
  120.0 0.6 scan.1
  120.5 11.1 %all_to_all.36 = bf16[16,32,128]{2,1,0:T(8,128)(2,1)S(1)} all-to-all(bf16[16,32,128]{2,1,0:T(8,128)(2,1)S(1)} %scan.1), channel_id=1, replica_groups=mesh['step'=8,'y'=4,'x'=4,'core'=2] {'y','x'}, dimensions={0} | all-to-all | bytes 262144 | tf_op jit(solution)/shard_map/all_to_all | solution.py:494
  131.6 3.9 %attention.3 = bf16[16,64,128]{2,1,0:T(8,128)(2,1)} custom-call(s32[3]{0:T(128)S(1)} %pad_add_fusion.place_ref, bf16[512,128]{1,0:T(8,128)(2,1)S(1)} %bitcast.67, f32[112,128]{1,0:T(8,128)S(1)} %get-tuple-element.35.mine_ref, f32[112,128]{1,0:T(8,128)S(1)} %collective-permute-done.10.theirs_ref, f32[64,64]{1,0:T(8,128)S(1)} %get-tuple-element.36.gram_ref, ...), custom_call_target="tpu_custom_call" | custom-call | flops 805306368 | bytes 2097152 | tf_op jit(solution)/shard_map/attention/pallas_call | solution.py:273
  135.5 3.5 %all-to-all-start.5 = ((bf16[16,64,128]{2,1,0:T(8,128)(2,1)}), bf16[16,64,128]{2,1,0:T(8,128)(2,1)S(1)}, u32[]{:S(2)}, u32[]{:S(2)}) async-start(bf16[16,64,128]{2,1,0:T(8,128)(2,1)} %attention.3), calls=%async_computation.5 | async-start | bytes 524288 | tf_op jit(solution)/shard_map/all_to_all | solution.py:486
  139.1 7.5 %all-to-all-done.5.attended_ref = bf16[16,64,128]{2,1,0:T(8,128)(2,1)S(1)} async-done(((bf16[16,64,128]{2,1,0:T(8,128)(2,1)}), bf16[16,64,128]{2,1,0:T(8,128)(2,1)S(1)}, u32[]{:S(2)}, u32[]{:S(2)}) %all-to-all-start.5) | async-done | bytes 262176 | tf_op jit(solution)/shard_map/all_to_all | solution.py:486
  146.6 4.6 %copy-done.1 = bf16[3072,2048]{1,0:T(8,128)(2,1)S(1)} copy-done((bf16[3072,2048]{1,0:T(8,128)(2,1)S(1)}, bf16[3072,2048]{1,0:T(8,128)(2,1)}, u32[]{:S(2)}) %copy-start.1) | copy-done | bytes 12582936
  151.1 4.4 %output_stage.3 = f32[8,32,128]{2,1,0:T(8,128)S(1)} custom-call(bf16[16,64,128]{2,1,0:T(8,128)(2,1)S(1)} %all-to-all-done.5.attended_ref, bf16[3072,2048]{1,0:T(8,128)(2,1)S(1)} %copy-done.1, bf16[32,128]{1,0:T(8,128)(2,1)S(1)} %slice_bitcast_fusion.8.x_ref, bf16[64,3072]{1,0:T(8,128)(2,1)S(1)} %copy-done.2, f32[7,3072]{1,0:T(8,128)S(1)} %bitcast.63, ...), custom_call_target="tpu_custom_call" | custom-call | flops 805306368 | bytes 12582912 | tf_op jit(solution)/shard_map/output_stage/pallas_call | solution.py:334
  155.6 16.7 %all_to_all.37.everyone_ref = f32[16,16,128]{2,1,0:T(8,128)S(1)} all-to-all(f32[16,16,128]{2,1,0:T(8,128)S(1)} %bitcast.66), channel_id=1, replica_groups=mesh['step'=8,'y'=4,'x'=4,'core'=2] {'step','core'}, dimensions={0} | all-to-all | bytes 262144 | tf_op jit(solution)/shard_map/all_to_all | solution.py:496
  172.3 1.2 total_rows.1
  (66 shorter events, 0.6 us)
Async XLA Ops:
  6.5 4.7 %copy-start.9 = (f32[1,7,3072]{2,0,1:T(1,128)S(1)}, f32[1,7,3072]{2,0,1:T(1,128)}, u32[]{:S(2)}) copy-start(f32[1,7,3072]{2,0,1:T(1,128)} %param.14) | copy-start | bytes 258052
  6.5 4.7 %copy-start.7 = (bf16[96,3,16,128]{3,2,1,0:T(8,128)(2,1)S(1)}, bf16[96,3,16,128]{3,2,1,0:T(8,128)(2,1)}, u32[]{:S(2)}) copy-start(bf16[96,3,16,128]{3,2,1,0:T(8,128)(2,1)} %param.17) | copy-start | bytes 3538948
  6.5 89.3 %all-gather.2.cloned.1.call-start = ((), (), s32[]{:S(2)}) async-start(), calls=%async_computation.7 | async-start | bytes 12976128 | tf_op jit(solution)/shard_map/all_gather | solution.py:455
  11.6 1.1 copy-start.8
  12.7 1.0 copy-start.2
  13.6 6.7 %copy-start.10 = (f32[1,2,32,64]{3,2,1,0:T(8,128)S(1)}, f32[1,2,32,64]{3,2,1,0:T(8,128)}, u32[]{:S(2)}) copy-start(f32[1,2,32,64]{3,2,1,0:T(8,128)} %param.12) | copy-start | bytes 49156
  13.6 6.8 %copy-start.11 = (f32[1,2,32,64]{3,2,1,0:T(8,128)S(1)}, f32[1,2,32,64]{3,2,1,0:T(8,128)}, u32[]{:S(2)}) copy-start(f32[1,2,32,64]{3,2,1,0:T(8,128)} %param.11) | copy-start | bytes 49156
  17.1 26.2 %collective-permute-start = (f32[16,112,128]{2,1,0:T(8,128)}, f32[16,112,128]{2,1,0:T(8,128)}, u32[]{:S(2)}, u32[]{:S(2)}) collective-permute-start(f32[16,112,128]{2,1,0:T(8,128)} %get-tuple-element.28), channel_id=1, source_target_pairs={{0,1},{1,0},{2,3},{3,2},{4,5},{5,4},{6,7},{7,6},{8,9},{9,8},{10,11... | collective-permute-start | bytes 2752520 | tf_op jit(solution)/shard_map/ppermute | solution.py:33
  20.5 5.9 %slice-start = ((f32[1,7,3072]{2,0,1:T(1,128)}), f32[1,2,3072]{2,0,1:T(1,128)S(1)}, s32[]{:S(2)}) async-start(f32[1,7,3072]{2,0,1:T(1,128)} %param.14), calls=%async_computation.8 | async-start | bytes 49152 | tf_op jit(solution)/shard_map/slice | solution.py:434
  20.5 7.7 %collective-permute-start.1 = (f32[2,16,128]{2,1,0:T(8,128)S(1)}, f32[2,16,128]{2,1,0:T(8,128)S(1)}, u32[]{:S(2)}, u32[]{:S(2)}) collective-permute-start(f32[2,16,128]{2,1,0:T(8,128)S(1)} %fusion.7), channel_id=1, source_target_pairs={{0,1},{1,0},{2,3},{3,2},{4,5},{5,4},{6,7},{7,6},{8,9},{9,8},{10,11... | collective-permute-start | bytes 49160 | tf_op jit(solution)/shard_map/ppermute | solution.py:33
  20.5 28.7 %all-to-all-start = ((bf16[32,144,128]{2,1,0:T(8,128)(2,1)}), bf16[32,144,128]{2,1,0:T(8,128)(2,1)S(1)}, u32[]{:S(2)}, u32[]{:S(2)}) async-start(bf16[32,144,128]{2,1,0:T(8,128)(2,1)} %pad_maximum_fusion), calls=%async_computation | async-start | bytes 2359296 | tf_op jit(solution)/shard_map/all_to_all | solution.py:456
  26.4 7.2 %collective-permute-start.2 = (f32[1,2,3072]{2,1,0:T(2,128)S(1)}, f32[1,2,3072]{2,1,0:T(2,128)S(1)}, u32[]{:S(2)}, u32[]{:S(2)}) collective-permute-start(f32[1,2,3072]{2,1,0:T(2,128)S(1)} %get-tuple-element.59), channel_id=1, source_target_pairs={{0,32},{32,64},{64,96},{96,128},{128,160},{160,192},{192,224},{224... | collective-permute-start | bytes 73736 | tf_op jit(solution)/shard_map/ppermute | solution.py:45
  33.6 7.7 %collective-permute-start.3 = (f32[2,2,3072]{2,1,0:T(2,128)S(1)}, f32[2,2,3072]{2,1,0:T(2,128)S(1)}, u32[]{:S(2)}, u32[]{:S(2)}) collective-permute-start(f32[2,2,3072]{2,1,0:T(2,128)S(1)} %get-tuple-element.55), channel_id=1, source_target_pairs={{0,64},{32,96},{64,128},{96,160},{128,192},{160,224},{192,0},{224,... | collective-permute-start | bytes 147464 | tf_op jit(solution)/shard_map/ppermute | solution.py:45
  33.7 8.2 %collective-permute-start.4 = (f32[2,2,3072]{2,1,0:T(2,128)S(1)}, f32[2,2,3072]{2,1,0:T(2,128)S(1)}, u32[]{:S(2)}, u32[]{:S(2)}) collective-permute-start(f32[2,2,3072]{2,1,0:T(2,128)S(1)} %get-tuple-element.55), channel_id=1, source_target_pairs={{0,128},{32,160},{64,192},{96,224},{128,0},{160,32},{192,64},{224,... | collective-permute-start | bytes 147464 | tf_op jit(solution)/shard_map/ppermute | solution.py:45
  37.8 5.4 %collective-permute-start.5 = (f32[2,2,3072]{2,1,0:T(2,128)S(1)}, f32[2,2,3072]{2,1,0:T(2,128)S(1)}, u32[]{:S(2)}, u32[]{:S(2)}) collective-permute-start(f32[2,2,3072]{2,1,0:T(2,128)S(1)} %get-tuple-element.55), channel_id=1, source_target_pairs={{0,192},{32,224},{64,0},{96,32},{128,64},{160,96},{192,128},{224,1... | collective-permute-start | bytes 147464 | tf_op jit(solution)/shard_map/ppermute | solution.py:45
  43.3 2.2 %copy-start.4 = (f32[8,2,3072]{2,1,0:T(2,128)}, f32[8,2,3072]{2,1,0:T(2,128)S(1)}, u32[]{:S(2)}) copy-start(f32[8,2,3072]{2,1,0:T(2,128)S(1)} %constant_dynamic-update-slice_fusion.2.mods_ref) | copy-start | bytes 589828
  45.5 8.6 %copy-start.6 = (f32[3,128]{1,0:T(4,128)S(1)}, f32[3,128]{1,0:T(4,128)}, u32[]{:S(2)}) copy-start(f32[3,128]{1,0:T(4,128)} %gains_ref.5) | copy-start | bytes 4612
  49.2 4.9 %collective-permute-start.6 = (bf16[32,144,128]{2,1,0:T(8,128)(2,1)S(1)}, bf16[32,144,128]{2,1,0:T(8,128)(2,1)S(1)}, u32[]{:S(2)}, u32[]{:S(2)}) collective-permute-start(bf16[32,144,128]{2,1,0:T(8,128)(2,1)S(1)} %all-to-all-done.mine_ref), channel_id=1, source_target_pairs={{0,1},{1,0},{2,3},{3,2},{4,5},{5,4},{6,7},{7,6},{8,9},{9,8},{10,11... | collective-permute-start | bytes 3538952 | tf_op jit(solution)/shard_map/ppermute | solution.py:33
  50.4 23.3 %all-to-all-start.1 = ((bf16[16,144,128]{2,1,0:T(8,128)(2,1)}), bf16[16,144,128]{2,1,0:T(8,128)(2,1)S(1)}, u32[]{:S(2)}, u32[]{:S(2)}) async-start(bf16[16,144,128]{2,1,0:T(8,128)(2,1)} %add_parts.1), calls=%async_computation.1 | async-start | bytes 1179648 | tf_op jit(solution)/shard_map/all_to_all | solution.py:468
  54.1 0.9 copy-start.5
  57.6 11.6 %collective-permute-start.7 = (bf16[64,256]{1,0:T(8,128)(2,1)S(1)}, bf16[64,256]{1,0:T(8,128)(2,1)S(1)}, u32[]{:S(2)}, u32[]{:S(2)}) collective-permute-start(bf16[64,256]{1,0:T(8,128)(2,1)S(1)} %get-tuple-element.51), channel_id=1, source_target_pairs={{0,224},{32,0},{64,32},{96,64},{128,96},{160,128},{192,160},{224,1... | collective-permute-start | bytes 98312 | tf_op jit(solution)/shard_map/ppermute | solution.py:45
  64.5 5.6 %collective-permute-start.8 = (bf16[64,256]{1,0:T(8,128)(2,1)S(1)}, bf16[64,256]{1,0:T(8,128)(2,1)S(1)}, u32[]{:S(2)}, u32[]{:S(2)}) collective-permute-start(bf16[64,256]{1,0:T(8,128)(2,1)S(1)} %get-tuple-element.50), channel_id=1, source_target_pairs={{0,32},{32,64},{64,96},{96,128},{128,160},{160,192},{192,224},{224... | collective-permute-start | bytes 98312 | tf_op jit(solution)/shard_map/ppermute | solution.py:45
  64.5 9.2 %collective-permute-start.9 = (bf16[64,256]{1,0:T(8,128)(2,1)S(1)}, bf16[64,256]{1,0:T(8,128)(2,1)S(1)}, u32[]{:S(2)}, u32[]{:S(2)}) collective-permute-start(bf16[64,256]{1,0:T(8,128)(2,1)S(1)} %get-tuple-element.49), channel_id=1, source_target_pairs={{0,192},{32,224},{64,0},{96,32},{128,64},{160,96},{192,128},{224,1... | collective-permute-start | bytes 98312 | tf_op jit(solution)/shard_map/ppermute | solution.py:45
  66.4 9.3 %collective-permute-start.11 = (bf16[64,256]{1,0:T(8,128)(2,1)S(1)}, bf16[64,256]{1,0:T(8,128)(2,1)S(1)}, u32[]{:S(2)}, u32[]{:S(2)}) collective-permute-start(bf16[64,256]{1,0:T(8,128)(2,1)S(1)} %get-tuple-element.48), channel_id=1, source_target_pairs={{0,64},{32,96},{64,128},{96,160},{128,192},{160,224},{192,0},{224,... | collective-permute-start | bytes 98312 | tf_op jit(solution)/shard_map/ppermute | solution.py:45
  66.9 8.8 %collective-permute-start.12 = (bf16[64,256]{1,0:T(8,128)(2,1)S(1)}, bf16[64,256]{1,0:T(8,128)(2,1)S(1)}, u32[]{:S(2)}, u32[]{:S(2)}) collective-permute-start(bf16[64,256]{1,0:T(8,128)(2,1)S(1)} %get-tuple-element.47), channel_id=1, source_target_pairs={{0,160},{32,192},{64,224},{96,0},{128,32},{160,64},{192,96},{224,1... | collective-permute-start | bytes 98312 | tf_op jit(solution)/shard_map/ppermute | solution.py:45
  69.3 6.5 %collective-permute-start.13 = (bf16[64,256]{1,0:T(8,128)(2,1)S(1)}, bf16[64,256]{1,0:T(8,128)(2,1)S(1)}, u32[]{:S(2)}, u32[]{:S(2)}) collective-permute-start(bf16[64,256]{1,0:T(8,128)(2,1)S(1)} %get-tuple-element.46), channel_id=1, source_target_pairs={{0,96},{32,128},{64,160},{96,192},{128,224},{160,0},{192,32},{224,... | collective-permute-start | bytes 98312 | tf_op jit(solution)/shard_map/ppermute | solution.py:45
  70.1 7.6 %collective-permute-start.14 = (bf16[64,256]{1,0:T(8,128)(2,1)S(1)}, bf16[64,256]{1,0:T(8,128)(2,1)S(1)}, u32[]{:S(2)}, u32[]{:S(2)}) collective-permute-start(bf16[64,256]{1,0:T(8,128)(2,1)S(1)} %get-tuple-element.45), channel_id=1, source_target_pairs={{0,128},{32,160},{64,192},{96,224},{128,0},{160,32},{192,64},{224,... | collective-permute-start | bytes 98312 | tf_op jit(solution)/shard_map/ppermute | solution.py:45
  73.8 3.9 %collective-permute-start.10 = (f32[112,128]{1,0:T(8,128)S(1)}, f32[112,128]{1,0:T(8,128)S(1)}, u32[]{:S(2)}, u32[]{:S(2)}) collective-permute-start(f32[112,128]{1,0:T(8,128)S(1)} %get-tuple-element.35.mine_ref), channel_id=1, source_target_pairs={{0,1},{1,0},{2,3},{3,2},{4,5},{5,4},{6,7},{7,6},{8,9},{9,8},{10,11... | collective-permute-start | bytes 172040 | tf_op jit(solution)/shard_map/ppermute | solution.py:33
  77.8 18.1 %copy-start.3 = (bf16[3072,64]{0,1:T(8,128)(2,1)S(1)}, bf16[3072,64]{0,1:T(8,128)(2,1)}, u32[]{:S(2)}) copy-start(bf16[3072,64]{0,1:T(8,128)(2,1)} %param.21) | copy-start | bytes 1179652
  81.7 14.2 %all-to-all-start.2 = ((bf16[16,64,128]{2,1,0:T(8,128)(2,1)}), bf16[16,64,128]{2,1,0:T(8,128)(2,1)S(1)}, u32[]{:S(2)}, u32[]{:S(2)}) async-start(bf16[16,64,128]{2,1,0:T(8,128)(2,1)} %attention.2), calls=%async_computation.2 | async-start | bytes 524288 | tf_op jit(solution)/shard_map/all_to_all | solution.py:486
  95.9 4.6 %copy-start = (bf16[3072,2048]{1,0:T(8,128)(2,1)S(1)}, bf16[3072,2048]{1,0:T(8,128)(2,1)}, u32[]{:S(2)}) copy-start(bf16[3072,2048]{1,0:T(8,128)(2,1)} %all-gather.2.cloned.1.call-done.w_out_ref) | copy-start | bytes 37748740
  135.5 11.0 %all-to-all-start.5 = ((bf16[16,64,128]{2,1,0:T(8,128)(2,1)}), bf16[16,64,128]{2,1,0:T(8,128)(2,1)S(1)}, u32[]{:S(2)}, u32[]{:S(2)}) async-start(bf16[16,64,128]{2,1,0:T(8,128)(2,1)} %attention.3), calls=%async_computation.5 | async-start | bytes 524288 | tf_op jit(solution)/shard_map/all_to_all | solution.py:486
  146.6 4.6 %copy-start.1 = (bf16[3072,2048]{1,0:T(8,128)(2,1)S(1)}, bf16[3072,2048]{1,0:T(8,128)(2,1)}, u32[]{:S(2)}) copy-start(bf16[3072,2048]{1,0:T(8,128)(2,1)} %all-gather.2.cloned.1.call-done.w_out_ref) | copy-start | bytes 37748740
Sparse Core Ops, SparseCore 0:
  13.7 80.2 all-gather.1

commit v7 on v6

--- a/solution.py
+++ b/solution.py
@@ -107,7 +107,7 @@
         in_specs=[pl.BlockSpec(memory_space=pltpu.SMEM)]
         + [pl.BlockSpec(memory_space=pltpu.VMEM)] * 3,
         out_shape=(sent, sent, jax.ShapeDtypeStruct((chans, chans), F32)),
-        compiler_params=pltpu.CompilerParams(vmem_limit_bytes=24 * MIB),
+        compiler_params=pltpu.CompilerParams(vmem_limit_bytes=16 * MIB),
         cost_estimate=FREE,
         name="fold",
     )(place, shifts, w_latent, columns)
@@ -201,7 +201,7 @@
             pltpu.VMEM((sources, tokens // sources * (width // hd), hd), F32),
             pltpu.VMEM((steps * tokens, width), BF16),
         ],
-        compiler_params=pltpu.CompilerParams(vmem_limit_bytes=24 * MIB),
+        compiler_params=pltpu.CompilerParams(vmem_limit_bytes=16 * MIB),
         cost_estimate=FREE,
         name="text_pairs",
     )(place, mine, other, mods, gains)

time: 181 us -> 181 us (level)
  no operation moved by 1% of the time
where the time goes in v7:
time: 181 us; the launch traced here: 180 us
  starting transfers between devices  51.4 us (28%)
  blocking collectives  42.9 us (24%)
  waiting for transfers between devices  27.7 us (15%)
  Pallas kernels  26.6 us (15%)
  between operations  14.4 us (8%)
  local copies, waits for them, and re-layouts  13.1 us (7%)
  other arithmetic  4.4 us (2%)
    ppermute x11, starting transfers between devices, shift_steps(): lax.ppermute(values, 'step', [(i, (i + by) % steps) for i in range(steps)])  25.5 us
    all_to_all x1, blocking collectives, local(): everyone = lax.all_to_all(contrib, ('step', 'core'), 0, 0, tiled=True)  16.7 us
    all_to_all x1, blocking collectives, local(): everyone = lax.all_to_all(contrib, 'step', 0, 0, tiled=True)  15.1 us
    all_to_all x2, waiting for transfers between devices, local(): attended = lax.all_to_all(attended, CHIPS, 0, 0, tiled=True)  14.5 us
    unnamed x37, local copies, waits for them, and re-layouts  11.4 us
    all_to_all x1, blocking collectives, local(): lax.all_to_all(latents, CHIPS, 0, 0, tiled=True).reshape(-1, 2 * chans)  11.1 us
    all_to_all x2, starting transfers between devices, local(): attended = lax.all_to_all(attended, CHIPS, 0, 0, tiled=True)  10 us
    ppermute x11, waiting for transfers between devices, shift_steps(): lax.ppermute(values, 'step', [(i, (i + by) % steps) for i in range(steps)])  9.39 us
  transfers between devices with their start and end apart: 20, of which 7 were waited for; matrix products, arithmetic and copies ran while one was open for 0% of the time, Pallas kernels for 7%

profile of v7, /device:TPU:1, one launch (start us, length us, event | category | flops | bytes accessed | tf_op | source)
XLA Modules:
  0.0 180.4 jit_solution(18230127628193344073)
XLA Ops:
  6.5 1.1 convert_reduce_fusion
  7.7 1.1 fusion.2
  8.8 1.0 fusion.3
  9.8 1.4 copy.12
  11.3 0.3 copy.13
  11.7 1.1 pad_maximum_fusion
  12.8 0.8 copy.25
  13.6 0.1 pad_add_fusion.place_ref
  13.7 3.3 %fold.1 = (f32[16,112,128]{2,1,0:T(8,128)S(1)}, f32[16,112,128]{2,1,0:T(8,128)}, f32[64,64]{1,0:T(8,128)S(1)}) custom-call(s32[3]{0:T(128)S(1)} %pad_add_fusion.place_ref, f32[7,3072]{1,0:T(8,128)S(1)} %bitcast.61, bf16[64,3072]{1,0:T(8,128)(2,1)S(1)} %copy-done.2, bf16[48,96,128]{2,1,0:T(8,128)(2,1)S(1)} %bitcast.60), custom_call_target="tpu_custom_call" | custom-call | tf_op jit(solution)/shard_map/fold/pallas_call | solution.py:105
  17.1 3.2 %collective-permute-start = (f32[16,112,128]{2,1,0:T(8,128)}, f32[16,112,128]{2,1,0:T(8,128)}, u32[]{:S(2)}, u32[]{:S(2)}) collective-permute-start(f32[16,112,128]{2,1,0:T(8,128)} %get-tuple-element.28), channel_id=1, source_target_pairs={{0,1},{1,0},{2,3},{3,2},{4,5},{5,4},{6,7},{7,6},{8,9},{9,8},{10,11... | collective-permute-start | bytes 2752520 | tf_op jit(solution)/shard_map/ppermute | solution.py:33
  20.3 0.1 stack_reshape_squeeze.6
  20.5 5.8 %all-to-all-start = ((bf16[32,144,128]{2,1,0:T(8,128)(2,1)}), bf16[32,144,128]{2,1,0:T(8,128)(2,1)S(1)}, u32[]{:S(2)}, u32[]{:S(2)}) async-start(bf16[32,144,128]{2,1,0:T(8,128)(2,1)} %pad_maximum_fusion), calls=%async_computation | async-start | bytes 2359296 | tf_op jit(solution)/shard_map/all_to_all | solution.py:456
  26.4 1.7 collective-permute-start.2
  28.2 5.4 %collective-permute-done.2 = f32[1,2,3072]{2,1,0:T(2,128)S(1)} collective-permute-done((f32[1,2,3072]{2,1,0:T(2,128)S(1)}, f32[1,2,3072]{2,1,0:T(2,128)S(1)}, u32[]{:S(2)}, u32[]{:S(2)}) %collective-permute-start.2) | collective-permute-done | bytes 24608 | tf_op jit(solution)/shard_map/ppermute | solution.py:45
  33.6 0.1 collective-permute-start.3
  33.7 4.1 %collective-permute-start.4 = (f32[2,2,3072]{2,1,0:T(2,128)S(1)}, f32[2,2,3072]{2,1,0:T(2,128)S(1)}, u32[]{:S(2)}, u32[]{:S(2)}) collective-permute-start(f32[2,2,3072]{2,1,0:T(2,128)S(1)} %get-tuple-element.55), channel_id=1, source_target_pairs={{0,128},{32,160},{64,192},{96,224},{128,0},{160,32},{192,64},{224,... | collective-permute-start | bytes 147464 | tf_op jit(solution)/shard_map/ppermute | solution.py:45
  37.8 3.5 %collective-permute-start.5 = (f32[2,2,3072]{2,1,0:T(2,128)S(1)}, f32[2,2,3072]{2,1,0:T(2,128)S(1)}, u32[]{:S(2)}, u32[]{:S(2)}) collective-permute-start(f32[2,2,3072]{2,1,0:T(2,128)S(1)} %get-tuple-element.55), channel_id=1, source_target_pairs={{0,192},{32,224},{64,0},{96,32},{128,64},{160,96},{192,128},{224,1... | collective-permute-start | bytes 147464 | tf_op jit(solution)/shard_map/ppermute | solution.py:45
  41.3 0.7 collective-permute-done.4
  42.0 1.3 collective-permute-done.5
  43.3 2.2 %add_parts.1 = bf16[16,144,128]{2,1,0:T(8,128)(2,1)} custom-call(f32[16,112,128]{2,1,0:T(8,128)S(1)} %get-tuple-element.27.one_ref, f32[16,112,128]{2,1,0:T(8,128)} %collective-permute-done.other_ref, f32[32,128]{1,0:T(8,128)S(1)} %get-tuple-element.44.x_ref.start_ref), custom_call_target="tpu_custom_call" | custom-call | tf_op jit(solution)/shard_map/add_parts/pallas_call | solution.py:125
  45.5 3.7 %all-to-all-done.mine_ref = bf16[32,144,128]{2,1,0:T(8,128)(2,1)S(1)} async-done(((bf16[32,144,128]{2,1,0:T(8,128)(2,1)}), bf16[32,144,128]{2,1,0:T(8,128)(2,1)S(1)}, u32[]{:S(2)}, u32[]{:S(2)}) %all-to-all-start) | async-done | bytes 1179680 | tf_op jit(solution)/shard_map/all_to_all | solution.py:456
  49.2 1.2 collective-permute-start.6
  50.4 3.7 %all-to-all-start.1 = ((bf16[16,144,128]{2,1,0:T(8,128)(2,1)}), bf16[16,144,128]{2,1,0:T(8,128)(2,1)S(1)}, u32[]{:S(2)}, u32[]{:S(2)}) async-start(bf16[16,144,128]{2,1,0:T(8,128)(2,1)} %add_parts.1), calls=%async_computation.1 | async-start | bytes 1179648 | tf_op jit(solution)/shard_map/all_to_all | solution.py:468
  54.1 0.9 copy-done.5
  55.1 2.5 %text_pairs.1 = bf16[8,64,256]{2,1,0:T(8,128)(2,1)S(1)} custom-call(s32[3]{0:T(128)S(1)} %pad_add_fusion.place_ref, bf16[32,144,128]{2,1,0:T(8,128)(2,1)S(1)} %all-to-all-done.mine_ref, bf16[32,144,128]{2,1,0:T(8,128)(2,1)S(1)} %collective-permute-done.6.other_ref, f32[8,2,3072]{2,1,0:T(2,128)S(1)} %copy-done.5, f32[3,128]{1,0:T(4,128)S(1)} %copy-done.6), custom_call_target="tpu_custom_call" | custom-call | tf_op jit(solution)/shard_map/text_pairs/pallas_call | solution.py:195
  57.6 6.9 %collective-permute-start.7 = (bf16[64,256]{1,0:T(8,128)(2,1)S(1)}, bf16[64,256]{1,0:T(8,128)(2,1)S(1)}, u32[]{:S(2)}, u32[]{:S(2)}) collective-permute-start(bf16[64,256]{1,0:T(8,128)(2,1)S(1)} %get-tuple-element.51), channel_id=1, source_target_pairs={{0,224},{32,0},{64,32},{96,64},{128,96},{160,128},{192,160},{224,1... | collective-permute-start | bytes 98312 | tf_op jit(solution)/shard_map/ppermute | solution.py:45
  64.5 1.9 %collective-permute-start.9 = (bf16[64,256]{1,0:T(8,128)(2,1)S(1)}, bf16[64,256]{1,0:T(8,128)(2,1)S(1)}, u32[]{:S(2)}, u32[]{:S(2)}) collective-permute-start(bf16[64,256]{1,0:T(8,128)(2,1)S(1)} %get-tuple-element.49), channel_id=1, source_target_pairs={{0,192},{32,224},{64,0},{96,32},{128,64},{160,96},{192,128},{224,1... | collective-permute-start | bytes 98312 | tf_op jit(solution)/shard_map/ppermute | solution.py:45
  66.4 0.4 collective-permute-start.11
  66.9 2.4 %collective-permute-start.12 = (bf16[64,256]{1,0:T(8,128)(2,1)S(1)}, bf16[64,256]{1,0:T(8,128)(2,1)S(1)}, u32[]{:S(2)}, u32[]{:S(2)}) collective-permute-start(bf16[64,256]{1,0:T(8,128)(2,1)S(1)} %get-tuple-element.47), channel_id=1, source_target_pairs={{0,160},{32,192},{64,224},{96,0},{128,32},{160,64},{192,96},{224,1... | collective-permute-start | bytes 98312 | tf_op jit(solution)/shard_map/ppermute | solution.py:45
  69.3 0.9 collective-permute-start.13
  70.1 3.6 %collective-permute-start.14 = (bf16[64,256]{1,0:T(8,128)(2,1)S(1)}, bf16[64,256]{1,0:T(8,128)(2,1)S(1)}, u32[]{:S(2)}, u32[]{:S(2)}) collective-permute-start(bf16[64,256]{1,0:T(8,128)(2,1)S(1)} %get-tuple-element.45), channel_id=1, source_target_pairs={{0,128},{32,160},{64,192},{96,224},{128,0},{160,32},{192,64},{224,... | collective-permute-start | bytes 98312 | tf_op jit(solution)/shard_map/ppermute | solution.py:45
  73.8 1.8 %collective-permute-start.10 = (f32[112,128]{1,0:T(8,128)S(1)}, f32[112,128]{1,0:T(8,128)S(1)}, u32[]{:S(2)}, u32[]{:S(2)}) collective-permute-start(f32[112,128]{1,0:T(8,128)S(1)} %get-tuple-element.35.mine_ref), channel_id=1, source_target_pairs={{0,1},{1,0},{2,3},{3,2},{4,5},{5,4},{6,7},{7,6},{8,9},{9,8},{10,11... | collective-permute-start | bytes 172040 | tf_op jit(solution)/shard_map/ppermute | solution.py:33
  75.8 2.0 %collective-permute-done.14 = bf16[64,256]{1,0:T(8,128)(2,1)S(1)} collective-permute-done((bf16[64,256]{1,0:T(8,128)(2,1)S(1)}, bf16[64,256]{1,0:T(8,128)(2,1)S(1)}, u32[]{:S(2)}, u32[]{:S(2)}) %collective-permute-start.14) | collective-permute-done | bytes 32800 | tf_op jit(solution)/shard_map/ppermute | solution.py:45
  77.8 3.9 %attention.2 = bf16[16,64,128]{2,1,0:T(8,128)(2,1)} custom-call(s32[3]{0:T(128)S(1)} %pad_add_fusion.place_ref, bf16[512,128]{1,0:T(8,128)(2,1)S(1)} %bitcast.68, f32[112,128]{1,0:T(8,128)S(1)} %get-tuple-element.35.mine_ref, f32[112,128]{1,0:T(8,128)S(1)} %collective-permute-done.10.theirs_ref, f32[64,64]{1,0:T(8,128)S(1)} %get-tuple-element.36.gram_ref, ...), custom_call_target="tpu_custom_call" | custom-call | flops 805306368 | bytes 2097152 | tf_op jit(solution)/shard_map/attention/pallas_call | solution.py:273
  81.7 6.5 %all-to-all-start.2 = ((bf16[16,64,128]{2,1,0:T(8,128)(2,1)}), bf16[16,64,128]{2,1,0:T(8,128)(2,1)S(1)}, u32[]{:S(2)}, u32[]{:S(2)}) async-start(bf16[16,64,128]{2,1,0:T(8,128)(2,1)} %attention.2), calls=%async_computation.2 | async-start | bytes 524288 | tf_op jit(solution)/shard_map/all_to_all | solution.py:486
  88.8 7.0 %all-to-all-done.2.attended_ref = bf16[16,64,128]{2,1,0:T(8,128)(2,1)S(1)} async-done(((bf16[16,64,128]{2,1,0:T(8,128)(2,1)}), bf16[16,64,128]{2,1,0:T(8,128)(2,1)S(1)}, u32[]{:S(2)}, u32[]{:S(2)}) %all-to-all-start.2) | async-done | bytes 262176 | tf_op jit(solution)/shard_map/all_to_all | solution.py:486
  95.9 4.6 %copy-done = bf16[3072,2048]{1,0:T(8,128)(2,1)S(1)} copy-done((bf16[3072,2048]{1,0:T(8,128)(2,1)S(1)}, bf16[3072,2048]{1,0:T(8,128)(2,1)}, u32[]{:S(2)}) %copy-start) | copy-done | bytes 12582936
  100.4 4.4 %output_stage.2 = f32[8,32,128]{2,1,0:T(8,128)S(1)} custom-call(bf16[16,64,128]{2,1,0:T(8,128)(2,1)S(1)} %all-to-all-done.2.attended_ref, bf16[3072,2048]{1,0:T(8,128)(2,1)S(1)} %copy-done, bf16[32,128]{1,0:T(8,128)(2,1)S(1)} %convert_element_type.11.x_ref, bf16[64,3072]{1,0:T(8,128)(2,1)S(1)} %copy-done.2, f32[7,3072]{1,0:T(8,128)S(1)} %bitcast.62, ...), custom_call_target="tpu_custom_call" | custom-call | flops 805306368 | bytes 12582912 | tf_op jit(solution)/shard_map/output_stage/pallas_call | solution.py:334
  104.9 15.1 %all_to_all.35.everyone_ref = f32[8,32,128]{2,1,0:T(8,128)S(1)} all-to-all(f32[8,32,128]{2,1,0:T(8,128)S(1)} %output_stage.2), channel_id=1, replica_groups=mesh['step'=8,'y'=4,'x'=4,'core'=2] {'step'}, dimensions={0} | all-to-all | bytes 262144 | tf_op jit(solution)/shard_map/all_to_all | solution.py:491
  120.0 0.6 scan.1
  120.5 11.1 %all_to_all.36 = bf16[16,32,128]{2,1,0:T(8,128)(2,1)S(1)} all-to-all(bf16[16,32,128]{2,1,0:T(8,128)(2,1)S(1)} %scan.1), channel_id=1, replica_groups=mesh['step'=8,'y'=4,'x'=4,'core'=2] {'y','x'}, dimensions={0} | all-to-all | bytes 262144 | tf_op jit(solution)/shard_map/all_to_all | solution.py:494
  131.6 3.9 %attention.3 = bf16[16,64,128]{2,1,0:T(8,128)(2,1)} custom-call(s32[3]{0:T(128)S(1)} %pad_add_fusion.place_ref, bf16[512,128]{1,0:T(8,128)(2,1)S(1)} %bitcast.67, f32[112,128]{1,0:T(8,128)S(1)} %get-tuple-element.35.mine_ref, f32[112,128]{1,0:T(8,128)S(1)} %collective-permute-done.10.theirs_ref, f32[64,64]{1,0:T(8,128)S(1)} %get-tuple-element.36.gram_ref, ...), custom_call_target="tpu_custom_call" | custom-call | flops 805306368 | bytes 2097152 | tf_op jit(solution)/shard_map/attention/pallas_call | solution.py:273
  135.5 3.5 %all-to-all-start.5 = ((bf16[16,64,128]{2,1,0:T(8,128)(2,1)}), bf16[16,64,128]{2,1,0:T(8,128)(2,1)S(1)}, u32[]{:S(2)}, u32[]{:S(2)}) async-start(bf16[16,64,128]{2,1,0:T(8,128)(2,1)} %attention.3), calls=%async_computation.5 | async-start | bytes 524288 | tf_op jit(solution)/shard_map/all_to_all | solution.py:486
  139.1 7.5 %all-to-all-done.5.attended_ref = bf16[16,64,128]{2,1,0:T(8,128)(2,1)S(1)} async-done(((bf16[16,64,128]{2,1,0:T(8,128)(2,1)}), bf16[16,64,128]{2,1,0:T(8,128)(2,1)S(1)}, u32[]{:S(2)}, u32[]{:S(2)}) %all-to-all-start.5) | async-done | bytes 262176 | tf_op jit(solution)/shard_map/all_to_all | solution.py:486
  146.6 4.6 %copy-done.1 = bf16[3072,2048]{1,0:T(8,128)(2,1)S(1)} copy-done((bf16[3072,2048]{1,0:T(8,128)(2,1)S(1)}, bf16[3072,2048]{1,0:T(8,128)(2,1)}, u32[]{:S(2)}) %copy-start.1) | copy-done | bytes 12582936
  151.1 4.4 %output_stage.3 = f32[8,32,128]{2,1,0:T(8,128)S(1)} custom-call(bf16[16,64,128]{2,1,0:T(8,128)(2,1)S(1)} %all-to-all-done.5.attended_ref, bf16[3072,2048]{1,0:T(8,128)(2,1)S(1)} %copy-done.1, bf16[32,128]{1,0:T(8,128)(2,1)S(1)} %slice_bitcast_fusion.8.x_ref, bf16[64,3072]{1,0:T(8,128)(2,1)S(1)} %copy-done.2, f32[7,3072]{1,0:T(8,128)S(1)} %bitcast.63, ...), custom_call_target="tpu_custom_call" | custom-call | flops 805306368 | bytes 12582912 | tf_op jit(solution)/shard_map/output_stage/pallas_call | solution.py:334
  155.6 16.7 %all_to_all.37.everyone_ref = f32[16,16,128]{2,1,0:T(8,128)S(1)} all-to-all(f32[16,16,128]{2,1,0:T(8,128)S(1)} %bitcast.66), channel_id=1, replica_groups=mesh['step'=8,'y'=4,'x'=4,'core'=2] {'step','core'}, dimensions={0} | all-to-all | bytes 262144 | tf_op jit(solution)/shard_map/all_to_all | solution.py:496
  172.3 1.2 total_rows.1
  (66 shorter events, 0.6 us)
Async XLA Ops:
  6.5 4.7 %copy-start.9 = (f32[1,7,3072]{2,0,1:T(1,128)S(1)}, f32[1,7,3072]{2,0,1:T(1,128)}, u32[]{:S(2)}) copy-start(f32[1,7,3072]{2,0,1:T(1,128)} %param.14) | copy-start | bytes 258052
  6.5 4.7 %copy-start.7 = (bf16[96,3,16,128]{3,2,1,0:T(8,128)(2,1)S(1)}, bf16[96,3,16,128]{3,2,1,0:T(8,128)(2,1)}, u32[]{:S(2)}) copy-start(bf16[96,3,16,128]{3,2,1,0:T(8,128)(2,1)} %param.17) | copy-start | bytes 3538948
  6.5 89.3 %all-gather.2.cloned.1.call-start = ((), (), s32[]{:S(2)}) async-start(), calls=%async_computation.7 | async-start | bytes 12976128 | tf_op jit(solution)/shard_map/all_gather | solution.py:455
  11.6 1.1 copy-start.8
  12.7 1.0 copy-start.2
  13.6 6.7 %copy-start.10 = (f32[1,2,32,64]{3,2,1,0:T(8,128)S(1)}, f32[1,2,32,64]{3,2,1,0:T(8,128)}, u32[]{:S(2)}) copy-start(f32[1,2,32,64]{3,2,1,0:T(8,128)} %param.12) | copy-start | bytes 49156
  13.6 6.8 %copy-start.11 = (f32[1,2,32,64]{3,2,1,0:T(8,128)S(1)}, f32[1,2,32,64]{3,2,1,0:T(8,128)}, u32[]{:S(2)}) copy-start(f32[1,2,32,64]{3,2,1,0:T(8,128)} %param.11) | copy-start | bytes 49156
  17.1 26.2 %collective-permute-start = (f32[16,112,128]{2,1,0:T(8,128)}, f32[16,112,128]{2,1,0:T(8,128)}, u32[]{:S(2)}, u32[]{:S(2)}) collective-permute-start(f32[16,112,128]{2,1,0:T(8,128)} %get-tuple-element.28), channel_id=1, source_target_pairs={{0,1},{1,0},{2,3},{3,2},{4,5},{5,4},{6,7},{7,6},{8,9},{9,8},{10,11... | collective-permute-start | bytes 2752520 | tf_op jit(solution)/shard_map/ppermute | solution.py:33
  20.5 5.9 %slice-start = ((f32[1,7,3072]{2,0,1:T(1,128)}), f32[1,2,3072]{2,0,1:T(1,128)S(1)}, s32[]{:S(2)}) async-start(f32[1,7,3072]{2,0,1:T(1,128)} %param.14), calls=%async_computation.8 | async-start | bytes 49152 | tf_op jit(solution)/shard_map/slice | solution.py:434
  20.5 7.7 %collective-permute-start.1 = (f32[2,16,128]{2,1,0:T(8,128)S(1)}, f32[2,16,128]{2,1,0:T(8,128)S(1)}, u32[]{:S(2)}, u32[]{:S(2)}) collective-permute-start(f32[2,16,128]{2,1,0:T(8,128)S(1)} %fusion.7), channel_id=1, source_target_pairs={{0,1},{1,0},{2,3},{3,2},{4,5},{5,4},{6,7},{7,6},{8,9},{9,8},{10,11... | collective-permute-start | bytes 49160 | tf_op jit(solution)/shard_map/ppermute | solution.py:33
  20.5 28.7 %all-to-all-start = ((bf16[32,144,128]{2,1,0:T(8,128)(2,1)}), bf16[32,144,128]{2,1,0:T(8,128)(2,1)S(1)}, u32[]{:S(2)}, u32[]{:S(2)}) async-start(bf16[32,144,128]{2,1,0:T(8,128)(2,1)} %pad_maximum_fusion), calls=%async_computation | async-start | bytes 2359296 | tf_op jit(solution)/shard_map/all_to_all | solution.py:456
  26.4 7.2 %collective-permute-start.2 = (f32[1,2,3072]{2,1,0:T(2,128)S(1)}, f32[1,2,3072]{2,1,0:T(2,128)S(1)}, u32[]{:S(2)}, u32[]{:S(2)}) collective-permute-start(f32[1,2,3072]{2,1,0:T(2,128)S(1)} %get-tuple-element.59), channel_id=1, source_target_pairs={{0,32},{32,64},{64,96},{96,128},{128,160},{160,192},{192,224},{224... | collective-permute-start | bytes 73736 | tf_op jit(solution)/shard_map/ppermute | solution.py:45
  33.6 7.7 %collective-permute-start.3 = (f32[2,2,3072]{2,1,0:T(2,128)S(1)}, f32[2,2,3072]{2,1,0:T(2,128)S(1)}, u32[]{:S(2)}, u32[]{:S(2)}) collective-permute-start(f32[2,2,3072]{2,1,0:T(2,128)S(1)} %get-tuple-element.55), channel_id=1, source_target_pairs={{0,64},{32,96},{64,128},{96,160},{128,192},{160,224},{192,0},{224,... | collective-permute-start | bytes 147464 | tf_op jit(solution)/shard_map/ppermute | solution.py:45
  33.7 8.2 %collective-permute-start.4 = (f32[2,2,3072]{2,1,0:T(2,128)S(1)}, f32[2,2,3072]{2,1,0:T(2,128)S(1)}, u32[]{:S(2)}, u32[]{:S(2)}) collective-permute-start(f32[2,2,3072]{2,1,0:T(2,128)S(1)} %get-tuple-element.55), channel_id=1, source_target_pairs={{0,128},{32,160},{64,192},{96,224},{128,0},{160,32},{192,64},{224,... | collective-permute-start | bytes 147464 | tf_op jit(solution)/shard_map/ppermute | solution.py:45
  37.8 5.4 %collective-permute-start.5 = (f32[2,2,3072]{2,1,0:T(2,128)S(1)}, f32[2,2,3072]{2,1,0:T(2,128)S(1)}, u32[]{:S(2)}, u32[]{:S(2)}) collective-permute-start(f32[2,2,3072]{2,1,0:T(2,128)S(1)} %get-tuple-element.55), channel_id=1, source_target_pairs={{0,192},{32,224},{64,0},{96,32},{128,64},{160,96},{192,128},{224,1... | collective-permute-start | bytes 147464 | tf_op jit(solution)/shard_map/ppermute | solution.py:45
  43.3 2.2 %copy-start.4 = (f32[8,2,3072]{2,1,0:T(2,128)}, f32[8,2,3072]{2,1,0:T(2,128)S(1)}, u32[]{:S(2)}) copy-start(f32[8,2,3072]{2,1,0:T(2,128)S(1)} %constant_dynamic-update-slice_fusion.2.mods_ref) | copy-start | bytes 589828
  45.5 8.6 %copy-start.6 = (f32[3,128]{1,0:T(4,128)S(1)}, f32[3,128]{1,0:T(4,128)}, u32[]{:S(2)}) copy-start(f32[3,128]{1,0:T(4,128)} %gains_ref.5) | copy-start | bytes 4612
  49.2 4.9 %collective-permute-start.6 = (bf16[32,144,128]{2,1,0:T(8,128)(2,1)S(1)}, bf16[32,144,128]{2,1,0:T(8,128)(2,1)S(1)}, u32[]{:S(2)}, u32[]{:S(2)}) collective-permute-start(bf16[32,144,128]{2,1,0:T(8,128)(2,1)S(1)} %all-to-all-done.mine_ref), channel_id=1, source_target_pairs={{0,1},{1,0},{2,3},{3,2},{4,5},{5,4},{6,7},{7,6},{8,9},{9,8},{10,11... | collective-permute-start | bytes 3538952 | tf_op jit(solution)/shard_map/ppermute | solution.py:33
  50.4 23.3 %all-to-all-start.1 = ((bf16[16,144,128]{2,1,0:T(8,128)(2,1)}), bf16[16,144,128]{2,1,0:T(8,128)(2,1)S(1)}, u32[]{:S(2)}, u32[]{:S(2)}) async-start(bf16[16,144,128]{2,1,0:T(8,128)(2,1)} %add_parts.1), calls=%async_computation.1 | async-start | bytes 1179648 | tf_op jit(solution)/shard_map/all_to_all | solution.py:468
  54.1 0.9 copy-start.5
  57.6 11.6 %collective-permute-start.7 = (bf16[64,256]{1,0:T(8,128)(2,1)S(1)}, bf16[64,256]{1,0:T(8,128)(2,1)S(1)}, u32[]{:S(2)}, u32[]{:S(2)}) collective-permute-start(bf16[64,256]{1,0:T(8,128)(2,1)S(1)} %get-tuple-element.51), channel_id=1, source_target_pairs={{0,224},{32,0},{64,32},{96,64},{128,96},{160,128},{192,160},{224,1... | collective-permute-start | bytes 98312 | tf_op jit(solution)/shard_map/ppermute | solution.py:45
  64.5 5.6 %collective-permute-start.8 = (bf16[64,256]{1,0:T(8,128)(2,1)S(1)}, bf16[64,256]{1,0:T(8,128)(2,1)S(1)}, u32[]{:S(2)}, u32[]{:S(2)}) collective-permute-start(bf16[64,256]{1,0:T(8,128)(2,1)S(1)} %get-tuple-element.50), channel_id=1, source_target_pairs={{0,32},{32,64},{64,96},{96,128},{128,160},{160,192},{192,224},{224... | collective-permute-start | bytes 98312 | tf_op jit(solution)/shard_map/ppermute | solution.py:45
  64.5 9.2 %collective-permute-start.9 = (bf16[64,256]{1,0:T(8,128)(2,1)S(1)}, bf16[64,256]{1,0:T(8,128)(2,1)S(1)}, u32[]{:S(2)}, u32[]{:S(2)}) collective-permute-start(bf16[64,256]{1,0:T(8,128)(2,1)S(1)} %get-tuple-element.49), channel_id=1, source_target_pairs={{0,192},{32,224},{64,0},{96,32},{128,64},{160,96},{192,128},{224,1... | collective-permute-start | bytes 98312 | tf_op jit(solution)/shard_map/ppermute | solution.py:45
  66.4 9.3 %collective-permute-start.11 = (bf16[64,256]{1,0:T(8,128)(2,1)S(1)}, bf16[64,256]{1,0:T(8,128)(2,1)S(1)}, u32[]{:S(2)}, u32[]{:S(2)}) collective-permute-start(bf16[64,256]{1,0:T(8,128)(2,1)S(1)} %get-tuple-element.48), channel_id=1, source_target_pairs={{0,64},{32,96},{64,128},{96,160},{128,192},{160,224},{192,0},{224,... | collective-permute-start | bytes 98312 | tf_op jit(solution)/shard_map/ppermute | solution.py:45
  66.9 8.8 %collective-permute-start.12 = (bf16[64,256]{1,0:T(8,128)(2,1)S(1)}, bf16[64,256]{1,0:T(8,128)(2,1)S(1)}, u32[]{:S(2)}, u32[]{:S(2)}) collective-permute-start(bf16[64,256]{1,0:T(8,128)(2,1)S(1)} %get-tuple-element.47), channel_id=1, source_target_pairs={{0,160},{32,192},{64,224},{96,0},{128,32},{160,64},{192,96},{224,1... | collective-permute-start | bytes 98312 | tf_op jit(solution)/shard_map/ppermute | solution.py:45
  69.3 6.5 %collective-permute-start.13 = (bf16[64,256]{1,0:T(8,128)(2,1)S(1)}, bf16[64,256]{1,0:T(8,128)(2,1)S(1)}, u32[]{:S(2)}, u32[]{:S(2)}) collective-permute-start(bf16[64,256]{1,0:T(8,128)(2,1)S(1)} %get-tuple-element.46), channel_id=1, source_target_pairs={{0,96},{32,128},{64,160},{96,192},{128,224},{160,0},{192,32},{224,... | collective-permute-start | bytes 98312 | tf_op jit(solution)/shard_map/ppermute | solution.py:45
  70.1 7.6 %collective-permute-start.14 = (bf16[64,256]{1,0:T(8,128)(2,1)S(1)}, bf16[64,256]{1,0:T(8,128)(2,1)S(1)}, u32[]{:S(2)}, u32[]{:S(2)}) collective-permute-start(bf16[64,256]{1,0:T(8,128)(2,1)S(1)} %get-tuple-element.45), channel_id=1, source_target_pairs={{0,128},{32,160},{64,192},{96,224},{128,0},{160,32},{192,64},{224,... | collective-permute-start | bytes 98312 | tf_op jit(solution)/shard_map/ppermute | solution.py:45
  73.8 3.9 %collective-permute-start.10 = (f32[112,128]{1,0:T(8,128)S(1)}, f32[112,128]{1,0:T(8,128)S(1)}, u32[]{:S(2)}, u32[]{:S(2)}) collective-permute-start(f32[112,128]{1,0:T(8,128)S(1)} %get-tuple-element.35.mine_ref), channel_id=1, source_target_pairs={{0,1},{1,0},{2,3},{3,2},{4,5},{5,4},{6,7},{7,6},{8,9},{9,8},{10,11... | collective-permute-start | bytes 172040 | tf_op jit(solution)/shard_map/ppermute | solution.py:33
  77.8 18.1 %copy-start.3 = (bf16[3072,64]{0,1:T(8,128)(2,1)S(1)}, bf16[3072,64]{0,1:T(8,128)(2,1)}, u32[]{:S(2)}) copy-start(bf16[3072,64]{0,1:T(8,128)(2,1)} %param.21) | copy-start | bytes 1179652
  81.7 14.2 %all-to-all-start.2 = ((bf16[16,64,128]{2,1,0:T(8,128)(2,1)}), bf16[16,64,128]{2,1,0:T(8,128)(2,1)S(1)}, u32[]{:S(2)}, u32[]{:S(2)}) async-start(bf16[16,64,128]{2,1,0:T(8,128)(2,1)} %attention.2), calls=%async_computation.2 | async-start | bytes 524288 | tf_op jit(solution)/shard_map/all_to_all | solution.py:486
  95.9 4.6 %copy-start = (bf16[3072,2048]{1,0:T(8,128)(2,1)S(1)}, bf16[3072,2048]{1,0:T(8,128)(2,1)}, u32[]{:S(2)}) copy-start(bf16[3072,2048]{1,0:T(8,128)(2,1)} %all-gather.2.cloned.1.call-done.w_out_ref) | copy-start | bytes 37748740
  135.5 11.0 %all-to-all-start.5 = ((bf16[16,64,128]{2,1,0:T(8,128)(2,1)}), bf16[16,64,128]{2,1,0:T(8,128)(2,1)S(1)}, u32[]{:S(2)}, u32[]{:S(2)}) async-start(bf16[16,64,128]{2,1,0:T(8,128)(2,1)} %attention.3), calls=%async_computation.5 | async-start | bytes 524288 | tf_op jit(solution)/shard_map/all_to_all | solution.py:486
  146.6 4.6 %copy-start.1 = (bf16[3072,2048]{1,0:T(8,128)(2,1)S(1)}, bf16[3072,2048]{1,0:T(8,128)(2,1)}, u32[]{:S(2)}) copy-start(bf16[3072,2048]{1,0:T(8,128)(2,1)} %all-gather.2.cloned.1.call-done.w_out_ref) | copy-start | bytes 37748740
Sparse Core Ops, SparseCore 0:
  13.7 80.2 all-gather.1
